TPU v7x, 32 devices: a whole 2x2x4 slice. The times are simulated.
32 devices in a mesh: emb: 16 (over z, y, core), wide: 2 (over x).
Axes of the slice: x: 2, y: 2, z: 4, core: 2. Of those that a mesh axis runs over, the one named last changes fastest.
Arguments:
- tables: bfloat16 [512, 512, 256], P('emb'), may hold values from -3 to 3
- bag_ids: int32 [2, 64, 512, 4], P('wide', None, 'emb'), may hold values from 0 to 511
- bag_lengths: int32 [2, 64, 512], P('wide', None, 'emb'), may hold values from 1 to 4
- slot_field: int32 [512], replicated, may hold values from 0 to 511, each once
- proj_y: bfloat16 [512, 256], replicated, may hold values from -0.25 to 0.25
- proj_p: bfloat16 [128, 512], replicated, may hold values from -0.25 to 0.25
- linear_w: bfloat16 [384, 512], replicated, may hold values from -0.25 to 0.25
- fm_gain: float32 [256], replicated, may hold values from 0.5 to 1.5
- w_up: bfloat16 [8192, 256], P('wide'), may hold values from -0.375 to 0.375
- w_down: bfloat16 [8192, 256], P('wide'), may hold values from -0.0625 to 0.0625
- out_gain: float32 [256], replicated, may hold values from 0.5 to 1.5
- cotangent: bfloat16 [2, 64, 512, 256], P('wide', 'emb'), may hold values from -6 to 6
Outputs:
- layer_out: bfloat16 [2, 64, 512, 256], P('wide', 'emb')
- pooled_grad: bfloat16 [2, 64, 512, 256], P('wide', None, 'emb')
- grad_up: float32 [8192, 256], P('wide')
- grad_down: float32 [8192, 256], P('wide')
Inputs may be any that keep to these rules, and one draw needn't show every extreme that they name: `bag_ids`: each id indexes a bucket of the table of its slot. `slot_field`: each field appears in exactly one slot.
All inputs are finite; a program needn't handle non-finite values.
Results may differ from a plain program's by a relative error of at most 0.008.
Values may be sent and summed in bfloat16 or wider, within the bound.
No kernel may reach another device: no remote copies, remote signals or barrier semaphores. Data moves between devices by JAX's collectives and lax.ppermute only.
A program may use at most 128 MiB of HBM per device.

v0:
```python
import jax
import jax.numpy as jnp
from jax import lax
from jax.sharding import PartitionSpec as P

NF = 128


norm_eps = 1e-05


def layer_norm(values):
    centre = jnp.mean(values, axis=-1, keepdims=True)
    shifted = values - centre
    scale = lax.rsqrt(jnp.mean(shifted * shifted, axis=-1, keepdims=True) + norm_eps)
    return (shifted * scale, scale)


def norm_back(unit, scale, gain, upstream):
    scaled = upstream * gain
    return scale * (
        scaled
        - jnp.mean(scaled, axis=-1, keepdims=True)
        - unit * jnp.mean(scaled * unit, axis=-1, keepdims=True)
    )


def silu_back(values):
    sigma = jax.nn.sigmoid(values)
    return sigma * (1.0 + values * (1.0 - sigma))


def pool_bags(tables, ids, lengths):
    slots_here = tables.shape[0]
    bucket_count = tables.shape[1]
    flat_ids = ids + (jnp.arange(slots_here, dtype=jnp.int32) * bucket_count)[None, :, None]
    gathered = jnp.take(tables.reshape(slots_here * bucket_count, -1), flat_ids, axis=0)
    live = (jnp.arange(ids.shape[2], dtype=jnp.int32)[None, None, :] < lengths[:, :, None]).astype(
        jnp.bfloat16
    )
    return jnp.einsum("gfj,gfje->gfe", live, gathered, preferred_element_type=jnp.float32).astype(
        jnp.bfloat16
    )


def body(
    tables,
    bag_ids,
    bag_lengths,
    slot_field,
    proj_y,
    proj_p,
    linear_w,
    fm_gain,
    w_up,
    w_down,
    out_gain,
    cotangent,
):
    pooled = pool_bags(tables, bag_ids[0], bag_lengths[0])[None]
    received = lax.all_to_all(pooled, "emb", split_axis=1, concat_axis=2, tiled=True)
    slot_embeds = received[0]
    embeds = jnp.zeros_like(slot_embeds).at[:, slot_field].set(slot_embeds)
    samples = embeds.shape[0]
    crossed = jnp.einsum("bfe,fk->bek", embeds, proj_y, preferred_element_type=jnp.float32).astype(
        jnp.bfloat16
    )
    mixing = jnp.einsum("nf,bfe->bne", proj_p, embeds, preferred_element_type=jnp.float32).astype(
        jnp.bfloat16
    )
    inter = jnp.einsum("bne,bek->bnk", mixing, crossed, preferred_element_type=jnp.float32)
    inter_unit, inter_scale = layer_norm(inter)
    inter_norm = (inter_unit * fm_gain).astype(jnp.bfloat16)
    inter_rows = inter_norm.reshape(samples * NF, -1)
    row_total = inter_rows.shape[0]
    up_all, down_all = (
        lax.all_gather(w_up, "wide", axis=0, tiled=True),
        lax.all_gather(w_down, "wide", axis=0, tiled=True),
    )
    gate_pre = jnp.einsum("rk,hk->rh", inter_rows, up_all, preferred_element_type=jnp.float32)
    hidden = jax.nn.silu(gate_pre).astype(jnp.bfloat16)
    ff_rows = jnp.dot(hidden, down_all, preferred_element_type=jnp.float32)
    linear_out = jnp.einsum("lf,bfe->ble", linear_w, embeds, preferred_element_type=jnp.float32)
    summed = jnp.concatenate(
        [ff_rows.reshape(samples, NF, -1), linear_out], axis=1
    ) + embeds.astype(jnp.float32)
    summed_unit, summed_scale = layer_norm(summed)
    layer_out = (summed_unit * out_gain).astype(jnp.bfloat16)
    grad_summed = norm_back(summed_unit, summed_scale, out_gain, cotangent[0].astype(jnp.float32))
    grad_ff = grad_summed[:, :NF].astype(jnp.bfloat16)
    grad_lin = grad_summed[:, NF:].astype(jnp.bfloat16)
    grad_ff_rows = grad_ff.reshape(row_total, -1)
    grad_hidden = jnp.einsum(
        "re,he->rh", grad_ff_rows, down_all, preferred_element_type=jnp.float32
    )
    grad_gate = (grad_hidden * silu_back(gate_pre)).astype(jnp.bfloat16)
    grad_rows = jnp.dot(grad_gate, up_all, preferred_element_type=jnp.float32)
    rank_width = w_up.shape[1]
    up_term = jnp.einsum("rh,rk->hk", grad_gate, inter_rows, preferred_element_type=jnp.float32)
    down_term_part = jnp.einsum(
        "rh,re->he", hidden, grad_ff_rows, preferred_element_type=jnp.float32
    )
    both_terms = lax.psum_scatter(
        jnp.concatenate([up_term, down_term_part], axis=1), "wide", scatter_dimension=0, tiled=True
    )
    up_local = both_terms[:, :rank_width]
    down_local = both_terms[:, rank_width:]
    grad_up, grad_down = lax.psum((up_local, down_local), "emb")
    grad_norm = grad_rows.reshape(samples, NF, -1)
    grad_inter = norm_back(inter_unit, inter_scale, fm_gain, grad_norm).astype(jnp.bfloat16)
    grad_mixing = jnp.einsum(
        "bnk,bek->bne", grad_inter, crossed, preferred_element_type=jnp.float32
    ).astype(jnp.bfloat16)
    grad_crossed = jnp.einsum(
        "bne,bnk->bek", mixing, grad_inter, preferred_element_type=jnp.float32
    ).astype(jnp.bfloat16)
    grad_embeds = grad_summed + jnp.einsum(
        "lf,ble->bfe", linear_w, grad_lin, preferred_element_type=jnp.float32
    )
    grad_embeds = grad_embeds + jnp.einsum(
        "nf,bne->bfe", proj_p, grad_mixing, preferred_element_type=jnp.float32
    )
    grad_embeds = grad_embeds + jnp.einsum(
        "fk,bek->bfe", proj_y, grad_crossed, preferred_element_type=jnp.float32
    )
    grad_embeds = grad_embeds.astype(jnp.bfloat16)
    slot_grads = grad_embeds[:, slot_field]
    returned = lax.all_to_all(slot_grads[None], "emb", split_axis=2, concat_axis=1, tiled=True)
    return (layer_out[None], returned, grad_up, grad_down)


def solution(mesh):
    placed = (
        P("emb", None, None),
        P("wide", None, "emb", None),
        P("wide", None, "emb"),
        P(),
        P(),
        P(),
        P(),
        P(),
        P("wide", None),
        P("wide", None),
        P(),
        P("wide", "emb", None, None),
    )
    return jax.shard_map(
        body,
        mesh=mesh,
        in_specs=placed,
        out_specs=(
            P("wide", "emb", None, None),
            P("wide", None, "emb", None),
            P("wide", None),
            P("wide", None),
        ),
        check_vma=False,
    )
```

profile of v0, /device:TPU:9, one launch (start us, length us, event | category | flops | bytes accessed | tf_op | source)
XLA Modules:
  0.0 580.4 jit_solution(1037751574176465792)
XLA Ops:
  7.2 0.7 all-gather.3.cloned.1.call-update
  7.9 0.9 compare_select_fusion
  8.9 1.0 copy.67
  9.8 0.7 reshape.112
  10.5 35.6 %gather_fusion = bf16[8192,256]{1,0:T(8,128)(2,1)} fusion(bf16[16384,256]{1,0:T(8,128)(2,1)} %bitcast.109, s32[8192]{0:T(1024)S(1)} %broadcast_clamp_fusion), kind=kCustom, calls=%fused_computation | custom fusion | bytes 8421376 | tf_op jit(solution)/shard_map/jit(_take)/gather | solution.py:37
  46.1 6.9 %reshape.111 = bf16[64,32,4,256]{3,2,1,0:T(4,128)(2,1)} reshape(bf16[8192,256]{1,0:T(8,128)(2,1)} %gather_fusion) | data formatting | bytes 8388608 | tf_op jit(solution)/shard_map/jit(_take)/gather | solution.py:37
  53.2 1.0 copy.66
  54.6 5.9 %fusion = bf16[64,32,1,256]{3,2,1,0:T(2,128)(2,1)S(1)} fusion(bf16[64,32,4,256]{3,2,1,0:T(4,128)(2,1)} %reshape.111, pred[64,32,4]{2,1,0:T(8,128)(4,1)S(1)} %copy.66, pred[64,32,4,1]{2,1,0,3:T(32,128)(4,1)S(1)} %fusion.15), kind=kOutput, calls=%fused_computation.7 | convolution fusion | flops 6291456 | bytes 5259264 | tf_op jit(solution)/shard_map/gfj,gfje->gfe/dot_general | solution.py:41
  60.5 1.3 copy.95
  61.8 6.6 %all-to-all-start = ((bf16[1,64,32,256]{3,2,0,1:T(8,128)(2,1)}), bf16[1,64,32,256]{3,2,0,1:T(8,128)(2,1)S(1)}, u32[]{:S(2)}, u32[]{:S(2)}) async-start(bf16[1,64,32,256]{3,2,0,1:T(8,128)(2,1)} %bitcast.108), calls=%async_computation | async-start | bytes 2097152 | tf_op jit(solution)/shard_map/all_to_all | solution.py:61
  68.5 0.7 all-gather.5.cloned.1.call-update
  69.4 1.3 copy.76
  70.7 22.5 %all-to-all-done = bf16[1,64,32,256]{3,2,0,1:T(8,128)(2,1)S(1)} async-done(((bf16[1,64,32,256]{3,2,0,1:T(8,128)(2,1)}), bf16[1,64,32,256]{3,2,0,1:T(8,128)(2,1)S(1)}, u32[]{:S(2)}, u32[]{:S(2)}) %all-to-all-start) | async-done | bytes 1048608 | tf_op jit(solution)/shard_map/all_to_all | solution.py:61
  93.3 0.8 copy.69
  94.5 13.6 %scatter_fusion = bf16[4,512,256]{2,0,1:T(4,128)(2,1)S(1)} fusion(bf16[4,512,256]{2,0,1:T(4,128)(2,1)S(1)} %broadcast_in_dim.20, s32[512]{0:T(512)S(1)} %compare_select_fusion.2, bf16[512,4,256]{2,1,0:T(4,128)(2,1)S(1)} %copy.69), kind=kCustom, calls=%fused_computation.2 | custom fusion | bytes 3147776 | tf_op jit(solution)/shard_map/scatter | solution.py:63
  108.0 1.0 copy.70
  109.0 1.3 convolution_convert_fusion.3
  110.4 1.5 convolution_convert_fusion
  113.9 1.9 convolution_bitcast_fusion
  115.7 13.1 %multiply_convert_fusion.1 = (bf16[512,8192]{1,0:T(8,128)(2,1)}, f32[512,8192]{1,0:T(8,128)}) fusion(bf16[512,256]{1,0:T(8,128)(2,1)S(1)} %bitcast.114, bf16[8192,256]{1,0:T(8,128)(2,1)} %all-gather.3.cloned.1.call-done), kind=kOutput, calls=%fused_computation.5 | convolution fusion | flops 2168455168 | bytes 29622272 | tf_op jit(solution)/shard_map/rk,hk->rh/dot_general | solution.py:80
  128.8 6.9 %fusion.29 = f32[512,256]{1,0:T(8,128)S(1)} fusion(bf16[512,8192]{1,0:T(8,128)(2,1)} %get-tuple-element.32, bf16[8192,256]{1,0:T(8,128)(2,1)} %all-gather.5.cloned.1.call-done), kind=kOutput, calls=%fused_computation.74 | convolution fusion | flops 2147483648 | bytes 13107200 | tf_op jit(solution)/shard_map/dot_general | solution.py:82
  135.7 1.0 copy.74
  136.7 1.9 fusion.26
  139.0 0.6 fusion.6
  139.7 1.9 fusion.22
  141.6 1.0 copy-done.7
  142.7 5.8 %fusion.31 = f32[8192,256]{0,1:T(8,128)S(1)} fusion(bf16[512,8192]{1,0:T(8,128)(2,1)} %get-tuple-element.32, bf16[512,256]{1,0:T(8,128)(2,1)S(1)} %bitcast.116), kind=kOutput, calls=%fused_computation.76 | convolution fusion | flops 2147483648 | bytes 17039360 | tf_op jit(solution)/shard_map/rh,re->he/dot_general | solution.py:100
  148.6 13.6 %multiply_convert_fusion = bf16[512,8192]{1,0:T(8,128)(2,1)} fusion(f32[512,8192]{1,0:T(8,128)} %get-tuple-element.33, bf16[512,256]{1,0:T(8,128)(2,1)S(1)} %bitcast.117, bf16[8192,256]{1,0:T(8,128)(2,1)} %all-gather.5.cloned.1.call-done), kind=kOutput, calls=%fused_computation.4 | convolution fusion | flops 2185232384 | bytes 29622272 | tf_op jit(solution)/shard_map/re,he->rh/dot_general | solution.py:93
  162.2 6.0 %fusion.30 = f32[8192,256]{0,1:T(8,128)S(1)} fusion(bf16[512,8192]{1,0:T(8,128)(2,1)} %multiply_convert_fusion, bf16[512,256]{1,0:T(8,128)(2,1)S(1)} %bitcast.115), kind=kOutput, calls=%fused_computation.75 | convolution fusion | flops 2147483648 | bytes 17039360 | tf_op jit(solution)/shard_map/rh,rk->hk/dot_general | solution.py:99
  168.2 6.1 %pad_maximum_fusion = f32[8192,512]{0,1:T(8,128)} fusion(f32[8192,256]{0,1:T(8,128)S(1)} %fusion.31, f32[8192,256]{0,1:T(8,128)S(1)} %fusion.30), kind=kLoop, calls=%fused_computation.3 | loop fusion | flops 4194304 | bytes 33554432 | tf_op jit(solution)/shard_map/concatenate | solution.py:104
  174.3 0.6 copy-done.20
  175.5 187.5 %reduce-scatter.2.cloned.1.call-done = f32[4096,512]{0,1:T(8,128)} async-done(((f32[8192,512]{0,1:T(8,128)}), f32[4096,512]{0,1:T(8,128)}) %reduce-scatter.2.cloned.1.call-update) | async-done | bytes 8388624 | tf_op jit(solution)/shard_map/reduce_scatter | solution.py:103
  363.1 7.9 %fusion.27 = (f32[4096,256]{0,1:T(8,128)}, f32[4096,256]{0,1:T(8,128)}) fusion(f32[4096,512]{0,1:T(8,128)} %reduce-scatter.2.cloned.1.call-done), kind=kLoop, calls=%fused_computation.72 | loop fusion | bytes 16777216 | tf_op jit(solution)/shard_map/slice | solution.py:107
  371.0 0.7 copy-done.23
  371.6 7.0 %multiply_reduce_fusion.2 = (f32[512]{0:T(512)S(1)}, f32[512,256]{1,0:T(8,128)S(1)}) fusion(f32[256]{0:T(256)S(1)} %copy-done.23, bf16[512,8192]{1,0:T(8,128)(2,1)} %multiply_convert_fusion, bf16[8192,256]{1,0:T(8,128)(2,1)} %all-gather.3.cloned.1.call-done), kind=kOutput, calls=%fused_computation.42 | convolution fusion | flops 2147745280 | bytes 13110272 | tf_op jit(solution)/shard_map/dot_general | solution.py:97
  379.1 1.0 multiply_convert_fusion.3
  380.1 3.2 fusion.12
  383.3 3.2 fusion.16
  386.4 4.6 fusion.10
  391.0 1.8 copy.79
  392.8 3.1 gather_fusion.1
  395.8 6.4 %all-to-all-start.1 = ((bf16[1,4,512,256]{3,1,0,2:T(4,128)(2,1)}), bf16[1,4,512,256]{3,1,0,2:T(4,128)(2,1)S(1)}, u32[]{:S(2)}, u32[]{:S(2)}) async-start(bf16[1,4,512,256]{3,1,0,2:T(4,128)(2,1)} %bitcast.27), calls=%async_computation.1 | async-start | bytes 2097152 | tf_op jit(solution)/shard_map/all_to_all | solution.py:128
  402.2 1.3 copy.83
  403.5 35.1 %all-to-all-done.1 = bf16[1,4,512,256]{3,1,0,2:T(4,128)(2,1)S(1)} async-done(((bf16[1,4,512,256]{3,1,0,2:T(4,128)(2,1)}), bf16[1,4,512,256]{3,1,0,2:T(4,128)(2,1)S(1)}, u32[]{:S(2)}, u32[]{:S(2)}) %all-to-all-start.1) | async-done | bytes 1048608 | tf_op jit(solution)/shard_map/all_to_all | solution.py:128
  438.7 1.1 copy.82
  439.8 122.9 %all-reduce.3.cloned.1.call-done = (f32[4096,256]{0,1:T(8,128)}, f32[4096,256]{0,1:T(8,128)}) async-done(((f32[4096,256]{0,1:T(8,128)}, f32[4096,256]{0,1:T(8,128)}), (f32[4096,256]{0,1:T(8,128)}, f32[4096,256]{0,1:T(8,128)})) %all-reduce.3.cloned.1.call-update) | async-done | bytes 8388624 | tf_op jit(solution)/shard_map/psum | solution.py:108
  562.7 5.6 copy.84
  568.3 5.6 copy.85
  (83 shorter events, 4.9 us)
Async XLA Ops:
  7.2 106.7 %copy-start = (bf16[384,512]{1,0:T(8,128)(2,1)S(1)}, bf16[384,512]{1,0:T(8,128)(2,1)}, u32[]{:S(2)}) copy-start(bf16[384,512]{1,0:T(8,128)(2,1)} %param.18) | copy-start | bytes 1179652
  7.2 108.6 %all-gather.3.cloned.1.call-start = ((), (), s32[]{:S(2)}) async-start(), calls=%async_computation.3 | async-start | bytes 6291456 | tf_op jit(solution)/shard_map/all_gather | solution.py:77
  46.1 6.9 %copy-start.12 = (s32[1,64,32,4]{1,3,2,0:T(4,128)S(1)}, s32[1,64,32,4]{1,3,2,0:T(4,128)}, u32[]{:S(2)}) copy-start(s32[1,64,32,4]{1,3,2,0:T(4,128)} %param.13) | copy-start | bytes 98308
  46.1 8.0 %copy-start.21 = (s32[1,64,32]{1,2,0:T(8,128)S(1)}, s32[1,64,32]{1,2,0:T(8,128)}, u32[]{:S(2)}) copy-start(s32[1,64,32]{1,2,0:T(8,128)} %param.14) | copy-start | bytes 24580
  60.5 8.9 %copy-start.11 = (bf16[1,4,512,256]{3,2,1,0:T(8,128)(2,1)S(1)}, bf16[1,4,512,256]{3,2,1,0:T(8,128)(2,1)}, u32[]{:S(2)}) copy-start(bf16[1,4,512,256]{3,2,1,0:T(8,128)(2,1)} %param.23) | copy-start | bytes 3145732
  60.5 10.2 %copy-start.26 = (s32[512]{0:T(512)S(1)}, s32[512]{0:T(512)}, u32[]{:S(2)}) copy-start(s32[512]{0:T(512)} %param.15) | copy-start | bytes 6148
  61.8 31.5 %all-to-all-start = ((bf16[1,64,32,256]{3,2,0,1:T(8,128)(2,1)}), bf16[1,64,32,256]{3,2,0,1:T(8,128)(2,1)S(1)}, u32[]{:S(2)}, u32[]{:S(2)}) async-start(bf16[1,64,32,256]{3,2,0,1:T(8,128)(2,1)} %bitcast.108), calls=%async_computation | async-start | bytes 2097152 | tf_op jit(solution)/shard_map/all_to_all | solution.py:61
  68.4 60.4 %all-gather.5.cloned.1.call-start = ((), (), s32[]{:S(2)}) async-start(), calls=%async_computation.4 | async-start | bytes 6291456 | tf_op jit(solution)/shard_map/all_gather | solution.py:78
  69.2 293.9 %reduce-scatter.2.cloned.1.call-start = ((), (), s32[]{:S(2)}) async-start(), calls=%async_computation.5 | async-start | bytes 25165824 | tf_op jit(solution)/shard_map/reduce_scatter | solution.py:103
  70.7 23.7 %copy-start.19 = (s32[512]{0:T(512)}, s32[512]{0:T(512)S(1)}, u32[]{:S(2)}) copy-start(s32[512]{0:T(512)S(1)} %compare_select_fusion.2) | copy-start | bytes 6148
  108.0 5.6 copy-start.22
  110.4 3.5 copy-start.8
  111.8 2.0 copy-start.5
  112.2 0.8 copy-start.3
  112.2 0.8 copy-start.15
  113.0 0.6 copy-start.17
  113.9 15.0 %copy-start.9 = (bf16[4,128,256]{2,1,0:T(8,128)(2,1)}, bf16[4,128,256]{2,1,0:T(8,128)(2,1)S(1)}, u32[]{:S(2)}) copy-start(bf16[4,128,256]{2,1,0:T(8,128)(2,1)S(1)} %multiply_convert_fusion.4) | copy-start | bytes 786436
  136.7 2.3 copy-start.1
  136.7 2.3 copy-start.25
  139.7 1.9 copy-start.13
  139.7 1.9 copy-start.14
  141.5 1.0 copy-start.7
  148.6 13.6 %copy-start.10 = (bf16[4,128,256]{2,1,0:T(8,128)(2,1)S(1)}, bf16[4,128,256]{2,1,0:T(8,128)(2,1)}, u32[]{:S(2)}) copy-start(bf16[4,128,256]{2,1,0:T(8,128)(2,1)} %copy-done.9) | copy-start | bytes 786436
  174.3 0.7 copy-start.20
  174.3 388.4 %all-reduce.3.cloned.1.call-start = ((), (), s32[]{:S(2)}) async-start(), calls=%async_computation.6 | async-start | bytes 16777216 | tf_op jit(solution)/shard_map/psum | solution.py:108
  370.9 0.7 copy-start.23
  371.6 7.1 %copy-start.4 = (f32[4,128,256]{2,1,0:T(8,128)S(1)}, f32[4,128,256]{2,1,0:T(8,128)}, u32[]{:S(2)}) copy-start(f32[4,128,256]{2,1,0:T(8,128)} %copy-done.3) | copy-start | bytes 1572868
  371.6 7.1 %copy-start.16 = (f32[4,128]{1,0:T(4,128)S(1)}, f32[4,128]{1,0:T(4,128)}, u32[]{:S(2)}) copy-start(f32[4,128]{1,0:T(4,128)} %copy-done.15) | copy-start | bytes 6148
  371.6 7.1 %copy-start.18 = (f32[4,128]{1,0:T(4,128)S(1)}, f32[4,128]{1,0:T(4,128)}, u32[]{:S(2)}) copy-start(f32[4,128]{1,0:T(4,128)} %copy-done.17) | copy-start | bytes 6148
  371.6 7.1 %copy-start.24 = (f32[256]{0:T(256)S(1)}, f32[256]{0:T(256)}, u32[]{:S(2)}) copy-start(f32[256]{0:T(256)} %param.19) | copy-start | bytes 3076
  378.7 7.7 %copy-start.2 = (bf16[1,4,512,256]{2,3,1,0:T(8,128)(2,1)S(1)}, bf16[1,4,512,256]{2,3,1,0:T(8,128)(2,1)}, u32[]{:S(2)}) copy-start(bf16[1,4,512,256]{2,3,1,0:T(8,128)(2,1)} %copy.76) | copy-start | bytes 3145732
  391.0 11.2 %copy-start.6 = (bf16[1,4,512,256]{2,3,1,0:T(8,128)(2,1)S(1)}, bf16[1,4,512,256]{2,3,1,0:T(8,128)(2,1)}, u32[]{:S(2)}) copy-start(bf16[1,4,512,256]{2,3,1,0:T(8,128)(2,1)} %get-tuple-element.29) | copy-start | bytes 3145732
  395.8 42.7 %all-to-all-start.1 = ((bf16[1,4,512,256]{3,1,0,2:T(4,128)(2,1)}), bf16[1,4,512,256]{3,1,0,2:T(4,128)(2,1)S(1)}, u32[]{:S(2)}, u32[]{:S(2)}) async-start(bf16[1,4,512,256]{3,1,0,2:T(4,128)(2,1)} %bitcast.27), calls=%async_computation.1 | async-start | bytes 2097152 | tf_op jit(solution)/shard_map/all_to_all | solution.py:128
Sparse Core Ops, SparseCore 0:
  9.6 57.8 all-gather.2
  70.8 57.2 all-gather.4
  174.4 188.6 reduce-scatter.1
  371.1 191.5 all-reduce.2
where the time goes:
time: 583 us; the launch traced here: 580 us
  waiting for transfers between devices  369 us (63%)
  local copies, waits for them, and re-layouts  94.5 us (16%)
  matrix products  74.3 us (13%)
  other arithmetic  14.7 us (3%)
  between operations  14.2 us (2%)
  starting transfers between devices  13.3 us (2%)
    reduce_scatter x1, waiting for transfers between devices, body(): lax.psum_scatter(jnp.concatenate([up_term, down_term_part], axis=1), 'wid...  188 us
    psum x1, waiting for transfers between devices, body(): grad_up, grad_down = lax.psum((up_local, down_local), 'emb')  123 us
    gather x2, local copies, waits for them, and re-layouts, pool_bags(): jnp.take(tables.reshape(slots_here * bucket_count, -1), flat_ids, axis=0)  42.5 us
    all_to_all x1, waiting for transfers between devices, body(): lax.all_to_all(slot_grads[None], 'emb', split_axis=2, concat_axis=1, tile...  35.1 us
    all_to_all x1, waiting for transfers between devices, body(): lax.all_to_all(pooled, 'emb', split_axis=1, concat_axis=2, tiled=True)  22.5 us
    unnamed x58, local copies, waits for them, and re-layouts  17.3 us
    scatter x2, local copies, waits for them, and re-layouts, body(): embeds = jnp.zeros_like(slot_embeds).at[:, slot_field].set(slot_embeds)  14.5 us
    dot_general x1, matrix products, body(): jnp.einsum('re,he->rh', grad_ff_rows, down_all, preferred_element_type=jn...  13.6 us
  transfers between devices with their start and end apart: 6, of which 4 were waited for; matrix products, arithmetic and copies ran while one was open for 20% of the time, Pallas kernels for 0%

commit v1 on v0

v1 whole, which is shorter than its diff:
```python
import functools

import jax
import jax.numpy as jnp
from jax import lax
from jax.experimental import pallas as pl
from jax.experimental.pallas import tpu as pltpu
from jax.sharding import Mesh
from jax.sharding import PartitionSpec as P

norm_eps = 1e-05
VMEM_BYTES = 44 * 1024 * 1024
BF = jnp.bfloat16
F32 = jnp.float32
LANES = 128
EMB = ("z", "y", "core")


def params():
    return pltpu.CompilerParams(vmem_limit_bytes=VMEM_BYTES)


def nn(left, right):
    return lax.dot_general(left, right, (((1,), (0,)), ((), ())), preferred_element_type=F32)


def nt(left, right):
    return lax.dot_general(left, right, (((1,), (1,)), ((), ())), preferred_element_type=F32)


def tn(left, right):
    return lax.dot_general(left, right, (((0,), (0,)), ((), ())), preferred_element_type=F32)


def layer_norm(values):
    centre = jnp.mean(values, axis=-1, keepdims=True)
    shifted = values - centre
    scale = lax.rsqrt(jnp.mean(shifted * shifted, axis=-1, keepdims=True) + norm_eps)
    return (shifted * scale, scale)


def norm_back(unit, scale, gain, upstream):
    scaled = upstream * gain
    return scale * (
        scaled
        - jnp.mean(scaled, axis=-1, keepdims=True)
        - unit * jnp.mean(scaled * unit, axis=-1, keepdims=True)
    )


def pool_kernel(ids_ref, tables_ref, out_ref, sums):
    slots, samples, bag = ids_ref.shape
    buckets = tables_ref.shape[1]
    bucket = lax.broadcasted_iota(jnp.int32, (samples, buckets), 1)
    for s in range(slots):
        ids = ids_ref[s]
        count = jnp.zeros((samples, buckets), F32)
        for j in range(bag):
            count = count + jnp.where(ids[:, j : j + 1] == bucket, 1.0, 0.0)
        bags = nn(count.astype(BF), tables_ref[s])
        for c in range(sums.shape[0]):
            sums[c, pl.ds(s * samples, samples), :] = bags[:, c * LANES : (c + 1) * LANES]
    for c in range(sums.shape[0]):
        for b in range(samples):
            bag_sums = sums.at[c][pl.ds(b, slots, stride=samples), :]
            out_ref[b, :, c * LANES : (c + 1) * LANES] = bag_sums.astype(BF)


def pool_bags(tables, ids, lengths):
    slots, buckets, width = tables.shape
    samples, _, bag = ids.shape
    live = jnp.arange(bag, dtype=jnp.int32)[None, None, :] < lengths[:, :, None]
    masked = jnp.where(live, ids, -1).transpose(1, 0, 2)
    step = 16 if slots % 16 == 0 else slots
    return pl.pallas_call(
        pool_kernel,
        grid=(slots // step,),
        in_specs=[
            pl.BlockSpec((step, samples, bag), lambda g: (g, 0, 0)),
            pl.BlockSpec((step, buckets, width), lambda g: (g, 0, 0)),
        ],
        out_specs=pl.BlockSpec((samples, step, width), lambda g: (0, g, 0)),
        out_shape=jax.ShapeDtypeStruct((samples, slots, width), BF),
        scratch_shapes=[pltpu.VMEM((width // LANES, step * samples, LANES), F32)],
        compiler_params=params(),
        name="pool",
    )(masked, tables)


def front_kernel(rec, slot_row, proj_y, proj_p, gain, embeds, crossed, mixing, inter, rows):
    owners, samples, slots, width = rec.shape
    fields = owners * slots
    made = proj_p.shape[0]
    field = lax.broadcasted_iota(jnp.int32, (fields, fields), 0)
    place = jnp.where(field == slot_row[...], 1.0, 0.0).astype(BF)
    for b in range(samples):
        x = nn(place, rec[:, b].reshape(fields, width)).astype(BF)
        embeds[b] = x
        c = tn(x, proj_y[...]).astype(BF)
        crossed[b] = c
        m = nn(proj_p[...], x).astype(BF)
        mixing[b] = m
        v = nn(m, c)
        inter[pl.ds(b * made, made), :] = v
        unit, _ = layer_norm(v)
        rows[pl.ds(b * made, made), :] = (unit * gain[...]).astype(BF)


def linear_kernel(embeds, linear_w, linear_wt, gain, cot, layer_out, partial):
    samples = embeds.shape[0]
    made = linear_w.shape[0]
    first = embeds.shape[1] - made
    for b in range(samples):
        x = embeds[b]
        summed = nn(linear_w[...], x) + x[first:].astype(F32)
        unit, scale = layer_norm(summed)
        layer_out[b, :first] = jnp.zeros_like(layer_out[b, :first])
        layer_out[b, first:] = (unit * gain[...]).astype(BF)
        grad = norm_back(unit, scale, gain[...], cot[b, first:].astype(F32))
        back = nn(linear_wt[...], grad.astype(BF))
        partial[b, :first] = back[:first]
        partial[b, first:] = back[first:] + grad


def up_kernel(rows, w_up, w_down_t, hidden, slope, out, total):
    step = pl.program_id(0)
    tile = w_up.shape[0]
    part = 256
    gained = None
    for s in range(tile // part):
        at = pl.ds(s * part, part)
        gate = nt(w_up[at, :], rows[...])
        sig = 0.5 * jnp.tanh(0.5 * gate) + 0.5
        h = gate * sig
        hb = h.astype(BF)
        hidden[at, :] = hb
        slope[at, :] = (sig + h * (1.0 - sig)).astype(BF)
        term = nn(w_down_t[:, at], hb)
        gained = term if gained is None else gained + term

    @pl.when(step == 0)
    def _():
        total[...] = gained

    @pl.when(step > 0)
    def _():
        total[...] += gained

    @pl.when(step == pl.num_programs(0) - 1)
    def _():
        out[...] = total[...].T.astype(out.dtype)


def tile_of(units, count):
    return min(units, 1024 if count <= 1024 else 256)


def mlp_up(rows, w_up, w_down_t, kind, name):
    count, width = rows.shape
    units = w_up.shape[0]
    tile = tile_of(units, count)
    return pl.pallas_call(
        up_kernel,
        grid=(units // tile,),
        in_specs=[
            pl.BlockSpec((count, width), lambda g: (0, 0)),
            pl.BlockSpec((tile, width), lambda g: (g, 0)),
            pl.BlockSpec((width, tile), lambda g: (0, g)),
        ],
        out_specs=[
            pl.BlockSpec((tile, count), lambda g: (g, 0)),
            pl.BlockSpec((tile, count), lambda g: (g, 0)),
            pl.BlockSpec((count, width), lambda g: (0, 0)),
        ],
        out_shape=[
            jax.ShapeDtypeStruct((units, count), BF),
            jax.ShapeDtypeStruct((units, count), BF),
            jax.ShapeDtypeStruct((count, width), kind),
        ],
        scratch_shapes=[pltpu.VMEM((width, count), F32)],
        compiler_params=params(),
        name=name,
    )(rows, w_up, w_down_t)


def top_kernel(ff_own, ff_other, embeds, gain, cot, _, layer_out, grad, grad_ff):
    samples, made, width = embeds.shape
    for b in range(samples):
        at = pl.ds(b * made, made)
        summed = ff_own[at, :] + embeds[b].astype(F32)
        for w in range(ff_other.shape[0]):
            summed = summed + ff_other[w, at, :].astype(F32)
        unit, scale = layer_norm(summed)
        layer_out[b] = (unit * gain[...]).astype(BF)
        g = norm_back(unit, scale, gain[...], cot[b].astype(F32))
        grad[at, :] = g
        grad_ff[at, :] = g.astype(BF)


def back_kernel(grad_ff, w_down, w_up_t, slope, grad_gate, out, total):
    step = pl.program_id(0)
    tile = w_down.shape[0]
    part = 256
    gained = None
    for s in range(tile // part):
        at = pl.ds(s * part, part)
        g = (nt(w_down[at, :], grad_ff[...]) * slope[at, :].astype(F32)).astype(BF)
        grad_gate[at, :] = g
        term = nn(w_up_t[:, at], g)
        gained = term if gained is None else gained + term

    @pl.when(step == 0)
    def _():
        total[...] = gained

    @pl.when(step > 0)
    def _():
        total[...] += gained

    @pl.when(step == pl.num_programs(0) - 1)
    def _():
        out[...] = total[...].T.astype(out.dtype)


def mlp_back(grad_ff, w_down, w_up_t, slope, kind, name):
    count, width = grad_ff.shape
    units = w_down.shape[0]
    tile = tile_of(units, count)
    return pl.pallas_call(
        back_kernel,
        grid=(units // tile,),
        in_specs=[
            pl.BlockSpec((count, width), lambda g: (0, 0)),
            pl.BlockSpec((tile, width), lambda g: (g, 0)),
            pl.BlockSpec((width, tile), lambda g: (0, g)),
            pl.BlockSpec((tile, count), lambda g: (g, 0)),
        ],
        out_specs=[
            pl.BlockSpec((tile, count), lambda g: (g, 0)),
            pl.BlockSpec((count, width), lambda g: (0, 0)),
        ],
        out_shape=[
            jax.ShapeDtypeStruct((units, count), BF),
            jax.ShapeDtypeStruct((count, width), kind),
        ],
        scratch_shapes=[pltpu.VMEM((width, count), F32)],
        compiler_params=params(),
        name=name,
    )(grad_ff, w_down, w_up_t, slope)


def weight_kernel(left_own, left_other, right_own, right_other, out):
    out[...] = (
        nn(left_own[...], right_own[...]) + nn(left_other[...], right_other[...])
    ).astype(out.dtype)


def weight_grad(left_own, left_other, right_own, right_other, name):
    units, count = left_own.shape
    others = left_other.shape[1]
    width = right_own.shape[1]
    tile = tile_of(units, others)
    return pl.pallas_call(
        weight_kernel,
        grid=(units // tile,),
        in_specs=[
            pl.BlockSpec((tile, count), lambda g: (g, 0)),
            pl.BlockSpec((tile, others), lambda g: (g, 0)),
            pl.BlockSpec((count, width), lambda g: (0, 0)),
            pl.BlockSpec((others, width), lambda g: (0, 0)),
        ],
        out_specs=pl.BlockSpec((tile, width), lambda g: (g, 0)),
        out_shape=jax.ShapeDtypeStruct((units, width), BF),
        compiler_params=params(),
        name=name,
    )(left_own, left_other, right_own, right_other)


def tail_kernel(
    norm_own, norm_other, inter, gain, crossed, mixing, grad_top, partial, proj_y, proj_p_t, slot_col, out
):
    owners, samples, slots, width = out.shape
    fields = owners * slots
    made = mixing.shape[1]
    field = lax.broadcasted_iota(jnp.int32, (fields, fields), 1)
    place = jnp.where(field == slot_col[...], 1.0, 0.0).astype(BF)
    for b in range(samples):
        at = pl.ds(b * made, made)
        upstream = norm_own[at, :]
        for w in range(norm_other.shape[0]):
            upstream = upstream + norm_other[w, at, :].astype(F32)
        unit, scale = layer_norm(inter[at, :])
        grad_inter = norm_back(unit, scale, gain[...], upstream).astype(BF)
        grad_mixing = nt(grad_inter, crossed[b]).astype(BF)
        grad_crossed = tn(mixing[b], grad_inter).astype(BF)
        grad = partial[b] + nn(proj_p_t[...], grad_mixing) + nt(proj_y[...], grad_crossed)
        top = (grad[:made] + grad_top[at, :]).astype(BF)
        grad = jnp.concatenate([top, grad[made:].astype(BF)], axis=0)
        out[:, b] = nn(place, grad).astype(BF).reshape(owners, slots, width)


def whole(kernel, shapes, name, **options):
    return pl.pallas_call(
        kernel,
        out_shape=[jax.ShapeDtypeStruct(shape, kind) for shape, kind in shapes],
        compiler_params=params(),
        name=name,
        **options,
    )


def body(
    wide,
    tables,
    bag_ids,
    bag_lengths,
    slot_field,
    proj_y,
    proj_p,
    linear_w,
    fm_gain,
    w_up,
    w_down,
    out_gain,
    cotangent,
):
    fields, width = proj_y.shape[0], tables.shape[2]
    made = proj_p.shape[0]
    cot = cotangent[0]
    samples = cot.shape[0]
    count = samples * made
    gain_fm, gain_out = fm_gain[None, :], out_gain[None, :]
    shifts = range(1, wide)

    def send(value, shift):
        return lax.ppermute(value, "wide", [(i, (i + shift) % wide) for i in range(wide)])

    def spread(value):
        return jnp.concatenate([send(value, k) for k in shifts], axis=0)

    def give_back(value):
        blocks = value.reshape(wide - 1, count, width)
        return jnp.concatenate([send(blocks[k - 1 : k], wide - k) for k in shifts], axis=0)

    pooled = pool_bags(tables, bag_ids[0], bag_lengths[0])
    owners = pooled.shape[0] // samples
    slots = pooled.shape[1]
    received = lax.all_to_all(pooled, EMB, split_axis=0, concat_axis=0, tiled=True)
    received = received.reshape(owners, samples, slots, width)
    w_up_t, w_down_t = w_up.T, w_down.T
    linear_wt, proj_p_t = linear_w.T, proj_p.T

    embeds, crossed, mixing, inter, rows = whole(
        front_kernel,
        [
            ((samples, fields, width), BF),
            ((samples, width, proj_y.shape[1]), BF),
            ((samples, made, width), BF),
            ((count, width), F32),
            ((count, width), BF),
        ],
        "front",
    )(received, slot_field[None, :], proj_y, proj_p, gain_fm)
    rows_other = spread(rows)
    layer_out, partial = whole(
        linear_kernel,
        [((samples, fields, width), BF), ((samples, fields, width), F32)],
        "linear",
    )(embeds, linear_w, linear_wt, gain_out, cot)
    hidden, slope, ff = mlp_up(rows, w_up, w_down_t, F32, "up_own")
    hidden_other, slope_other, ff_away = mlp_up(rows_other, w_up, w_down_t, BF, "up_other")
    ff_other = give_back(ff_away)

    head = pl.BlockSpec((samples, made, width), lambda g: (0, 0, 0))
    full = pl.BlockSpec(memory_space=pltpu.VMEM)
    layer_out, grad_top, grad_ff = whole(
        top_kernel,
        [((samples, fields, width), BF), ((count, width), F32), ((count, width), BF)],
        "top",
        grid=(1,),
        in_specs=[full, full, head, full, head, pl.BlockSpec(memory_space=pl.ANY)],
        out_specs=[head, full, full],
        input_output_aliases={5: 0},
    )(ff, ff_other, embeds, gain_out, cot, layer_out)
    grad_ff_other = spread(grad_ff)
    grad_gate, norm_own = mlp_back(grad_ff, w_down, w_up_t, slope, F32, "back_own")
    grad_gate_other, norm_away = mlp_back(
        grad_ff_other, w_down, w_up_t, slope_other, BF, "back_other"
    )
    norm_other = give_back(norm_away)
    down_part = weight_grad(hidden, hidden_other, grad_ff, grad_ff_other, "grad_down")
    up_part = weight_grad(grad_gate, grad_gate_other, rows, rows_other, "grad_up")
    down = lax.psum(down_part, EMB).astype(F32)
    up = lax.psum(up_part, EMB).astype(F32)
    (slot_grads,) = whole(tail_kernel, [((owners, samples, slots, width), BF)], "tail")(
        norm_own,
        norm_other,
        inter,
        gain_fm,
        crossed,
        mixing,
        grad_top,
        partial,
        proj_y,
        proj_p_t,
        slot_field[:, None],
    )
    returned = lax.all_to_all(
        slot_grads.reshape(owners * samples, slots, width), EMB, split_axis=0, concat_axis=0, tiled=True
    )
    return (layer_out[None], returned[None], up, down)


def solution(mesh):
    emb, wide = mesh.shape["emb"], mesh.shape["wide"]
    near = 2 if emb % 2 == 0 else 1
    far = 4 if (emb // near) % 4 == 0 else 1
    split = Mesh(
        mesh.devices.reshape(far, emb // near // far, near, wide), ("z", "y", "core", "wide")
    )
    return jax.shard_map(
        functools.partial(body, wide),
        mesh=split,
        in_specs=(
            P(EMB, None, None),
            P("wide", None, EMB, None),
            P("wide", None, EMB),
            P(),
            P(),
            P(),
            P(),
            P(),
            P("wide", None),
            P("wide", None),
            P(),
            P("wide", EMB, None, None),
        ),
        out_specs=(
            P("wide", EMB, None, None),
            P("wide", None, EMB, None),
            P("wide", None),
            P("wide", None),
        ),
        check_vma=False,
    )
```

time: 583 us -> 284 us (0.49)
  waiting for transfers between devices: 369 us -> 124 us
  matrix products: 74.3 us -> 0 us
  local copies, waits for them, and re-layouts: 94.5 us -> 34.2 us
  Pallas kernels: 0 us -> 59.8 us
  blocking collectives: 0 us -> 31.9 us
  other arithmetic: 14.7 us -> 7.48 us
    reduce_scatter x1 -> x0, waiting for transfers between devices: 188 us -> none  [body(): lax.psum_scatter(jnp.concatenate([up_term, down_term_part], axis=1), 'wid...]
    dot_general x14 -> x0, matrix products: 74.3 us -> none  [the longest x1 13.6 us: body(): jnp.einsum('re,he->rh', grad_ff_rows, down_all, preferred_element_type=jn...]
    pallas_call x0 -> x11, Pallas kernels: none -> 59.8 us  [the longest x2 15.6 us: mlp_up(): pl.pallas_call(up_kernel, grid=(units // tile,), in_specs=[pl.BlockSpec((...]
    all_to_all x2 -> x1, waiting for transfers between devices: 57.6 us -> 0.01 us  [body(): lax.all_to_all(slot_grads.reshape(owners * samples, slots, width), EMB, s...]
    gather x3 -> x0, local copies, waits for them, and re-layouts: 45.6 us -> none  [the longest x2 42.5 us: pool_bags(): jnp.take(tables.reshape(slots_here * bucket_count, -1), flat_ids, axis=0)]
    all_to_all x0 -> x1, blocking collectives: none -> 31.9 us  [body(): lax.all_to_all(pooled, EMB, split_axis=0, concat_axis=0, tiled=True)]
    unnamed x58 -> x86, local copies, waits for them, and re-layouts: 17.3 us -> 34.1 us
    scatter x2 -> x0, local copies, waits for them, and re-layouts: 14.5 us -> none  [body(): embeds = jnp.zeros_like(slot_embeds).at[:, slot_field].set(slot_embeds)]
  transfers between devices with their start and end apart: 6 -> 6, of which waited for: 4 -> 3; matrix products, arithmetic and copies ran while one was open for 20% -> 5% of each run, Pallas kernels for 0% -> 12%
where the time goes in v1:
time: 284 us; the launch traced here: 280 us
  waiting for transfers between devices  124 us (44%)
  Pallas kernels  59.8 us (21%)
  local copies, waits for them, and re-layouts  34.2 us (12%)
  blocking collectives  31.9 us (11%)
  between operations  14.2 us (5%)
  starting transfers between devices  9.14 us (3%)
  other arithmetic  7.48 us (3%)
    psum x1, waiting for transfers between devices, body(): up = lax.psum(up_part, EMB).astype(F32)  117 us
    unnamed x86, local copies, waits for them, and re-layouts  34.1 us
    all_to_all x1, blocking collectives, body(): lax.all_to_all(pooled, EMB, split_axis=0, concat_axis=0, tiled=True)  31.9 us
    pallas_call x2, Pallas kernels, mlp_up(): pl.pallas_call(up_kernel, grid=(units // tile,), in_specs=[pl.BlockSpec((...  15.6 us
    pallas_call x2, Pallas kernels, mlp_back(): pl.pallas_call(back_kernel, grid=(units // tile,), in_specs=[pl.BlockSpec...  13.4 us
    pallas_call x2, Pallas kernels, weight_grad(): pl.pallas_call(weight_kernel, grid=(units // tile,), in_specs=[pl.BlockSp...  11.6 us
    ppermute x4, waiting for transfers between devices, send(): lax.ppermute(value, 'wide', [(i, (i + shift) % wide) for i in range(wide)])  6.29 us
    pallas_call x1, Pallas kernels, pool_bags(): pl.pallas_call(pool_kernel, grid=(slots // step,), in_specs=[pl.BlockSpec...  6.19 us
  transfers between devices with their start and end apart: 6, of which 3 were waited for; matrix products, arithmetic and copies ran while one was open for 5% of the time, Pallas kernels for 12%

profile of v1, /device:TPU:9, one launch (start us, length us, event | category | flops | bytes accessed | tf_op | source)
XLA Modules:
  0.0 280.3 jit_solution(14752761239409515732)
XLA Ops:
  7.2 1.2 copy.22
  8.4 1.1 fusion.ids_ref
  9.6 6.2 %pool.1 = bf16[64,32,256]{2,1,0:T(8,128)(2,1)S(1)} custom-call(s32[32,64,4]{2,1,0:T(8,128)S(1)} %fusion.ids_ref, bf16[32,512,256]{2,1,0:T(8,128)(2,1)} %tables_ref.1), custom_call_target="tpu_custom_call" | custom-call | tf_op jit(solution)/shard_map/pool/pallas_call | solution.py:75
  15.8 31.9 %all_to_all.10 = bf16[64,32,256]{2,1,0:T(8,128)(2,1)S(1)} all-to-all(bf16[64,32,256]{2,1,0:T(8,128)(2,1)S(1)} %pool.1), channel_id=1, replica_groups=mesh['z'=4,'y'=2,'core'=2,'wide'=2] {'z','y','core'}, dimensions={0} | all-to-all | bytes 2097152 | tf_op jit(solution)/shard_map/all_to_all | solution.py:348
  47.7 3.0 %front.1 = (bf16[4,512,256]{2,1,0:T(8,128)(2,1)S(1)}, bf16[4,256,256]{2,1,0:T(8,128)(2,1)S(1)}, bf16[4,128,256]{2,1,0:T(8,128)(2,1)S(1)}, f32[512,256]{1,0:T(8,128)S(1)}, bf16[512,256]{1,0:T(8,128)(2,1)S(1)}) custom-call(bf16[16,4,32,256]{3,2,1,0:T(8,128)(2,1)S(1)} %bitcast.28, s32[1,512]{1,0:T(1,128)S(1)} %bitcast.31, bf16[512,256]{1,0:T(8,128)(2,1)S(1)} %copy-done.22, ...), custom_call_target="tpu_custom_call" | custom-call | tf_op jit(solution)/shard_map/front/pallas_call | solution.py:353
  50.8 1.0 copy-done.6
  51.7 0.8 copy-done.26
  52.5 0.8 copy-done.28
  53.3 0.7 copy-done.34
  54.0 1.2 collective-permute-start
  55.2 4.1 %copy.23 = bf16[4096,256]{0,1:T(8,128)(2,1)} copy(bf16[4096,256]{1,0:T(8,128)(2,1)} %w_down.3) | data formatting | bytes 4194304 | tf_op args[9]
  59.3 2.7 collective-permute-done.rows.right_other
  62.0 0.7 copy-done.19
  62.7 1.6 copy-done.1
  64.3 0.9 copy-done.20
  65.3 7.8 %up_other.1 = (bf16[4096,512]{1,0:T(8,128)(2,1)S(1)}, bf16[4096,512]{1,0:T(8,128)(2,1)}, bf16[512,256]{1,0:T(8,128)(2,1)}) custom-call(bf16[512,256]{1,0:T(8,128)(2,1)S(1)} %copy-done.20, bf16[4096,256]{1,0:T(8,128)(2,1)S(1)} %copy-done, bf16[256,4096]{1,0:T(8,128)(2,1)S(1)} %bitcast.22), custom_call_target="tpu_custom_call" | custom-call | tf_op jit(solution)/shard_map/up_other/pallas_call | solution.py:162
  73.1 2.0 copy-done.8
  75.1 1.2 collective-permute-start.1
  76.3 0.9 copy.24
  77.2 1.6 copy-done.2
  78.8 0.9 copy-done.17
  79.8 7.8 %up_own.1 = (bf16[4096,512]{1,0:T(8,128)(2,1)S(1)}, bf16[4096,512]{1,0:T(8,128)(2,1)}, f32[512,256]{1,0:T(8,128)S(1)}) custom-call(bf16[512,256]{1,0:T(8,128)(2,1)S(1)} %copy-done.17, bf16[4096,256]{1,0:T(8,128)(2,1)S(1)} %copy-done, bf16[256,4096]{1,0:T(8,128)(2,1)S(1)} %bitcast.23), custom_call_target="tpu_custom_call" | custom-call | tf_op jit(solution)/shard_map/up_own/pallas_call | solution.py:162
  87.6 2.0 copy-done.9
  89.6 2.7 linear.1
  92.3 2.3 top.1
  94.7 0.8 copy-done.30
  95.5 0.2 collective-permute-start.2
  95.7 3.0 %copy.25 = bf16[4096,256]{0,1:T(8,128)(2,1)} copy(bf16[4096,256]{1,0:T(8,128)(2,1)S(1)} %copy-done) | data formatting | bytes 4194304 | tf_op args[8]
  98.7 3.6 %collective-permute-done.2.grad_ff.right_other = bf16[512,256]{1,0:T(8,128)(2,1)S(1)} collective-permute-done((bf16[512,256]{1,0:T(8,128)(2,1)S(1)}, bf16[512,256]{1,0:T(8,128)(2,1)S(1)}, u32[]{:S(2)}, u32[]{:S(2)}) %collective-permute-start.2) | collective-permute-done | bytes 262176 | tf_op jit(solution)/shard_map/ppermute | solution.py:336
  102.3 1.6 copy-done.3
  103.9 1.6 copy-done.4
  105.4 7.0 %back_other.1 = (bf16[4096,512]{1,0:T(8,128)(2,1)S(1)}, bf16[512,256]{1,0:T(8,128)(2,1)}) custom-call(bf16[512,256]{1,0:T(8,128)(2,1)S(1)} %collective-permute-done.2.grad_ff.right_other, bf16[4096,256]{1,0:T(8,128)(2,1)S(1)} %copy-done.3, bf16[256,4096]{1,0:T(8,128)(2,1)S(1)} %bitcast.24, bf16[4096,512]{1,0:T(8,128)(2,1)} %get-tuple-element.33.slope), custom_call_target="tpu_custom_call" | custom-call | tf_op jit(solution)/shard_map/back_other/pallas_call | solution.py:229
  112.4 2.0 copy-done.11
  114.4 0.3 collective-permute-start.3
  114.7 6.5 %back_own.1 = (bf16[4096,512]{1,0:T(8,128)(2,1)S(1)}, f32[512,256]{1,0:T(8,128)S(1)}) custom-call(bf16[512,256]{1,0:T(8,128)(2,1)S(1)} %get-tuple-element.30.grad_ff.right_own, bf16[4096,256]{1,0:T(8,128)(2,1)S(1)} %copy-done.3, bf16[256,4096]{1,0:T(8,128)(2,1)S(1)} %bitcast.25, bf16[4096,512]{1,0:T(8,128)(2,1)} %get-tuple-element.31.slope), custom_call_target="tpu_custom_call" | custom-call | tf_op jit(solution)/shard_map/back_own/pallas_call | solution.py:229
  121.2 5.9 %grad_down.1 = bf16[4096,256]{1,0:T(8,128)(2,1)} custom-call(bf16[4096,512]{1,0:T(8,128)(2,1)S(1)} %copy-done.10, bf16[4096,512]{1,0:T(8,128)(2,1)} %copy-done.8, bf16[512,256]{1,0:T(8,128)(2,1)S(1)} %get-tuple-element.30.grad_ff.right_own, bf16[512,256]{1,0:T(8,128)(2,1)S(1)} %collective-permute-done.2.grad_ff.right_other), custom_call_target="tpu_custom_call" | custom-call | tf_op jit(solution)/shard_map/grad_down/pallas_call | solution.py:263
  127.1 5.7 %grad_up.1 = bf16[4096,256]{1,0:T(8,128)(2,1)} custom-call(bf16[4096,512]{1,0:T(8,128)(2,1)S(1)} %get-tuple-element.40.left_own, bf16[4096,512]{1,0:T(8,128)(2,1)} %copy-done.11, bf16[512,256]{1,0:T(8,128)(2,1)S(1)} %copy-done.18, bf16[512,256]{1,0:T(8,128)(2,1)S(1)} %copy-done.21), custom_call_target="tpu_custom_call" | custom-call | tf_op jit(solution)/shard_map/grad_up/pallas_call | solution.py:263
  132.9 0.9 copy-done.25
  134.0 0.5 copy-done.13
  134.7 1.0 copy-done.29
  135.7 1.0 copy-done.31
  136.8 1.0 copy-done.33
  137.8 4.9 %tail.1 = bf16[16,4,32,256]{3,2,1,0:T(8,128)(2,1)} custom-call(f32[512,256]{1,0:T(8,128)S(1)} %copy-done.33, bf16[1,512,256]{2,1,0:T(8,128)(2,1)} %collective-permute-done.3.norm_other, f32[512,256]{1,0:T(8,128)S(1)} %copy-done.29, f32[1,256]{1,0:T(1,128)S(1)} %bitcast.36, bf16[4,256,256]{2,1,0:T(8,128)(2,1)S(1)} %copy-done.27, ...), custom_call_target="tpu_custom_call" | custom-call | tf_op jit(solution)/shard_map/tail/pallas_call | solution.py:395
  142.7 6.2 %all-to-all-start.1 = ((bf16[64,32,256]{2,1,0:T(8,128)(2,1)}), bf16[64,32,256]{2,1,0:T(8,128)(2,1)S(1)}, u32[]{:S(2)}, u32[]{:S(2)}) async-start(bf16[64,32,256]{2,1,0:T(8,128)(2,1)} %bitcast.16), calls=%async_computation.1 | async-start | bytes 2097152 | tf_op jit(solution)/shard_map/all_to_all | solution.py:408
  148.8 117.2 %all-reduce.3.cloned.1.call-done = (bf16[4096,256]{1,0:T(8,128)(2,1)}, bf16[4096,256]{1,0:T(8,128)(2,1)}) async-done(((bf16[4096,256]{1,0:T(8,128)(2,1)}, bf16[4096,256]{1,0:T(8,128)(2,1)}), (bf16[4096,256]{1,0:T(8,128)(2,1)}, bf16[4096,256]{1,0:T(8,128)(2,1)})) %all-reduce.3.cloned.1.call-update) | async-done | bytes 4194320 | tf_op jit(solution)/shard_map/psum | solution.py:394
  266.1 4.1 %convert_element_type.6 = f32[4096,256]{1,0:T(8,128)} convert(bf16[4096,256]{1,0:T(8,128)(2,1)} %get-tuple-element.44) | non-fusion elementwise | flops 1048576 | bytes 6291456 | tf_op jit(solution)/shard_map/convert_element_type | solution.py:394
  270.2 2.3 convert_element_type.7
  272.5 1.0 copy.32
  (67 shorter events, 0.7 us)
Async XLA Ops:
  7.2 258.9 %all-reduce.3.cloned.1.call-start = ((), (), s32[]{:S(2)}) async-start(), calls=%async_computation.2 | async-start | bytes 8388608 | tf_op jit(solution)/shard_map/psum | solution.py:394
  9.5 38.2 %copy-start.22 = (bf16[512,256]{1,0:T(8,128)(2,1)S(1)}, bf16[512,256]{1,0:T(8,128)(2,1)}, u32[]{:S(2)}) copy-start(bf16[512,256]{1,0:T(8,128)(2,1)} %proj_y.3) | copy-start | bytes 786436
  9.5 38.2 %copy-start.24 = (bf16[128,512]{1,0:T(8,128)(2,1)S(1)}, bf16[128,512]{1,0:T(8,128)(2,1)}, u32[]{:S(2)}) copy-start(bf16[128,512]{1,0:T(8,128)(2,1)} %proj_p.1) | copy-start | bytes 393220
  9.5 38.2 %copy-start.36 = (s32[512]{0:T(512)S(1)}, s32[512]{0:T(512)}, u32[]{:S(2)}) copy-start(s32[512]{0:T(512)} %param.15) | copy-start | bytes 6148
  9.5 38.2 %copy-start.38 = (f32[256]{0:T(256)S(1)}, f32[256]{0:T(256)}, u32[]{:S(2)}) copy-start(f32[256]{0:T(256)} %param.19) | copy-start | bytes 3076
  15.8 47.0 %copy-start = (bf16[4096,256]{1,0:T(8,128)(2,1)S(1)}, bf16[4096,256]{1,0:T(8,128)(2,1)}, u32[]{:S(2)}) copy-start(bf16[4096,256]{1,0:T(8,128)(2,1)} %w_up.3) | copy-start | bytes 6291460
  50.8 1.0 copy-start.6
  51.7 0.8 copy-start.26
  52.5 0.8 copy-start.28
  53.3 0.7 copy-start.34
  54.0 8.0 %copy-start.16 = (bf16[512,256]{1,0:T(8,128)(2,1)}, bf16[512,256]{1,0:T(8,128)(2,1)S(1)}, u32[]{:S(2)}) copy-start(bf16[512,256]{1,0:T(8,128)(2,1)S(1)} %get-tuple-element.24.rows.right_own) | copy-start | bytes 786436
  54.0 22.3 %copy-start.14 = (bf16[384,512]{1,0:T(8,128)(2,1)S(1)}, bf16[384,512]{1,0:T(8,128)(2,1)}, u32[]{:S(2)}) copy-start(bf16[384,512]{1,0:T(8,128)(2,1)} %linear_w.1) | copy-start | bytes 1179652
  54.0 8.0 %collective-permute-start = (bf16[512,256]{1,0:T(8,128)(2,1)S(1)}, bf16[512,256]{1,0:T(8,128)(2,1)S(1)}, u32[]{:S(2)}, u32[]{:S(2)}) collective-permute-start(bf16[512,256]{1,0:T(8,128)(2,1)S(1)} %get-tuple-element.24.rows.right_own), channel_id=1, source_target_pairs={{0,1},{1,0},{2,3},{3,2},{4,5},{5,4},{6,7},{7,6},{8,9},{9,8},{10,11... | collective-permute-start | bytes 786440 | tf_op jit(solution)/shard_map/ppermute | solution.py:336
  62.0 0.7 copy-start.19
  62.7 1.6 copy-start.1
  64.3 0.9 copy-start.20
  65.3 24.3 %copy-start.5 = (bf16[1,4,512,256]{3,2,1,0:T(8,128)(2,1)S(1)}, bf16[1,4,512,256]{3,2,1,0:T(8,128)(2,1)}, u32[]{:S(2)}) copy-start(bf16[1,4,512,256]{3,2,1,0:T(8,128)(2,1)} %param.23) | copy-start | bytes 3145732
  65.3 24.3 %copy-start.37 = (f32[256]{0:T(256)S(1)}, f32[256]{0:T(256)}, u32[]{:S(2)}) copy-start(f32[256]{0:T(256)} %param.22) | copy-start | bytes 3076
  73.1 2.0 copy-start.8
  75.1 17.3 %collective-permute-start.1 = (bf16[1,512,256]{2,1,0:T(8,128)(2,1)}, bf16[1,512,256]{2,1,0:T(8,128)(2,1)}, u32[]{:S(2)}, u32[]{:S(2)}) collective-permute-start(bf16[1,512,256]{2,1,0:T(8,128)(2,1)} %bitcast.7), channel_id=1, source_target_pairs={{0,1},{1,0},{2,3},{3,2},{4,5},{5,4},{6,7},{7,6},{8,9},{9,8},{10,11... | collective-permute-start | bytes 786440 | tf_op jit(solution)/shard_map/ppermute | solution.py:336
  77.2 1.6 copy-start.2
  78.8 0.9 copy-start.17
  79.7 9.8 %copy-start.7 = (bf16[4,512,256]{2,1,0:T(8,128)(2,1)S(1)}, bf16[4,512,256]{2,1,0:T(8,128)(2,1)}, u32[]{:S(2)}) copy-start(bf16[4,512,256]{2,1,0:T(8,128)(2,1)} %copy-done.6) | copy-start | bytes 3145732
  79.7 9.8 %copy-start.15 = (bf16[384,512]{0,1:T(8,128)(2,1)S(1)}, bf16[384,512]{0,1:T(8,128)(2,1)}, u32[]{:S(2)}) copy-start(bf16[384,512]{0,1:T(8,128)(2,1)} %copy.24) | copy-start | bytes 1179652
  87.6 2.0 copy-start.9
  92.3 2.3 copy-start.12
  94.6 0.8 copy-start.30
  95.5 6.8 %collective-permute-start.2 = (bf16[512,256]{1,0:T(8,128)(2,1)S(1)}, bf16[512,256]{1,0:T(8,128)(2,1)S(1)}, u32[]{:S(2)}, u32[]{:S(2)}) collective-permute-start(bf16[512,256]{1,0:T(8,128)(2,1)S(1)} %get-tuple-element.30.grad_ff.right_own), channel_id=1, source_target_pairs={{0,1},{1,0},{2,3},{3,2},{4,5},{5,4},{6,7},{7,6},{8,9},{9,8},{10,11... | collective-permute-start | bytes 786440 | tf_op jit(solution)/shard_map/ppermute | solution.py:336
  102.3 1.6 copy-start.3
  103.8 1.6 copy-start.4
  112.4 2.0 copy-start.11
  114.4 19.6 %collective-permute-start.3 = (bf16[1,512,256]{2,1,0:T(8,128)(2,1)}, bf16[1,512,256]{2,1,0:T(8,128)(2,1)}, u32[]{:S(2)}, u32[]{:S(2)}) collective-permute-start(bf16[1,512,256]{2,1,0:T(8,128)(2,1)} %bitcast.13), channel_id=1, source_target_pairs={{0,1},{1,0},{2,3},{3,2},{4,5},{5,4},{6,7},{7,6},{8,9},{9,8},{10,11... | collective-permute-start | bytes 786440 | tf_op jit(solution)/shard_map/ppermute | solution.py:336
  114.7 6.5 %copy-start.10 = (bf16[4096,512]{1,0:T(8,128)(2,1)S(1)}, bf16[4096,512]{1,0:T(8,128)(2,1)}, u32[]{:S(2)}) copy-start(bf16[4096,512]{1,0:T(8,128)(2,1)} %copy-done.9) | copy-start | bytes 12582916
  121.2 5.9 %copy-start.32 = (f32[512,256]{1,0:T(8,128)}, f32[512,256]{1,0:T(8,128)S(1)}, u32[]{:S(2)}) copy-start(f32[512,256]{1,0:T(8,128)S(1)} %get-tuple-element.32.norm_own) | copy-start | bytes 1572868
  121.2 5.9 %copy-start.18 = (bf16[512,256]{1,0:T(8,128)(2,1)S(1)}, bf16[512,256]{1,0:T(8,128)(2,1)}, u32[]{:S(2)}) copy-start(bf16[512,256]{1,0:T(8,128)(2,1)} %copy-done.16) | copy-start | bytes 786436
  121.2 5.9 %copy-start.21 = (bf16[512,256]{1,0:T(8,128)(2,1)S(1)}, bf16[512,256]{1,0:T(8,128)(2,1)}, u32[]{:S(2)}) copy-start(bf16[512,256]{1,0:T(8,128)(2,1)} %copy-done.19) | copy-start | bytes 786436
  132.8 0.9 copy-start.25
  132.8 1.7 copy-start.13
  132.8 1.7 copy-start.23
  132.8 1.8 copy-start.27
  132.8 1.9 copy-start.35
  134.7 1.0 copy-start.29
  135.7 1.0 copy-start.31
  136.8 1.0 copy-start.33
  142.7 129.8 %all-to-all-start.1 = ((bf16[64,32,256]{2,1,0:T(8,128)(2,1)}), bf16[64,32,256]{2,1,0:T(8,128)(2,1)S(1)}, u32[]{:S(2)}, u32[]{:S(2)}) async-start(bf16[64,32,256]{2,1,0:T(8,128)(2,1)} %bitcast.16), calls=%async_computation.1 | async-start | bytes 2097152 | tf_op jit(solution)/shard_map/all_to_all | solution.py:408
  266.1 4.1 %copy-start.39 = (bf16[4096,256]{1,0:T(8,128)(2,1)S(1)}, bf16[4096,256]{1,0:T(8,128)(2,1)}, u32[]{:S(2)}) copy-start(bf16[4096,256]{1,0:T(8,128)(2,1)} %get-tuple-element.45) | copy-start | bytes 6291460
Sparse Core Ops, SparseCore 0:
  133.0 133.0 all-reduce.2

commit v2 on v0

v2 whole, which is shorter than its diff:
```python
import functools

import jax
import jax.numpy as jnp
from jax import lax
from jax.experimental import pallas as pl
from jax.experimental.pallas import tpu as pltpu
from jax.sharding import Mesh
from jax.sharding import PartitionSpec as P

norm_eps = 1e-05
VMEM_BYTES = 48 * 1024 * 1024
BF = jnp.bfloat16
F32 = jnp.float32
LANES = 128
EMB = ("z", "y", "core")


def params():
    return pltpu.CompilerParams(vmem_limit_bytes=VMEM_BYTES)


def nn(left, right):
    return lax.dot_general(left, right, (((1,), (0,)), ((), ())), preferred_element_type=F32)


def nt(left, right):
    return lax.dot_general(left, right, (((1,), (1,)), ((), ())), preferred_element_type=F32)


def tn(left, right):
    return lax.dot_general(left, right, (((0,), (0,)), ((), ())), preferred_element_type=F32)


def layer_norm(values):
    centre = jnp.mean(values, axis=-1, keepdims=True)
    shifted = values - centre
    scale = lax.rsqrt(jnp.mean(shifted * shifted, axis=-1, keepdims=True) + norm_eps)
    return (shifted * scale, scale)


def norm_back(unit, scale, gain, upstream):
    scaled = upstream * gain
    return scale * (
        scaled
        - jnp.mean(scaled, axis=-1, keepdims=True)
        - unit * jnp.mean(scaled * unit, axis=-1, keepdims=True)
    )


def pool_kernel(ids_ref, tables_ref, *refs):
    outs, sums = refs[:-1], refs[-1]
    slots, samples, bag = ids_ref.shape
    buckets = tables_ref.shape[1]
    here = outs[0].shape[1]
    bucket = lax.broadcasted_iota(jnp.int32, (samples, buckets), 1)
    for s in range(slots):
        ids = ids_ref[s]
        count = jnp.zeros((samples, buckets), F32)
        for j in range(bag):
            count = count + jnp.where(ids[:, j : j + 1] == bucket, 1.0, 0.0)
        bags = nn(count.astype(BF), tables_ref[s])
        for c in range(sums.shape[0]):
            sums[c, pl.ds(s * samples, samples), :] = bags[:, c * LANES : (c + 1) * LANES]
    for b in range(samples):
        owner, local = divmod(b, here * len(outs))
        out = outs[local // here]
        for c in range(sums.shape[0]):
            bag_sums = sums.at[c][pl.ds(b, slots, stride=samples), :]
            out[owner, local % here, :, c * LANES : (c + 1) * LANES] = bag_sums.astype(BF)


def pool_bags(tables, ids, lengths, owners, halves):
    slots, buckets, width = tables.shape
    samples, _, bag = ids.shape
    here = samples // owners // halves
    live = jnp.arange(bag, dtype=jnp.int32)[None, None, :] < lengths[:, :, None]
    masked = jnp.where(live, ids, -1).transpose(1, 0, 2)
    step = 16 if slots % 16 == 0 else slots
    return pl.pallas_call(
        pool_kernel,
        grid=(slots // step,),
        in_specs=[
            pl.BlockSpec((step, samples, bag), lambda g: (g, 0, 0)),
            pl.BlockSpec((step, buckets, width), lambda g: (g, 0, 0)),
        ],
        out_specs=[pl.BlockSpec((owners, here, step, width), lambda g: (0, 0, g, 0))] * halves,
        out_shape=[jax.ShapeDtypeStruct((owners, here, slots, width), BF)] * halves,
        scratch_shapes=[pltpu.VMEM((width // LANES, step * samples, LANES), F32)],
        compiler_params=params(),
        name="pool",
    )(masked, tables)


def const(*shape):
    return pl.BlockSpec(shape, lambda *_: (0,) * len(shape))


def by_sample(*shape):
    return pl.BlockSpec(shape, lambda b: (b,) + (0,) * (len(shape) - 1))


def front_kernel(rec, slot_row, proj_y, proj_p, gain, embeds, crossed, mixing, inter, rows, place):
    owners, _, slots, width = rec.shape
    fields = owners * slots

    @pl.when(pl.program_id(0) == 0)
    def _():
        field = lax.broadcasted_iota(jnp.int32, (fields, fields), 0)
        place[...] = jnp.where(field == slot_row[...], 1.0, 0.0).astype(BF)

    x = nn(place[...], rec[:, 0].reshape(fields, width)).astype(BF)
    embeds[0] = x
    c = tn(x, proj_y[...]).astype(BF)
    crossed[0] = c
    m = nn(proj_p[...], x).astype(BF)
    mixing[0] = m
    v = nn(m, c)
    inter[...] = v
    unit, _ = layer_norm(v)
    rows[...] = (unit * gain[...]).astype(BF)


def front(received, slot_field, proj_y, proj_p, gain, name):
    owners, here, slots, width = received.shape
    fields, rank = proj_y.shape
    made = proj_p.shape[0]
    return pl.pallas_call(
        front_kernel,
        grid=(here,),
        in_specs=[
            pl.BlockSpec((owners, 1, slots, width), lambda b: (0, b, 0, 0)),
            const(1, fields),
            const(fields, rank),
            const(made, fields),
            const(1, rank),
        ],
        out_specs=[
            by_sample(1, fields, width),
            by_sample(1, width, rank),
            by_sample(1, made, width),
            by_sample(made, rank),
            by_sample(made, rank),
        ],
        out_shape=[
            jax.ShapeDtypeStruct((here, fields, width), BF),
            jax.ShapeDtypeStruct((here, width, rank), BF),
            jax.ShapeDtypeStruct((here, made, width), BF),
            jax.ShapeDtypeStruct((here * made, rank), F32),
            jax.ShapeDtypeStruct((here * made, rank), BF),
        ],
        scratch_shapes=[pltpu.VMEM((fields, fields), BF)],
        compiler_params=params(),
        name=name,
    )(received, slot_field[None, :], proj_y, proj_p, gain)


def linear_kernel(embeds, linear_w, gain, cot, *refs):
    layer_out, partial = refs[-2:]
    made = linear_w.shape[0]
    first = embeds.shape[1] - made
    x = embeds[0]
    summed = nn(linear_w[...], x) + x[first:].astype(F32)
    unit, scale = layer_norm(summed)
    layer_out[0, :first] = jnp.zeros_like(layer_out[0, :first])
    layer_out[0, first:] = (unit * gain[...]).astype(BF)
    grad = norm_back(unit, scale, gain[...], cot[0, first:].astype(F32))
    back = tn(linear_w[...], grad.astype(BF))
    partial[0, :first] = back[:first]
    partial[0, first:] = back[first:] + grad


def linear(embeds, linear_w, gain, cot, layer_out, start, name):
    here, fields, width = embeds.shape
    at_sample = pl.BlockSpec((1, fields, width), lambda b: (start + b, 0, 0))
    filled = [] if layer_out is None else [layer_out]
    return pl.pallas_call(
        linear_kernel,
        grid=(here,),
        in_specs=[
            by_sample(1, fields, width),
            const(*linear_w.shape),
            const(1, width),
            at_sample,
        ]
        + [pl.BlockSpec(memory_space=pl.ANY)] * len(filled),
        out_specs=[at_sample, by_sample(1, fields, width)],
        out_shape=[
            jax.ShapeDtypeStruct(cot.shape, BF),
            jax.ShapeDtypeStruct((here, fields, width), F32),
        ],
        input_output_aliases={4: 0} if filled else {},
        compiler_params=params(),
        name=name,
    )(embeds, linear_w, gain, cot, *filled)


def activate(gate):
    sig = 0.5 * jnp.tanh(0.5 * gate) + 0.5
    h = gate * sig
    return (h.astype(BF), sig + h * (1.0 - sig))


def up_kernel(rows_own, rows_other, w_up, w_down, out_own, out_other, rows, total):
    step = pl.program_id(0)
    own = rows_own.shape[0]

    @pl.when(step == 0)
    def _():
        rows[:own] = rows_own[...]
        rows[own:] = rows_other[...]

    hidden, _ = activate(nt(w_up[...], rows[...]))
    term = tn(w_down[...], hidden)

    @pl.when(step == 0)
    def _():
        total[...] = term

    @pl.when(step > 0)
    def _():
        total[...] += term

    @pl.when(step == pl.num_programs(0) - 1)
    def _():
        out_own[...] = total[:, :own].T
        out_other[...] = total[:, own:].T.astype(BF)


def mlp_up(rows_own, rows_other, w_up, w_down, name):
    own, width = rows_own.shape
    other = rows_other.shape[0]
    units = w_up.shape[0]
    tile = min(units, 1024 if own + other <= 1024 else 256)
    return pl.pallas_call(
        up_kernel,
        grid=(units // tile,),
        in_specs=[
            const(own, width),
            const(other, width),
            pl.BlockSpec((tile, width), lambda g: (g, 0)),
            pl.BlockSpec((tile, width), lambda g: (g, 0)),
        ],
        out_specs=[const(own, width), const(other, width)],
        out_shape=[
            jax.ShapeDtypeStruct((own, width), F32),
            jax.ShapeDtypeStruct((other, width), BF),
        ],
        scratch_shapes=[
            pltpu.VMEM((own + other, width), BF),
            pltpu.VMEM((width, own + other), F32),
        ],
        compiler_params=params(),
        name=name,
    )(rows_own, rows_other, w_up, w_down)


def top_kernel(ff_own, ff_other, embeds, gain, cot, _, layer_out, grad, grad_ff):
    summed = ff_own[...] + embeds[0].astype(F32)
    for w in range(ff_other.shape[0]):
        summed = summed + ff_other[w].astype(F32)
    unit, scale = layer_norm(summed)
    layer_out[0] = (unit * gain[...]).astype(BF)
    g = norm_back(unit, scale, gain[...], cot[0].astype(F32))
    grad[...] = g
    grad_ff[...] = g.astype(BF)


def top(ff_own, ff_other, embeds, gain, cot, layer_out, start, made, name):
    here, _, width = embeds.shape
    count = here * made
    at_sample = pl.BlockSpec((1, made, width), lambda b: (start + b, 0, 0))
    return pl.pallas_call(
        top_kernel,
        grid=(here,),
        in_specs=[
            by_sample(made, width),
            pl.BlockSpec((ff_other.shape[0], made, width), lambda b: (0, b, 0)),
            by_sample(1, made, width),
            const(1, width),
            at_sample,
            pl.BlockSpec(memory_space=pl.ANY),
        ],
        out_specs=[at_sample, by_sample(made, width), by_sample(made, width)],
        out_shape=[
            jax.ShapeDtypeStruct(cot.shape, BF),
            jax.ShapeDtypeStruct((count, width), F32),
            jax.ShapeDtypeStruct((count, width), BF),
        ],
        input_output_aliases={5: 0},
        compiler_params=params(),
        name=name,
    )(ff_own, ff_other, embeds, gain, cot, layer_out)


def back_kernel(blocks, begun, last, _, *refs):
    rows_in, grads_in = refs[:blocks], refs[blocks : 2 * blocks]
    w_up, w_down = refs[2 * blocks : 2 * blocks + 2]
    refs = refs[2 * blocks + 2 :]
    if begun:
        before, refs = refs[0], refs[1:]
    grad_down, grad_up = refs[:2]
    outs = refs[2:-3] if last else refs[2:3]
    rows, grads = refs[-2:]
    total = refs[-3] if last else outs[0]
    step = pl.program_id(0)

    @pl.when(step == 0)
    def _():
        at = 0
        for row_block, grad_block in zip(rows_in, grads_in):
            count = row_block.shape[0]
            rows[at : at + count] = row_block[...]
            grads[at : at + count] = grad_block[...]
            at += count
        total[...] = before[...] if begun else jnp.zeros_like(total)

    shares, _, units, width = w_up.shape
    up = w_up[...].reshape(shares * units, width)
    down = w_down[...].reshape(shares * units, width)
    hidden, slope = activate(nt(up, rows[...]))
    gate = (nt(down, grads[...]) * slope).astype(BF)
    grad_down[...] = nn(hidden, grads[...]).astype(grad_down.dtype).reshape(shares, units, width)
    grad_up[...] = nn(gate, rows[...]).astype(grad_up.dtype).reshape(shares, units, width)
    total[...] += tn(up, gate)

    if last:

        @pl.when(step == pl.num_programs(0) - 1)
        def _():
            at = 0
            for out in outs:
                count = out.shape[0]
                out[...] = total[:, at : at + count].T.astype(out.dtype)
                at += count


def mlp_back(half, rows, grads, w_up, w_down, before, kind, row_kinds, name):
    shares, _, units, width = w_up.shape
    blocks = len(rows)
    count = sum(block.shape[0] for block in rows)
    last = row_kinds is not None
    step = max(1, min(shares, 512 // units if count <= 1024 else 128 // units))
    shared = pl.BlockSpec((step, 1, units, width), lambda g, at: (g, at[0], 0, 0))
    given = pl.BlockSpec((step, units, width), lambda g, at: (g, 0, 0))
    if last:
        outs = [jax.ShapeDtypeStruct(block.shape, k) for block, k in zip(rows, row_kinds)]
    else:
        outs = [jax.ShapeDtypeStruct((width, count), F32)]
    begun = [] if before is None else [before]
    return pl.pallas_call(
        functools.partial(back_kernel, blocks, bool(begun), last),
        grid_spec=pltpu.PrefetchScalarGridSpec(
            num_scalar_prefetch=1,
            grid=(shares // step,),
            in_specs=[const(*block.shape) for block in (*rows, *grads)]
            + [shared, shared]
            + [const(*block.shape) for block in begun],
            out_specs=[given, given] + [const(*out.shape) for out in outs],
            scratch_shapes=([pltpu.VMEM((width, count), F32)] if last else [])
            + [pltpu.VMEM((count, width), BF)] * 2,
        ),
        out_shape=[jax.ShapeDtypeStruct((shares, units, width), kind)] * 2 + outs,
        compiler_params=params(),
        name=name,
    )(half, *rows, *grads, w_up, w_down, *begun)


def split_kernel(count, each, at, *refs):
    ins, outs = refs[: -count * len(each)], refs[-count * len(each) :]
    for k in reversed(range(count)):
        here = lax.rem(at[0] + k, count)
        first = 0
        for n, terms in enumerate(each):
            total = ins[first][:, here].astype(F32)
            for ref in ins[first + 1 : first + terms]:
                total = total + ref[:, here].astype(F32)
            out = outs[n * count + k]
            out[...] = total.astype(out.dtype)
            first += terms


def split_sum(at, count, sums, kind, name):
    outs = []
    for arrays in sums:
        before, _, units, width = arrays[0].shape
        outs += [((before, units, width), kind if k == 0 else BF) for k in range(count)]
    pieces = whole(
        functools.partial(split_kernel, count, [len(arrays) for arrays in sums]),
        outs,
        name,
        in_specs=[pl.BlockSpec(memory_space=pltpu.SMEM)]
        + [pl.BlockSpec(memory_space=pltpu.VMEM)] * sum(len(arrays) for arrays in sums),
    )(at, *[array for arrays in sums for array in arrays])
    return [pieces[n * count : (n + 1) * count] for n in range(len(sums))]


def join_kernel(at, *refs):
    ins, out = refs[:-1], refs[-1]
    count = len(ins)
    for k, ref in enumerate(ins):
        out[:, lax.rem(at[0] + (count - k), count)] = ref[...].astype(out.dtype)


def join(at, arrays, kind, name):
    before, units, width = arrays[0].shape
    (out,) = whole(
        join_kernel,
        [((before, len(arrays), units, width), kind)],
        name,
        in_specs=[pl.BlockSpec(memory_space=pltpu.SMEM)]
        + [pl.BlockSpec(memory_space=pltpu.VMEM)] * len(arrays),
    )(at, *arrays)
    return out


def tail_kernel(
    norm_own, norm_other, inter, gain, crossed, mixing, grad_top, partial, proj_y, proj_p, slot_col, *refs
):
    out, place = refs[-2:]
    owners, _, slots, width = out.shape
    fields = owners * slots
    made = mixing.shape[1]

    @pl.when(pl.program_id(0) == 0)
    def _():
        field = lax.broadcasted_iota(jnp.int32, (fields, fields), 1)
        place[...] = jnp.where(field == slot_col[...], 1.0, 0.0).astype(BF)

    upstream = norm_own[...]
    for w in range(norm_other.shape[0]):
        upstream = upstream + norm_other[w].astype(F32)
    unit, scale = layer_norm(inter[...])
    grad_inter = norm_back(unit, scale, gain[...], upstream).astype(BF)
    grad_mixing = nt(grad_inter, crossed[0]).astype(BF)
    grad_crossed = tn(mixing[0], grad_inter).astype(BF)
    grad = partial[0] + tn(proj_p[...], grad_mixing) + nt(proj_y[...], grad_crossed)
    head = (grad[:made] + grad_top[...]).astype(BF)
    grad = jnp.concatenate([head, grad[made:].astype(BF)], axis=0)
    out[:, 0] = nn(place[...], grad).astype(BF).reshape(owners, slots, width)


def tail(own, other, kept, gain, proj_y, proj_p, slot_field, filled, start, shape, name):
    inter, crossed, mixing, grad_top, partial = kept
    owners, _, slots, width = shape
    here, fields, _ = partial.shape
    rank = proj_y.shape[1]
    made = mixing.shape[1]
    filled = [] if filled is None else [filled]
    return pl.pallas_call(
        tail_kernel,
        grid=(here,),
        in_specs=[
            by_sample(made, width),
            pl.BlockSpec((other.shape[0], made, width), lambda b: (0, b, 0)),
            by_sample(made, rank),
            const(1, rank),
            by_sample(1, width, rank),
            by_sample(1, made, width),
            by_sample(made, width),
            by_sample(1, fields, width),
            const(fields, rank),
            const(made, fields),
            const(fields, 1),
        ]
        + [pl.BlockSpec(memory_space=pl.ANY)] * len(filled),
        out_specs=pl.BlockSpec((owners, 1, slots, width), lambda b: (0, start + b, 0, 0)),
        out_shape=jax.ShapeDtypeStruct(shape, BF),
        scratch_shapes=[pltpu.VMEM((fields, fields), BF)],
        input_output_aliases={11: 0} if filled else {},
        compiler_params=params(),
        name=name,
    )(
        own,
        other,
        inter,
        gain,
        crossed,
        mixing,
        grad_top,
        partial,
        proj_y,
        proj_p,
        slot_field[:, None],
        *filled,
    )


def whole(kernel, shapes, name, **options):
    return pl.pallas_call(
        kernel,
        out_shape=[jax.ShapeDtypeStruct(shape, kind) for shape, kind in shapes],
        compiler_params=params(),
        name=name,
        **options,
    )


def turn(value, axis, size, shift):
    return lax.ppermute(value, axis, [(i, (i + shift) % size) for i in range(size)])


def after(value, *others):
    return lax.optimization_barrier((value, *others))[0]


def body(
    sizes,
    tables,
    bag_ids,
    bag_lengths,
    slot_field,
    proj_y,
    proj_p,
    linear_w,
    fm_gain,
    w_up,
    w_down,
    out_gain,
    cotangent,
):
    wide = sizes["wide"]
    near, mid, far = sizes["core"], sizes["y"], sizes["z"]
    owners = near * mid * far
    width = tables.shape[2]
    made = proj_p.shape[0]
    cot = cotangent[0]
    samples = cot.shape[0]
    halves = 2 if samples % 2 == 0 else 1
    here = samples // halves
    gain_fm, gain_out = fm_gain[None, :], out_gain[None, :]
    places = {axis: lax.axis_index(axis).astype(jnp.int32)[None] for axis in EMB}

    def spread(value):
        others = [turn(value, "wide", wide, k) for k in range(1, wide)]
        return others[0] if len(others) == 1 else jnp.concatenate(others, axis=0)

    def give_back(value):
        blocks = value.reshape(wide - 1, -1, width)
        others = [turn(blocks[k - 1 : k], "wide", wide, wide - k) for k in range(1, wide)]
        return others[0] if len(others) == 1 else jnp.concatenate(others, axis=0)

    def exchange(value):
        flat = value.reshape(owners * value.shape[1], *value.shape[2:])
        moved = lax.all_to_all(flat, EMB, split_axis=0, concat_axis=0, tiled=True)
        return moved.reshape(value.shape)

    pooled = pool_bags(tables, bag_ids[0], bag_lengths[0], owners, halves)
    received = [exchange(pooled[0])]
    for h in range(1, halves):
        received.append(exchange(after(pooled[h], received[h - 1])))
    kept, rows, rows_other, embeds, partial = [], [], [], [], []
    ff, ff_other, grad_top, grads, grads_other = [], [], [], [], []
    layer_out, made_last = None, None

    def forward(h):
        nonlocal layer_out, made_last
        mine = embeds[h]
        layer_out, part = linear(
            after(mine, made_last), linear_w, gain_out, cot, layer_out, h * here, f"linear_{h}"
        )
        partial.append(part)

    def finish(h):
        nonlocal layer_out, made_last
        layer_out, kept_grad, grad = top(
            ff[h], ff_other[h], embeds[h], gain_out, cot, layer_out, h * here, made, f"top_{h}"
        )
        grad_top.append(kept_grad)
        grads.append(grad)
        grads_other.append(spread(grad))
        made_last = grad

    for h in range(halves):
        got = received[h] if made_last is None else after(received[h], made_last)
        x, crossed, mixing, inter, row = front(got, slot_field, proj_y, proj_p, gain_fm, f"front_{h}")
        embeds.append(x)
        kept.append((inter, crossed, mixing))
        rows.append(row)
        rows_other.append(spread(row))
        made_last = row
        if h:
            forward(h - 1)
            finish(h - 1)
        own, away = mlp_up(
            rows[h] if not h else after(rows[h], made_last), rows_other[h], w_up, w_down, f"up_{h}"
        )
        ff.append(own)
        ff_other.append(give_back(away))
        made_last = away
    forward(halves - 1)
    finish(halves - 1)

    units = w_up.shape[0] // owners
    shared = (mid * far, near, units, width)
    up_shared, down_shared = w_up.reshape(shared), w_down.reshape(shared)
    count = len(rows)
    row_kinds = [F32] * count + [BF] * count
    total, parts_down, parts_up = None, [], []
    for k in reversed(range(near)):
        grad_down, grad_up, *outs = mlp_back(
            lax.rem(places["core"] + k, near),
            [*rows, *rows_other],
            [*grads, *grads_other],
            up_shared,
            down_shared,
            total,
            BF if k else F32,
            None if k else row_kinds,
            f"back_{k}",
        )
        total = outs[0]
        parts_down.insert(0, turn(grad_down, "core", near, k) if k else grad_down)
        parts_up.insert(0, turn(grad_up, "core", near, k) if k else grad_up)
    norm_own, norm_other = outs[:count], [give_back(away) for away in outs[count:]]

    cut = lambda arrays, size: [a.reshape(-1, size, units, width) for a in arrays]
    pieces = split_sum(places["y"], mid, [cut(parts_down, mid), cut(parts_up, mid)], F32, "split_y")
    sums = [[p[0]] + [turn(p[k], "y", mid, k) for k in range(1, mid)] for p in pieces]
    slot_grads, last = None, pieces[0][0]
    for h in range(halves):
        slot_grads = tail(
            after(norm_own[h], last),
            norm_other[h],
            (*kept[h], grad_top[h], partial[h]),
            gain_fm,
            proj_y,
            proj_p,
            slot_field,
            slot_grads,
            h * here,
            (owners, samples, *pooled[0].shape[2:]),
            f"tail_{h}",
        )
    returned = exchange(slot_grads)
    weights = []
    last = slot_grads
    for n, name in enumerate(("down", "up")):
        sums[n][0] = after(sums[n][0], last)
        (pieces,) = split_sum(places["z"], far, [cut(sums[n], far)], F32, f"{name}_split_z")
        last = pieces[0]
        sums[n] = [pieces[0]] + [turn(pieces[k], "z", far, k) for k in range(1, far)]
    for n, name in enumerate(("down", "up")):
        sums[n][0] = after(sums[n][0], last)
        (pieces,) = split_sum(places["z"], 1, [cut(sums[n], 1)], BF, f"{name}_share")
        last = pieces[0]
        weights.append(last)
    for axis, size in (("z", far), ("y", mid), ("core", near)):
        for n, name in enumerate(("down", "up")):
            parts = [weights[n]] + [turn(weights[n], axis, size, k) for k in range(1, size)]
            parts[0] = after(parts[0], last)
            kind = F32 if axis == "core" else BF
            last = join(places[axis], parts, kind, f"{name}_join_{axis}")
            weights[n] = last.reshape(-1, units, width)
    down, up = [w.reshape(-1, width) for w in weights]
    return (layer_out[None], returned.reshape(1, owners * samples, -1, width), up, down)


def solution(mesh):
    emb, wide = mesh.shape["emb"], mesh.shape["wide"]
    near = 2 if emb % 2 == 0 else 1
    far = 4 if (emb // near) % 4 == 0 else 1
    split = Mesh(
        mesh.devices.reshape(far, emb // near // far, near, wide), ("z", "y", "core", "wide")
    )
    return jax.shard_map(
        functools.partial(body, dict(split.shape)),
        mesh=split,
        in_specs=(
            P(EMB, None, None),
            P("wide", None, EMB, None),
            P("wide", None, EMB),
            P(),
            P(),
            P(),
            P(),
            P(),
            P("wide", None),
            P("wide", None),
            P(),
            P("wide", EMB, None, None),
        ),
        out_specs=(
            P("wide", EMB, None, None),
            P("wide", None, EMB, None),
            P("wide", None),
            P("wide", None),
        ),
        check_vma=False,
    )
```

time: 583 us -> 239 us (0.41)
  waiting for transfers between devices: 369 us -> 67.5 us
  matrix products: 74.3 us -> 0 us
  Pallas kernels: 0 us -> 66.2 us
  local copies, waits for them, and re-layouts: 94.5 us -> 33.1 us
  starting transfers between devices: 13.3 us -> 48 us
  blocking collectives: 0 us -> 20.7 us
  other arithmetic: 14.7 us -> 1.05 us
  between operations: 14.2 us -> 0.99 us
    reduce_scatter x1 -> x0, waiting for transfers between devices: 188 us -> none  [body(): lax.psum_scatter(jnp.concatenate([up_term, down_term_part], axis=1), 'wid...]
    psum x1 -> x0, waiting for transfers between devices: 123 us -> none  [body(): grad_up, grad_down = lax.psum((up_local, down_local), 'emb')]
    dot_general x14 -> x0, matrix products: 74.3 us -> none  [the longest x1 13.6 us: body(): jnp.einsum('re,he->rh', grad_ff_rows, down_all, preferred_element_type=jn...]
    ppermute x0 -> x28, waiting for transfers between devices: none -> 67.5 us  [turn(): lax.ppermute(value, axis, [(i, (i + shift) % size) for i in range(size)])]
    pallas_call x0 -> x24, Pallas kernels: none -> 66.2 us  [the longest x2 19.8 us: mlp_back(): pl.pallas_call(functools.partial(back_kernel, blocks, bool(begun), last),...]
    all_to_all x2, waiting for transfers between devices: 57.6 us -> 0.01 us  [exchange(): moved = lax.all_to_all(flat, EMB, split_axis=0, concat_axis=0, tiled=True)]
    gather x3 -> x0, local copies, waits for them, and re-layouts: 45.6 us -> none  [the longest x2 42.5 us: pool_bags(): jnp.take(tables.reshape(slots_here * bucket_count, -1), flat_ids, axis=0)]
    ppermute x0 -> x28, starting transfers between devices: none -> 34.4 us  [turn(): lax.ppermute(value, axis, [(i, (i + shift) % size) for i in range(size)])]
  transfers between devices with their start and end apart: 6 -> 30, of which waited for: 4 -> 13; matrix products, arithmetic and copies ran while one was open for 20% -> 0% of each run, Pallas kernels for 0% -> 16%
where the time goes in v2:
time: 239 us; the launch traced here: 238 us
  waiting for transfers between devices  67.5 us (28%)
  Pallas kernels  66.2 us (28%)
  starting transfers between devices  48 us (20%)
  local copies, waits for them, and re-layouts  33.1 us (14%)
  blocking collectives  20.7 us (9%)
    ppermute x28, waiting for transfers between devices, turn(): lax.ppermute(value, axis, [(i, (i + shift) % size) for i in range(size)])  67.5 us
    ppermute x28, starting transfers between devices, turn(): lax.ppermute(value, axis, [(i, (i + shift) % size) for i in range(size)])  34.4 us
    unnamed x122, local copies, waits for them, and re-layouts  33 us
    all_to_all x1, blocking collectives, exchange(): moved = lax.all_to_all(flat, EMB, split_axis=0, concat_axis=0, tiled=True)  20.7 us
    pallas_call x2, Pallas kernels, mlp_back(): pl.pallas_call(functools.partial(back_kernel, blocks, bool(begun), last),...  19.8 us
    all_to_all x2, starting transfers between devices, exchange(): moved = lax.all_to_all(flat, EMB, split_axis=0, concat_axis=0, tiled=True)  13.6 us
    pallas_call x2, Pallas kernels, mlp_up(): pl.pallas_call(up_kernel, grid=(units // tile,), in_specs=[const(own, wid...  7.84 us
    pallas_call x1, Pallas kernels, pool_bags(): pl.pallas_call(pool_kernel, grid=(slots // step,), in_specs=[pl.BlockSpec...  6.84 us
  transfers between devices with their start and end apart: 30, of which 13 were waited for; matrix products, arithmetic and copies ran while one was open for 0% of the time, Pallas kernels for 16%

profile of v2, /device:TPU:9, one launch (start us, length us, event | category | flops | bytes accessed | tf_op | source)
XLA Modules:
  0.0 237.5 jit_solution(17104377477767452551)
XLA Ops:
  0.6 1.2 copy.21
  3.0 6.8 %pool.1 = (bf16[16,2,32,256]{3,2,1,0:T(8,128)(2,1)S(1)}, bf16[16,2,32,256]{3,2,1,0:T(8,128)(2,1)}) custom-call(s32[32,64,4]{2,1,0:T(8,128)S(1)} %fusion.ids_ref, bf16[32,512,256]{2,1,0:T(8,128)(2,1)} %tables_ref.1), custom_call_target="tpu_custom_call" | custom-call | tf_op jit(solution)/shard_map/pool/pallas_call | solution.py:80
  9.8 20.7 %all_to_all.15 = bf16[32,32,256]{2,1,0:T(8,128)(2,1)S(1)} all-to-all(bf16[32,32,256]{2,1,0:T(8,128)(2,1)S(1)} %bitcast.71), channel_id=1, replica_groups=mesh['z'=4,'y'=2,'core'=2,'wide'=2] {'z','y','core'}, dimensions={0} | all-to-all | bytes 1048576 | tf_op jit(solution)/shard_map/all_to_all | solution.py:545
  30.5 4.4 %all-to-all-start.1 = ((bf16[32,32,256]{2,1,0:T(8,128)(2,1)}), bf16[32,32,256]{2,1,0:T(8,128)(2,1)}, u32[]{:S(2)}, u32[]{:S(2)}) async-start(bf16[32,32,256]{2,1,0:T(8,128)(2,1)} %bitcast.5), calls=%async_computation.1 | async-start | bytes 1048576 | tf_op jit(solution)/shard_map/all_to_all | solution.py:545
  34.9 2.2 front_0.1
  41.2 3.6 %collective-permute-done.rows_other.refs_2_ = bf16[256,256]{1,0:T(8,128)(2,1)S(1)} collective-permute-done((bf16[256,256]{1,0:T(8,128)(2,1)S(1)}, bf16[256,256]{1,0:T(8,128)(2,1)S(1)}, u32[]{:S(2)}, u32[]{:S(2)}) %collective-permute-start) | collective-permute-done | bytes 131104 | tf_op jit(solution)/shard_map/ppermute | solution.py:500
  44.8 1.6 copy-done.1
  46.4 4.2 %up_0.1 = (f32[256,256]{1,0:T(8,128)S(1)}, bf16[256,256]{1,0:T(8,128)(2,1)}) custom-call(bf16[256,256]{1,0:T(8,128)(2,1)S(1)} %get-tuple-element.71.rows_own.refs_0_, bf16[256,256]{1,0:T(8,128)(2,1)S(1)} %collective-permute-done.rows_other.refs_2_, bf16[4096,256]{1,0:T(8,128)(2,1)S(1)} %copy-done, bf16[4096,256]{1,0:T(8,128)(2,1)S(1)} %copy-done.1), custom_call_target="tpu_custom_call" | custom-call | tf_op jit(solution)/shard_map/up_0/pallas_call | solution.py:235
  52.6 3.1 %front_1.1 = (bf16[2,512,256]{2,1,0:T(8,128)(2,1)S(1)}, bf16[2,256,256]{2,1,0:T(8,128)(2,1)S(1)}, bf16[2,128,256]{2,1,0:T(8,128)(2,1)S(1)}, f32[256,256]{1,0:T(8,128)S(1)}, bf16[256,256]{1,0:T(8,128)(2,1)S(1)}) custom-call(bf16[16,2,32,256]{3,2,1,0:T(8,128)(2,1)} %bitcast.6.rec, s32[1,512]{1,0:T(1,128)S(1)} %bitcast.81, bf16[512,256]{1,0:T(8,128)(2,1)S(1)} %copy-done.4, ...), custom_call_target="tpu_custom_call" | custom-call | tf_op jit(solution)/shard_map/front_1/pallas_call | solution.py:128
  60.1 2.3 linear_0.1
  63.3 2.1 top_0.1
  65.4 3.6 %up_1.1 = (f32[256,256]{1,0:T(8,128)S(1)}, bf16[256,256]{1,0:T(8,128)(2,1)S(1)}) custom-call(bf16[256,256]{1,0:T(8,128)(2,1)S(1)} %get-tuple-element.80.rows_own.refs_1_, bf16[256,256]{1,0:T(8,128)(2,1)S(1)} %collective-permute-done.2.rows_other.refs_3_, bf16[4096,256]{1,0:T(8,128)(2,1)S(1)} %copy-done, bf16[4096,256]{1,0:T(8,128)(2,1)S(1)} %copy-done.2), custom_call_target="tpu_custom_call" | custom-call | tf_op jit(solution)/shard_map/up_1/pallas_call | solution.py:235
  69.1 1.3 collective-permute-start.3
  70.6 2.3 linear_1.1
  76.2 2.6 %collective-permute-done.5.refs_7_ = bf16[256,256]{1,0:T(8,128)(2,1)S(1)} collective-permute-done((bf16[256,256]{1,0:T(8,128)(2,1)S(1)}, bf16[256,256]{1,0:T(8,128)(2,1)S(1)}, u32[]{:S(2)}, u32[]{:S(2)}) %collective-permute-start.5) | collective-permute-done | bytes 131104 | tf_op jit(solution)/shard_map/ppermute | solution.py:500
  78.9 9.6 %back_1.1 = (bf16[8,256,256]{2,1,0:T(8,128)(2,1)}, bf16[8,256,256]{2,1,0:T(8,128)(2,1)}, f32[256,1024]{1,0:T(8,128)S(1)}) custom-call(s32[1]{0:T(128)S(6)} %rem.37._, bf16[256,256]{1,0:T(8,128)(2,1)S(1)} %copy-done.12, bf16[256,256]{1,0:T(8,128)(2,1)S(1)} %copy-done.16, bf16[256,256]{1,0:T(8,128)(2,1)S(1)} %copy-done.14, bf16[256,256]{1,0:T(8,128)(2,1)S(1)} %copy-done.18, ...), custom_call_target="tpu_custom_call" | custom-call | tf_op jit(solution)/shard_map/back_1/pallas_call | solution.py:351
  89.4 3.7 %collective-permute-start.6 = (bf16[8,256,256]{2,1,0:T(8,128)(2,1)}, bf16[8,256,256]{2,1,0:T(8,128)(2,1)S(1)}, u32[]{:S(2)}, u32[]{:S(2)}) collective-permute-start(bf16[8,256,256]{2,1,0:T(8,128)(2,1)} %get-tuple-element.92), channel_id=1, source_target_pairs={{0,2},{2,0},{1,3},{3,1},{4,6},{6,4},{5,7},{7,5},{8,10},{10,8},{9,1... | collective-permute-start | bytes 3145736 | tf_op jit(solution)/shard_map/ppermute | solution.py:500
  93.2 1.2 copy-done.22
  96.2 10.2 %back_0.1 = (f32[8,256,256]{2,1,0:T(8,128)S(1)}, f32[8,256,256]{2,1,0:T(8,128)}, f32[256,256]{1,0:T(8,128)S(1)}, f32[256,256]{1,0:T(8,128)S(1)}, bf16[256,256]{1,0:T(8,128)(2,1)}, /*index=5*/bf16[256,256]{1,0:T(8,128)(2,1)}) custom-call(s32[1]{0:T(128)S(6)} %rem.31._, bf16[256,256]{1,0:T(8,128)(2,1)S(1)} %copy-done.12, bf16[256,256]{1,0:T(8,128)(2,1)S(1)} %copy-done.16, ...), custom_call_target="tpu_custom_call" | custom-call | tf_op jit(solution)/shard_map/back_0/pallas_call | solution.py:351
  106.4 1.3 copy-done.5
  107.7 4.0 %split_y.1 = (f32[4,256,256]{2,1,0:T(8,128)S(1)}, bf16[4,256,256]{2,1,0:T(8,128)(2,1)}, f32[4,256,256]{2,1,0:T(8,128)S(1)}, bf16[4,256,256]{2,1,0:T(8,128)(2,1)}) custom-call(s32[1]{0:T(128)} %bitcast.17.at, f32[4,2,256,256]{3,2,1,0:T(8,128)} %bitcast.62, bf16[4,2,256,256]{3,2,1,0:T(8,128)(2,1)S(1)} %bitcast.68, f32[4,2,256,256]{3,2,1,0:T(8,128)} %bitcast.95, ...), custom_call_target="tpu_custom_call" | custom-call | tf_op jit(solution)/shard_map/split_y/pallas_call | solution.py:388
  116.8 2.8 %collective-permute-done.9.norm_other = bf16[1,256,256]{2,1,0:T(8,128)(2,1)S(1)} collective-permute-done((bf16[1,256,256]{2,1,0:T(8,128)(2,1)}, bf16[1,256,256]{2,1,0:T(8,128)(2,1)S(1)}, u32[]{:S(2)}, u32[]{:S(2)}) %collective-permute-start.9) | collective-permute-done | bytes 131104 | tf_op jit(solution)/shard_map/ppermute | solution.py:500
  124.3 3.1 %tail_0.1.refs_0_ = bf16[16,4,32,256]{3,2,1,0:T(8,128)(2,1)} custom-call(f32[256,256]{1,0:T(8,128)S(1)} %copy-done.48, bf16[1,256,256]{2,1,0:T(8,128)(2,1)S(1)} %collective-permute-done.9.norm_other, f32[256,256]{1,0:T(8,128)S(1)} %copy-done.36, f32[1,256]{1,0:T(1,128)S(1)} %bitcast.89, bf16[2,256,256]{2,1,0:T(8,128)(2,1)S(1)} %copy-done.34, ...), custom_call_target="tpu_custom_call" | custom-call | tf_op jit(solution)/shard_map/tail_0/pallas_call | solution.py:450
  133.7 3.1 %tail_1.1 = bf16[16,4,32,256]{3,2,1,0:T(8,128)(2,1)} custom-call(f32[256,256]{1,0:T(8,128)S(1)} %copy-done.46, bf16[1,256,256]{2,1,0:T(8,128)(2,1)S(1)} %copy-done.56, f32[256,256]{1,0:T(8,128)S(1)} %copy-done.40, f32[1,256]{1,0:T(1,128)S(1)} %bitcast.90, bf16[2,256,256]{2,1,0:T(8,128)(2,1)S(1)} %copy-done.38, ...), custom_call_target="tpu_custom_call", output_to_operand_aliasing={{}: (11, {})} | custom-call | tf_op jit(solution)/shard_map/tail_1/pallas_call | solution.py:450
  138.0 1.2 collective-permute-start.12
  140.1 1.4 collective-permute-start.14
  141.5 9.2 %all-to-all-start.2 = ((bf16[64,32,256]{2,1,0:T(8,128)(2,1)}), bf16[64,32,256]{2,1,0:T(8,128)(2,1)}, u32[]{:S(2)}, u32[]{:S(2)}) async-start(bf16[64,32,256]{2,1,0:T(8,128)(2,1)} %bitcast.25), calls=%async_computation.2 | async-start | bytes 2097152 | tf_op jit(solution)/shard_map/all_to_all | solution.py:545
  151.9 1.3 collective-permute-start.15
  154.1 1.4 collective-permute-start.17
  155.7 3.2 %collective-permute-start.19 = (bf16[1,256,256]{2,1,0:T(8,128)(2,1)S(1)}, bf16[1,256,256]{2,1,0:T(8,128)(2,1)S(1)}, u32[]{:S(2)}, u32[]{:S(2)}) collective-permute-start(bf16[1,256,256]{2,1,0:T(8,128)(2,1)S(1)} %down_share.1.refs_0_), channel_id=1, source_target_pairs={{0,16},{8,24},{16,0},{24,8},{1,17},{9,25},{17,1},{25,9},{2,18},{10... | collective-permute-start | bytes 393224 | tf_op jit(solution)/shard_map/ppermute | solution.py:500
  158.9 28.7 %collective-permute-done.15 = bf16[1,256,256]{2,1,0:T(8,128)(2,1)S(1)} collective-permute-done((bf16[1,256,256]{2,1,0:T(8,128)(2,1)S(1)}, bf16[1,256,256]{2,1,0:T(8,128)(2,1)S(1)}, u32[]{:S(2)}, u32[]{:S(2)}) %collective-permute-start.15) | collective-permute-done | bytes 131104 | tf_op jit(solution)/shard_map/ppermute | solution.py:500
  187.6 2.8 %collective-permute-done.16 = bf16[1,256,256]{2,1,0:T(8,128)(2,1)S(1)} collective-permute-done((bf16[1,256,256]{2,1,0:T(8,128)(2,1)S(1)}, bf16[1,256,256]{2,1,0:T(8,128)(2,1)S(1)}, u32[]{:S(2)}, u32[]{:S(2)}) %collective-permute-start.16) | collective-permute-done | bytes 131104 | tf_op jit(solution)/shard_map/ppermute | solution.py:500
  190.4 1.9 collective-permute-done.17
  192.4 1.3 collective-permute-start.22
  193.7 1.4 collective-permute-start.23
  195.1 1.5 collective-permute-done.19.refs_2_
  196.5 7.0 %collective-permute-done.20.refs_3_ = bf16[1,256,256]{2,1,0:T(8,128)(2,1)S(1)} collective-permute-done((bf16[1,256,256]{2,1,0:T(8,128)(2,1)S(1)}, bf16[1,256,256]{2,1,0:T(8,128)(2,1)S(1)}, u32[]{:S(2)}, u32[]{:S(2)}) %collective-permute-start.20) | collective-permute-done | bytes 131104 | tf_op jit(solution)/shard_map/ppermute | solution.py:500
  203.5 1.3 collective-permute-start.24
  204.8 2.4 %collective-permute-done.22.refs_2_ = bf16[1,256,256]{2,1,0:T(8,128)(2,1)S(1)} collective-permute-done((bf16[1,256,256]{2,1,0:T(8,128)(2,1)S(1)}, bf16[1,256,256]{2,1,0:T(8,128)(2,1)S(1)}, u32[]{:S(2)}, u32[]{:S(2)}) %collective-permute-start.22) | collective-permute-done | bytes 131104 | tf_op jit(solution)/shard_map/ppermute | solution.py:500
  207.3 1.9 collective-permute-done.23.refs_3_
  209.2 1.3 collective-permute-start.25
  210.4 5.2 %collective-permute-done.24.refs_1_ = bf16[4,256,256]{2,1,0:T(8,128)(2,1)S(1)} collective-permute-done((bf16[4,256,256]{2,1,0:T(8,128)(2,1)S(1)}, bf16[4,256,256]{2,1,0:T(8,128)(2,1)S(1)}, u32[]{:S(2)}, u32[]{:S(2)}) %collective-permute-start.24) | collective-permute-done | bytes 524320 | tf_op jit(solution)/shard_map/ppermute | solution.py:500
  215.8 4.2 %collective-permute-start.26 = (bf16[8,256,256]{2,1,0:T(8,128)(2,1)S(1)}, bf16[8,256,256]{2,1,0:T(8,128)(2,1)S(1)}, u32[]{:S(2)}, u32[]{:S(2)}) collective-permute-start(bf16[8,256,256]{2,1,0:T(8,128)(2,1)S(1)} %bitcast.58), channel_id=1, source_target_pairs={{0,2},{2,0},{1,3},{3,1},{4,6},{6,4},{5,7},{7,5},{8,10},{10,8},{9,1... | collective-permute-start | bytes 3145736 | tf_op jit(solution)/shard_map/ppermute | solution.py:500
  220.0 7.0 %collective-permute-done.25.refs_1_ = bf16[4,256,256]{2,1,0:T(8,128)(2,1)S(1)} collective-permute-done((bf16[4,256,256]{2,1,0:T(8,128)(2,1)S(1)}, bf16[4,256,256]{2,1,0:T(8,128)(2,1)S(1)}, u32[]{:S(2)}, u32[]{:S(2)}) %collective-permute-start.25) | collective-permute-done | bytes 524320 | tf_op jit(solution)/shard_map/ppermute | solution.py:500
  227.0 2.3 collective-permute-start.27
  229.3 2.3 down_join_core.1
  231.7 3.5 %up_join_core.1 = f32[8,2,256,256]{3,2,1,0:T(8,128)} custom-call(s32[1]{0:T(128)} %bitcast.14.at, bf16[8,256,256]{2,1,0:T(8,128)(2,1)S(1)} %bitcast.61, bf16[8,256,256]{2,1,0:T(8,128)(2,1)} %collective-permute-done.27.refs_1_), custom_call_target="tpu_custom_call" | custom-call | tf_op jit(solution)/shard_map/up_join_core/pallas_call | solution.py:407
  235.3 2.3 copy.29
  (161 shorter events, 39.7 us)
Async XLA Ops:
  2.9 32.0 %copy-start.4 = (bf16[512,256]{1,0:T(8,128)(2,1)S(1)}, bf16[512,256]{1,0:T(8,128)(2,1)}, u32[]{:S(2)}) copy-start(bf16[512,256]{1,0:T(8,128)(2,1)} %proj_y.7) | copy-start | bytes 786436
  2.9 32.0 %copy-start.8 = (bf16[128,512]{1,0:T(8,128)(2,1)S(1)}, bf16[128,512]{1,0:T(8,128)(2,1)}, u32[]{:S(2)}) copy-start(bf16[128,512]{1,0:T(8,128)(2,1)} %proj_p.7) | copy-start | bytes 393220
  9.8 25.1 %copy-start.57 = (s32[512]{0:T(512)S(1)}, s32[512]{0:T(512)}, u32[]{:S(2)}) copy-start(s32[512]{0:T(512)} %param.15) | copy-start | bytes 6148
  9.8 25.1 %copy-start.59 = (f32[256]{0:T(256)S(1)}, f32[256]{0:T(256)}, u32[]{:S(2)}) copy-start(f32[256]{0:T(256)} %param.19) | copy-start | bytes 3076
  9.8 35.0 %copy-start = (bf16[4096,256]{1,0:T(8,128)(2,1)S(1)}, bf16[4096,256]{1,0:T(8,128)(2,1)}, u32[]{:S(2)}) copy-start(bf16[4096,256]{1,0:T(8,128)(2,1)} %w_up.3) | copy-start | bytes 6291460
  30.5 22.1 %all-to-all-start.1 = ((bf16[32,32,256]{2,1,0:T(8,128)(2,1)}), bf16[32,32,256]{2,1,0:T(8,128)(2,1)}, u32[]{:S(2)}, u32[]{:S(2)}) async-start(bf16[32,32,256]{2,1,0:T(8,128)(2,1)} %bitcast.5), calls=%async_computation.1 | async-start | bytes 1048576 | tf_op jit(solution)/shard_map/all_to_all | solution.py:545
  40.0 10.7 %copy-start.11 = (bf16[256,256]{1,0:T(8,128)(2,1)}, bf16[256,256]{1,0:T(8,128)(2,1)S(1)}, u32[]{:S(2)}) copy-start(bf16[256,256]{1,0:T(8,128)(2,1)S(1)} %get-tuple-element.71.rows_own.refs_0_) | copy-start | bytes 393220
  40.0 18.0 %copy-start.58 = (f32[256]{0:T(256)S(1)}, f32[256]{0:T(256)}, u32[]{:S(2)}) copy-start(f32[256]{0:T(256)} %param.22) | copy-start | bytes 3076
  40.0 4.8 %collective-permute-start = (bf16[256,256]{1,0:T(8,128)(2,1)S(1)}, bf16[256,256]{1,0:T(8,128)(2,1)S(1)}, u32[]{:S(2)}, u32[]{:S(2)}) collective-permute-start(bf16[256,256]{1,0:T(8,128)(2,1)S(1)} %get-tuple-element.71.rows_own.refs_0_), channel_id=1, source_target_pairs={{0,1},{1,0},{2,3},{3,2},{4,5},{5,4},{6,7},{7,6},{8,9},{9,8},{10,11... | collective-permute-start | bytes 393224 | tf_op jit(solution)/shard_map/ppermute | solution.py:500
  46.4 11.6 %copy-start.3 = (bf16[1,4,512,256]{3,2,1,0:T(8,128)(2,1)S(1)}, bf16[1,4,512,256]{3,2,1,0:T(8,128)(2,1)}, u32[]{:S(2)}) copy-start(bf16[1,4,512,256]{3,2,1,0:T(8,128)(2,1)} %param.23) | copy-start | bytes 3145732
  51.4 12.0 %collective-permute-start.1 = (bf16[1,256,256]{2,1,0:T(8,128)(2,1)}, bf16[1,256,256]{2,1,0:T(8,128)(2,1)}, u32[]{:S(2)}, u32[]{:S(2)}) collective-permute-start(bf16[1,256,256]{2,1,0:T(8,128)(2,1)} %bitcast.9), channel_id=1, source_target_pairs={{0,1},{1,0},{2,3},{3,2},{4,5},{5,4},{6,7},{7,6},{8,9},{9,8},{10,11... | collective-permute-start | bytes 393224 | tf_op jit(solution)/shard_map/ppermute | solution.py:500
  52.6 10.7 %copy-start.50 = (f32[256,256]{1,0:T(8,128)S(1)}, f32[256,256]{1,0:T(8,128)}, u32[]{:S(2)}) copy-start(f32[256,256]{1,0:T(8,128)} %copy-done.49) | copy-start | bytes 786436
  57.8 7.6 %copy-start.15 = (bf16[256,256]{1,0:T(8,128)(2,1)}, bf16[256,256]{1,0:T(8,128)(2,1)S(1)}, u32[]{:S(2)}) copy-start(bf16[256,256]{1,0:T(8,128)(2,1)S(1)} %get-tuple-element.80.rows_own.refs_1_) | copy-start | bytes 393220
  57.8 7.6 %collective-permute-start.2 = (bf16[256,256]{1,0:T(8,128)(2,1)S(1)}, bf16[256,256]{1,0:T(8,128)(2,1)S(1)}, u32[]{:S(2)}, u32[]{:S(2)}) collective-permute-start(bf16[256,256]{1,0:T(8,128)(2,1)S(1)} %get-tuple-element.80.rows_own.refs_1_), channel_id=1, source_target_pairs={{0,1},{1,0},{2,3},{3,2},{4,5},{5,4},{6,7},{7,6},{8,9},{9,8},{10,11... | collective-permute-start | bytes 393224 | tf_op jit(solution)/shard_map/ppermute | solution.py:500
  60.1 5.3 %copy-start.2 = (bf16[4096,256]{1,0:T(8,128)(2,1)S(1)}, bf16[4096,256]{1,0:T(8,128)(2,1)}, u32[]{:S(2)}) copy-start(bf16[4096,256]{1,0:T(8,128)(2,1)} %w_down.3) | copy-start | bytes 6291460
  65.4 5.2 %copy-start.10 = (bf16[384,512]{1,0:T(8,128)(2,1)S(1)}, bf16[384,512]{1,0:T(8,128)(2,1)}, u32[]{:S(2)}) copy-start(bf16[384,512]{1,0:T(8,128)(2,1)} %linear_w.3) | copy-start | bytes 1179652
  69.1 4.8 %collective-permute-start.3 = (bf16[1,256,256]{2,1,0:T(8,128)(2,1)S(1)}, bf16[1,256,256]{2,1,0:T(8,128)(2,1)S(1)}, u32[]{:S(2)}, u32[]{:S(2)}) collective-permute-start(bf16[1,256,256]{2,1,0:T(8,128)(2,1)S(1)} %bitcast.91), channel_id=1, source_target_pairs={{0,1},{1,0},{2,3},{3,2},{4,5},{5,4},{6,7},{7,6},{8,9},{9,8},{10,11... | collective-permute-start | bytes 393224 | tf_op jit(solution)/shard_map/ppermute | solution.py:500
  70.4 5.9 %collective-permute-start.4 = (bf16[256,256]{1,0:T(8,128)(2,1)}, bf16[256,256]{1,0:T(8,128)(2,1)S(1)}, u32[]{:S(2)}, u32[]{:S(2)}) collective-permute-start(bf16[256,256]{1,0:T(8,128)(2,1)} %get-tuple-element.79.refs_4_), channel_id=1, source_target_pairs={{0,1},{1,0},{2,3},{3,2},{4,5},{5,4},{6,7},{7,6},{8,9},{9,8},{10,11... | collective-permute-start | bytes 393224 | tf_op jit(solution)/shard_map/ppermute | solution.py:500
  75.0 13.4 %copy-start.31 = (bf16[256,256]{1,0:T(8,128)(2,1)}, bf16[256,256]{1,0:T(8,128)(2,1)S(1)}, u32[]{:S(2)}) copy-start(bf16[256,256]{1,0:T(8,128)(2,1)S(1)} %get-tuple-element.88.refs_5_) | copy-start | bytes 393220
  75.0 13.4 %copy-start.43 = (f32[256,256]{1,0:T(8,128)}, f32[256,256]{1,0:T(8,128)S(1)}, u32[]{:S(2)}) copy-start(f32[256,256]{1,0:T(8,128)S(1)} %get-tuple-element.101.grad_top) | copy-start | bytes 786436
  75.0 3.8 %collective-permute-start.5 = (bf16[256,256]{1,0:T(8,128)(2,1)S(1)}, bf16[256,256]{1,0:T(8,128)(2,1)S(1)}, u32[]{:S(2)}, u32[]{:S(2)}) collective-permute-start(bf16[256,256]{1,0:T(8,128)(2,1)S(1)} %get-tuple-element.88.refs_5_), channel_id=1, source_target_pairs={{0,1},{1,0},{2,3},{3,2},{4,5},{5,4},{6,7},{7,6},{8,9},{9,8},{10,11... | collective-permute-start | bytes 393224 | tf_op jit(solution)/shard_map/ppermute | solution.py:500
  76.2 12.2 %copy-start.29 = (bf16[256,256]{1,0:T(8,128)(2,1)}, bf16[256,256]{1,0:T(8,128)(2,1)S(1)}, u32[]{:S(2)}) copy-start(bf16[256,256]{1,0:T(8,128)(2,1)S(1)} %collective-permute-done.4.refs_6_) | copy-start | bytes 393220
  89.4 18.3 %collective-permute-start.6 = (bf16[8,256,256]{2,1,0:T(8,128)(2,1)}, bf16[8,256,256]{2,1,0:T(8,128)(2,1)S(1)}, u32[]{:S(2)}, u32[]{:S(2)}) collective-permute-start(bf16[8,256,256]{2,1,0:T(8,128)(2,1)} %get-tuple-element.92), channel_id=1, source_target_pairs={{0,2},{2,0},{1,3},{3,1},{4,6},{6,4},{5,7},{7,5},{8,10},{10,8},{9,1... | collective-permute-start | bytes 3145736 | tf_op jit(solution)/shard_map/ppermute | solution.py:500
  93.2 14.6 %collective-permute-start.7 = (bf16[8,256,256]{2,1,0:T(8,128)(2,1)}, bf16[8,256,256]{2,1,0:T(8,128)(2,1)}, u32[]{:S(2)}, u32[]{:S(2)}) collective-permute-start(bf16[8,256,256]{2,1,0:T(8,128)(2,1)} %get-tuple-element.94), channel_id=1, source_target_pairs={{0,2},{2,0},{1,3},{3,1},{4,6},{6,4},{5,7},{7,5},{8,10},{10,8},{9,1... | collective-permute-start | bytes 3145736 | tf_op jit(solution)/shard_map/ppermute | solution.py:500
  107.7 11.9 %copy-start.20 = (f32[2,512,256]{2,1,0:T(8,128)S(1)}, f32[2,512,256]{2,1,0:T(8,128)}, u32[]{:S(2)}) copy-start(f32[2,512,256]{2,1,0:T(8,128)} %copy-done.19) | copy-start | bytes 3145732
  113.7 23.1 %collective-permute-start.10 = (bf16[4,256,256]{2,1,0:T(8,128)(2,1)}, bf16[4,256,256]{2,1,0:T(8,128)(2,1)}, u32[]{:S(2)}, u32[]{:S(2)}) collective-permute-start(bf16[4,256,256]{2,1,0:T(8,128)(2,1)} %get-tuple-element.113), channel_id=1, source_target_pairs={{0,4},{4,0},{1,5},{5,1},{2,6},{6,2},{3,7},{7,3},{8,12},{12,8},{9,1... | collective-permute-start | bytes 1572872 | tf_op jit(solution)/shard_map/ppermute | solution.py:500
  114.9 35.8 %collective-permute-start.11 = (bf16[4,256,256]{2,1,0:T(8,128)(2,1)}, bf16[4,256,256]{2,1,0:T(8,128)(2,1)}, u32[]{:S(2)}, u32[]{:S(2)}) collective-permute-start(bf16[4,256,256]{2,1,0:T(8,128)(2,1)} %get-tuple-element.116), channel_id=1, source_target_pairs={{0,4},{4,0},{1,5},{5,1},{2,6},{6,2},{3,7},{7,3},{8,12},{12,8},{9,1... | collective-permute-start | bytes 1572872 | tf_op jit(solution)/shard_map/ppermute | solution.py:500
  115.2 4.4 %collective-permute-start.9 = (bf16[1,256,256]{2,1,0:T(8,128)(2,1)}, bf16[1,256,256]{2,1,0:T(8,128)(2,1)S(1)}, u32[]{:S(2)}, u32[]{:S(2)}) collective-permute-start(bf16[1,256,256]{2,1,0:T(8,128)(2,1)} %bitcast.24), channel_id=1, source_target_pairs={{0,1},{1,0},{2,3},{3,2},{4,5},{5,4},{6,7},{7,6},{8,9},{9,8},{10,11... | collective-permute-start | bytes 393224 | tf_op jit(solution)/shard_map/ppermute | solution.py:500
  116.4 11.0 %collective-permute-start.8 = (bf16[1,256,256]{2,1,0:T(8,128)(2,1)}, bf16[1,256,256]{2,1,0:T(8,128)(2,1)S(1)}, u32[]{:S(2)}, u32[]{:S(2)}) collective-permute-start(bf16[1,256,256]{2,1,0:T(8,128)(2,1)} %bitcast.22), channel_id=1, source_target_pairs={{0,1},{1,0},{2,3},{3,2},{4,5},{5,4},{6,7},{7,6},{8,9},{9,8},{10,11... | collective-permute-start | bytes 393224 | tf_op jit(solution)/shard_map/ppermute | solution.py:500
  116.8 11.3 %copy-start.28 = (f32[2,512,256]{2,1,0:T(8,128)S(1)}, f32[2,512,256]{2,1,0:T(8,128)}, u32[]{:S(2)}) copy-start(f32[2,512,256]{2,1,0:T(8,128)} %copy-done.27) | copy-start | bytes 3145732
  136.8 14.0 %copy-start.24 = (f32[4,256,256]{2,1,0:T(8,128)S(1)}, f32[4,256,256]{2,1,0:T(8,128)}, u32[]{:S(2)}) copy-start(f32[4,256,256]{2,1,0:T(8,128)} %copy-done.23) | copy-start | bytes 3145732
  138.0 16.2 %collective-permute-start.12 = (bf16[1,256,256]{2,1,0:T(8,128)(2,1)S(1)}, bf16[1,256,256]{2,1,0:T(8,128)(2,1)S(1)}, u32[]{:S(2)}, u32[]{:S(2)}) collective-permute-start(bf16[1,256,256]{2,1,0:T(8,128)(2,1)S(1)} %get-tuple-element.119), channel_id=1, source_target_pairs={{0,8},{8,16},{16,24},{24,0},{1,9},{9,17},{17,25},{25,1},{2,10},{10... | collective-permute-start | bytes 393224 | tf_op jit(solution)/shard_map/ppermute | solution.py:500
  139.2 16.3 %collective-permute-start.13 = (bf16[1,256,256]{2,1,0:T(8,128)(2,1)S(1)}, bf16[1,256,256]{2,1,0:T(8,128)(2,1)S(1)}, u32[]{:S(2)}, u32[]{:S(2)}) collective-permute-start(bf16[1,256,256]{2,1,0:T(8,128)(2,1)S(1)} %get-tuple-element.120), channel_id=1, source_target_pairs={{0,16},{8,24},{16,0},{24,8},{1,17},{9,25},{17,1},{25,9},{2,18},{10... | collective-permute-start | bytes 393224 | tf_op jit(solution)/shard_map/ppermute | solution.py:500
  140.1 15.4 %collective-permute-start.14 = (bf16[1,256,256]{2,1,0:T(8,128)(2,1)S(1)}, bf16[1,256,256]{2,1,0:T(8,128)(2,1)S(1)}, u32[]{:S(2)}, u32[]{:S(2)}) collective-permute-start(bf16[1,256,256]{2,1,0:T(8,128)(2,1)S(1)} %get-tuple-element.121), channel_id=1, source_target_pairs={{0,24},{8,0},{16,8},{24,16},{1,25},{9,1},{17,9},{25,17},{2,26},{10... | collective-permute-start | bytes 393224 | tf_op jit(solution)/shard_map/ppermute | solution.py:500
  141.5 87.8 %all-to-all-start.2 = ((bf16[64,32,256]{2,1,0:T(8,128)(2,1)}), bf16[64,32,256]{2,1,0:T(8,128)(2,1)}, u32[]{:S(2)}, u32[]{:S(2)}) async-start(bf16[64,32,256]{2,1,0:T(8,128)(2,1)} %bitcast.25), calls=%async_computation.2 | async-start | bytes 2097152 | tf_op jit(solution)/shard_map/all_to_all | solution.py:545
  151.9 35.7 %collective-permute-start.15 = (bf16[1,256,256]{2,1,0:T(8,128)(2,1)S(1)}, bf16[1,256,256]{2,1,0:T(8,128)(2,1)S(1)}, u32[]{:S(2)}, u32[]{:S(2)}) collective-permute-start(bf16[1,256,256]{2,1,0:T(8,128)(2,1)S(1)} %get-tuple-element.123), channel_id=1, source_target_pairs={{0,8},{8,16},{16,24},{24,0},{1,9},{9,17},{17,25},{25,1},{2,10},{10... | collective-permute-start | bytes 393224 | tf_op jit(solution)/shard_map/ppermute | solution.py:500
  153.1 37.2 %collective-permute-start.16 = (bf16[1,256,256]{2,1,0:T(8,128)(2,1)S(1)}, bf16[1,256,256]{2,1,0:T(8,128)(2,1)S(1)}, u32[]{:S(2)}, u32[]{:S(2)}) collective-permute-start(bf16[1,256,256]{2,1,0:T(8,128)(2,1)S(1)} %get-tuple-element.124), channel_id=1, source_target_pairs={{0,16},{8,24},{16,0},{24,8},{1,17},{9,25},{17,1},{25,9},{2,18},{10... | collective-permute-start | bytes 393224 | tf_op jit(solution)/shard_map/ppermute | solution.py:500
  154.1 38.1 %collective-permute-start.17 = (bf16[1,256,256]{2,1,0:T(8,128)(2,1)S(1)}, bf16[1,256,256]{2,1,0:T(8,128)(2,1)S(1)}, u32[]{:S(2)}, u32[]{:S(2)}) collective-permute-start(bf16[1,256,256]{2,1,0:T(8,128)(2,1)S(1)} %get-tuple-element.125), channel_id=1, source_target_pairs={{0,24},{8,0},{16,8},{24,16},{1,25},{9,1},{17,9},{25,17},{2,26},{10... | collective-permute-start | bytes 393224 | tf_op jit(solution)/shard_map/ppermute | solution.py:500
  155.6 38.1 %collective-permute-start.18 = (bf16[1,256,256]{2,1,0:T(8,128)(2,1)S(1)}, bf16[1,256,256]{2,1,0:T(8,128)(2,1)S(1)}, u32[]{:S(2)}, u32[]{:S(2)}) collective-permute-start(bf16[1,256,256]{2,1,0:T(8,128)(2,1)S(1)} %down_share.1.refs_0_), channel_id=1, source_target_pairs={{0,8},{8,16},{16,24},{24,0},{1,9},{9,17},{17,25},{25,1},{2,10},{10... | collective-permute-start | bytes 393224 | tf_op jit(solution)/shard_map/ppermute | solution.py:500
  155.7 40.8 %collective-permute-start.19 = (bf16[1,256,256]{2,1,0:T(8,128)(2,1)S(1)}, bf16[1,256,256]{2,1,0:T(8,128)(2,1)S(1)}, u32[]{:S(2)}, u32[]{:S(2)}) collective-permute-start(bf16[1,256,256]{2,1,0:T(8,128)(2,1)S(1)} %down_share.1.refs_0_), channel_id=1, source_target_pairs={{0,16},{8,24},{16,0},{24,8},{1,17},{9,25},{17,1},{25,9},{2,18},{10... | collective-permute-start | bytes 393224 | tf_op jit(solution)/shard_map/ppermute | solution.py:500
  187.6 15.9 %collective-permute-start.20 = (bf16[1,256,256]{2,1,0:T(8,128)(2,1)S(1)}, bf16[1,256,256]{2,1,0:T(8,128)(2,1)S(1)}, u32[]{:S(2)}, u32[]{:S(2)}) collective-permute-start(bf16[1,256,256]{2,1,0:T(8,128)(2,1)S(1)} %down_share.1.refs_0_), channel_id=1, source_target_pairs={{0,24},{8,0},{16,8},{24,16},{1,25},{9,1},{17,9},{25,17},{2,26},{10... | collective-permute-start | bytes 393224 | tf_op jit(solution)/shard_map/ppermute | solution.py:500
  192.3 12.5 %collective-permute-start.21 = (bf16[1,256,256]{2,1,0:T(8,128)(2,1)S(1)}, bf16[1,256,256]{2,1,0:T(8,128)(2,1)S(1)}, u32[]{:S(2)}, u32[]{:S(2)}) collective-permute-start(bf16[1,256,256]{2,1,0:T(8,128)(2,1)S(1)} %up_share.1.refs_0_), channel_id=1, source_target_pairs={{0,8},{8,16},{16,24},{24,0},{1,9},{9,17},{17,25},{25,1},{2,10},{10... | collective-permute-start | bytes 393224 | tf_op jit(solution)/shard_map/ppermute | solution.py:500
  192.4 14.9 %collective-permute-start.22 = (bf16[1,256,256]{2,1,0:T(8,128)(2,1)S(1)}, bf16[1,256,256]{2,1,0:T(8,128)(2,1)S(1)}, u32[]{:S(2)}, u32[]{:S(2)}) collective-permute-start(bf16[1,256,256]{2,1,0:T(8,128)(2,1)S(1)} %up_share.1.refs_0_), channel_id=1, source_target_pairs={{0,16},{8,24},{16,0},{24,8},{1,17},{9,25},{17,1},{25,9},{2,18},{10... | collective-permute-start | bytes 393224 | tf_op jit(solution)/shard_map/ppermute | solution.py:500
  193.7 15.4 %collective-permute-start.23 = (bf16[1,256,256]{2,1,0:T(8,128)(2,1)S(1)}, bf16[1,256,256]{2,1,0:T(8,128)(2,1)S(1)}, u32[]{:S(2)}, u32[]{:S(2)}) collective-permute-start(bf16[1,256,256]{2,1,0:T(8,128)(2,1)S(1)} %up_share.1.refs_0_), channel_id=1, source_target_pairs={{0,24},{8,0},{16,8},{24,16},{1,25},{9,1},{17,9},{25,17},{2,26},{10... | collective-permute-start | bytes 393224 | tf_op jit(solution)/shard_map/ppermute | solution.py:500
  203.5 12.1 %collective-permute-start.24 = (bf16[4,256,256]{2,1,0:T(8,128)(2,1)S(1)}, bf16[4,256,256]{2,1,0:T(8,128)(2,1)S(1)}, u32[]{:S(2)}, u32[]{:S(2)}) collective-permute-start(bf16[4,256,256]{2,1,0:T(8,128)(2,1)S(1)} %bitcast.63), channel_id=1, source_target_pairs={{0,4},{4,0},{1,5},{5,1},{2,6},{6,2},{3,7},{7,3},{8,12},{12,8},{9,1... | collective-permute-start | bytes 1572872 | tf_op jit(solution)/shard_map/ppermute | solution.py:500
  209.2 17.8 %collective-permute-start.25 = (bf16[4,256,256]{2,1,0:T(8,128)(2,1)S(1)}, bf16[4,256,256]{2,1,0:T(8,128)(2,1)S(1)}, u32[]{:S(2)}, u32[]{:S(2)}) collective-permute-start(bf16[4,256,256]{2,1,0:T(8,128)(2,1)S(1)} %bitcast.65), channel_id=1, source_target_pairs={{0,4},{4,0},{1,5},{5,1},{2,6},{6,2},{3,7},{7,3},{8,12},{12,8},{9,1... | collective-permute-start | bytes 1572872 | tf_op jit(solution)/shard_map/ppermute | solution.py:500
  215.8 13.6 %collective-permute-start.26 = (bf16[8,256,256]{2,1,0:T(8,128)(2,1)S(1)}, bf16[8,256,256]{2,1,0:T(8,128)(2,1)S(1)}, u32[]{:S(2)}, u32[]{:S(2)}) collective-permute-start(bf16[8,256,256]{2,1,0:T(8,128)(2,1)S(1)} %bitcast.58), channel_id=1, source_target_pairs={{0,2},{2,0},{1,3},{3,1},{4,6},{6,4},{5,7},{7,5},{8,10},{10,8},{9,1... | collective-permute-start | bytes 3145736 | tf_op jit(solution)/shard_map/ppermute | solution.py:500
  227.0 4.7 %collective-permute-start.27 = (bf16[8,256,256]{2,1,0:T(8,128)(2,1)S(1)}, bf16[8,256,256]{2,1,0:T(8,128)(2,1)}, u32[]{:S(2)}, u32[]{:S(2)}) collective-permute-start(bf16[8,256,256]{2,1,0:T(8,128)(2,1)S(1)} %bitcast.60), channel_id=1, source_target_pairs={{0,2},{2,0},{1,3},{3,1},{4,6},{6,4},{5,7},{7,5},{8,10},{10,8},{9,1... | collective-permute-start | bytes 3145736 | tf_op jit(solution)/shard_map/ppermute | solution.py:500
  (42 other events, 72.1 us)

commit v3 on v2

v3 whole, which is shorter than its diff:
```python
import functools

import jax
import jax.numpy as jnp
from jax import lax
from jax.experimental import pallas as pl
from jax.experimental.pallas import tpu as pltpu
from jax.sharding import Mesh
from jax.sharding import PartitionSpec as P

norm_eps = 1e-05
VMEM_BYTES = 24 * 1024 * 1024
BF = jnp.bfloat16
F32 = jnp.float32
LANES = 128
PART = 256


def params():
    return pltpu.CompilerParams(vmem_limit_bytes=VMEM_BYTES)


def ordered(kernel, ins, deps):
    return lambda *refs: kernel(*refs[:ins], *refs[ins + len(deps) :])


def unread(deps):
    return [pl.BlockSpec(memory_space=pl.ANY)] * len(deps)


def nn(left, right):
    return lax.dot_general(left, right, (((1,), (0,)), ((), ())), preferred_element_type=F32)


def nt(left, right):
    return lax.dot_general(left, right, (((1,), (1,)), ((), ())), preferred_element_type=F32)


def tn(left, right):
    return lax.dot_general(left, right, (((0,), (0,)), ((), ())), preferred_element_type=F32)


def layer_norm(values):
    centre = jnp.mean(values, axis=-1, keepdims=True)
    shifted = values - centre
    scale = lax.rsqrt(jnp.mean(shifted * shifted, axis=-1, keepdims=True) + norm_eps)
    return (shifted * scale, scale)


def norm_back(unit, scale, gain, upstream):
    scaled = upstream * gain
    return scale * (
        scaled
        - jnp.mean(scaled, axis=-1, keepdims=True)
        - unit * jnp.mean(scaled * unit, axis=-1, keepdims=True)
    )


def pool_kernel(ids_ref, tables_ref, *refs):
    outs, sums = refs[:-1], refs[-1]
    slots, samples, bag = ids_ref.shape
    buckets = tables_ref.shape[1]
    here = outs[0].shape[1]
    bucket = lax.broadcasted_iota(jnp.int32, (samples, buckets), 1)
    for s in range(slots):
        ids = ids_ref[s]
        count = jnp.zeros((samples, buckets), F32)
        for j in range(bag):
            count = count + jnp.where(ids[:, j : j + 1] == bucket, 1.0, 0.0)
        bags = nn(count.astype(BF), tables_ref[s])
        for c in range(sums.shape[0]):
            sums[c, pl.ds(s * samples, samples), :] = bags[:, c * LANES : (c + 1) * LANES]
    for b in range(samples):
        owner, local = divmod(b, here * len(outs))
        out = outs[local // here]
        for c in range(sums.shape[0]):
            bag_sums = sums.at[c][pl.ds(b, slots, stride=samples), :]
            out[owner, local % here, :, c * LANES : (c + 1) * LANES] = bag_sums.astype(BF)


def pool_bags(tables, ids, lengths, owners, halves):
    slots, buckets, width = tables.shape
    samples, _, bag = ids.shape
    here = samples // owners // halves
    live = jnp.arange(bag, dtype=jnp.int32)[None, None, :] < lengths[:, :, None]
    masked = jnp.where(live, ids, -1).transpose(1, 0, 2)
    step = 16 if slots % 16 == 0 else slots
    return pl.pallas_call(
        pool_kernel,
        grid=(slots // step,),
        in_specs=[
            pl.BlockSpec((step, samples, bag), lambda g: (g, 0, 0)),
            pl.BlockSpec((step, buckets, width), lambda g: (g, 0, 0)),
        ],
        out_specs=[pl.BlockSpec((owners, here, step, width), lambda g: (0, 0, g, 0))] * halves,
        out_shape=[jax.ShapeDtypeStruct((owners, here, slots, width), BF)] * halves,
        scratch_shapes=[pltpu.VMEM((width // LANES, step * samples, LANES), F32)],
        compiler_params=params(),
        name="pool",
    )(masked, tables)


def const(*shape):
    return pl.BlockSpec(shape, lambda *_: (0,) * len(shape))


def by_sample(*shape):
    return pl.BlockSpec(shape, lambda b: (b,) + (0,) * (len(shape) - 1))


def from_sample(start, *shape):
    return pl.BlockSpec(shape, lambda b: (start + b,) + (0,) * (len(shape) - 1))


def front_kernel(rec, slot_row, proj_y, proj_p, gain, *refs):
    embeds, crossed, mixing, inter, rows, place = refs[-6:]
    owners, _, slots, width = rec.shape
    fields = owners * slots

    @pl.when(pl.program_id(0) == 0)
    def _():
        field = lax.broadcasted_iota(jnp.int32, (fields, fields), 0)
        place[...] = jnp.where(field == slot_row[...], 1.0, 0.0).astype(BF)

    x = nn(place[...], rec[:, 0].reshape(fields, width)).astype(BF)
    embeds[0] = x
    c = tn(x, proj_y[...]).astype(BF)
    crossed[0] = c
    m = nn(proj_p[...], x).astype(BF)
    mixing[0] = m
    v = nn(m, c)
    inter[...] = v
    unit, _ = layer_norm(v)
    rows[...] = (unit * gain[...]).astype(BF)


def front(received, slot_field, proj_y, proj_p, gain, filled, samples, start, deps, name):
    owners, here, slots, width = received.shape
    fields, rank = proj_y.shape
    made = proj_p.shape[0]
    return pl.pallas_call(
        ordered(front_kernel, 5 + len(filled), deps),
        grid=(here,),
        in_specs=[
            pl.BlockSpec((owners, 1, slots, width), lambda b: (0, b, 0, 0)),
            const(1, fields),
            const(fields, rank),
            const(made, fields),
            const(1, rank),
        ]
        + unread(filled)
        + unread(deps),
        out_specs=[
            by_sample(1, fields, width),
            from_sample(start, 1, width, rank),
            from_sample(start, 1, made, width),
            from_sample(start, made, rank),
            by_sample(made, rank),
        ],
        out_shape=[
            jax.ShapeDtypeStruct((here, fields, width), BF),
            pltpu.HBM((samples, width, rank), BF),
            pltpu.HBM((samples, made, width), BF),
            pltpu.HBM((samples * made, rank), F32),
            jax.ShapeDtypeStruct((here * made, rank), BF),
        ],
        input_output_aliases={5: 1, 6: 2, 7: 3} if filled else {},
        scratch_shapes=[pltpu.VMEM((fields, fields), BF)],
        compiler_params=params(),
        name=name,
    )(received, slot_field[None, :], proj_y, proj_p, gain, *filled, *deps)


def linear_kernel(embeds, linear_w, gain, cot, before, layer_out, partial):
    made = linear_w.shape[0]
    first = embeds.shape[1] - made
    x = embeds[0]
    summed = nn(linear_w[...], x) + x[first:].astype(F32)
    unit, scale = layer_norm(summed)
    layer_out[0, :first] = before[0]
    layer_out[0, first:] = (unit * gain[...]).astype(BF)
    grad = norm_back(unit, scale, gain[...], cot[0, first:].astype(F32))
    back = tn(linear_w[...], grad.astype(BF))
    partial[0, :first] = back[:first]
    partial[0, first:] = back[first:] + grad


def linear(embeds, linear_w, gain, cot, top_out, deps):
    samples, fields, width = embeds.shape
    return pl.pallas_call(
        ordered(linear_kernel, 5, deps),
        grid=(samples,),
        in_specs=[
            by_sample(1, fields, width),
            const(*linear_w.shape),
            const(1, width),
            by_sample(1, fields, width),
            by_sample(1, top_out.shape[1], width),
        ]
        + unread(deps),
        out_specs=[by_sample(1, fields, width)] * 2,
        out_shape=[pltpu.HBM(cot.shape, BF), pltpu.HBM(cot.shape, F32)],
        compiler_params=params(),
        name="linear",
    )(embeds, linear_w, gain, cot, top_out, *deps)


def activate(gate):
    sig = 0.5 * jnp.tanh(0.5 * gate) + 0.5
    h = gate * sig
    return (h.astype(BF), sig + h * (1.0 - sig))


def tiles_of(weight, others, own, most):
    units, width = weight.shape
    tile = min(most, units)
    steps = units // tile
    specs = [
        pl.BlockSpec(
            (tile, width), lambda g, at, n=n: (jnp.clip(g - n * steps, 0, steps - 1), 0)
        )
        for n in range(own + len(others))
    ]
    return steps, specs


def tiles_at(steps, own, near, refs):
    step = pl.program_id(0)
    count = len(refs) // 2 - own
    up, down = (refs[0][...], refs[1][...]) if own else (None, None)
    for n in range(count):
        fetched, traded = refs[2 * own + n][...], refs[2 * own + count + n][...]
        far_up = jnp.where(near[0] == 0, fetched, traded)
        far_down = jnp.where(near[0] == 0, traded, fetched)
        here = step < (n + own) * steps
        up = far_up if up is None else jnp.where(here, up, far_up)
        down = far_down if down is None else jnp.where(here, down, far_down)
    return (up, down)


def accumulate(out, begun, term):
    @pl.when(pl.program_id(0) == 0)
    def _():
        out[...] = term if begun is None else begun[...] + term

    @pl.when(pl.program_id(0) > 0)
    def _():
        out[...] += term


def up_kernel(steps, own, begun, near, rows, *refs):
    up, down = tiles_at(steps, own, near, refs[begun:-1])
    term = None
    for at in range(0, up.shape[0], PART):
        hidden, _ = activate(nt(rows[...], up[at : at + PART]))
        more = nn(hidden, down[at : at + PART])
        term = more if term is None else term + more
    accumulate(refs[-1], refs[0] if begun else None, term)


def back_kernel(steps, own, begun, near, rows, grads, *refs):
    up, down = tiles_at(steps, own, near, refs[begun:-1])
    term = None
    for at in range(0, up.shape[0], PART):
        part = up[at : at + PART]
        _, slope = activate(nt(rows[...], part))
        more = nn((nt(grads[...], down[at : at + PART]) * slope).astype(BF), part)
        term = more if term is None else term + more
    accumulate(refs[-1], refs[0] if begun else None, term)


def mlp(kernel, near, blocks, w_up, w_down, fetched, traded, begun, deps, name, own=True):
    steps, specs = tiles_of(w_up, fetched, own, 1024)
    begun = [] if begun is None else [begun]
    weights = [w_up, w_down] if own else []
    ins = 1 + len(blocks) + len(begun) + len(weights) + 2 * len(fetched)
    return pl.pallas_call(
        ordered(functools.partial(kernel, steps, int(own), len(begun)), ins, deps),
        grid_spec=pltpu.PrefetchScalarGridSpec(
            num_scalar_prefetch=1,
            grid=(steps * len(specs),),
            in_specs=[const(*block.shape) for block in (*blocks, *begun)]
            + specs[:own] * 2
            + specs[own:] * 2
            + unread(deps),
            out_specs=const(*blocks[0].shape),
        ),
        out_shape=jax.ShapeDtypeStruct(blocks[0].shape, F32),
        compiler_params=params(),
        name=name,
    )(near, *blocks, *begun, *weights, *fetched, *traded, *deps)


def top_kernel(ff, embeds, gain, cot, layer_out, grad, grad_ff):
    summed = ff[...] + embeds[0].astype(F32)
    unit, scale = layer_norm(summed)
    layer_out[0] = (unit * gain[...]).astype(BF)
    g = norm_back(unit, scale, gain[...], cot[0].astype(F32))
    grad[...] = g
    grad_ff[...] = g.astype(BF)


def top(ff, embeds, gain, cot):
    samples, _, width = embeds.shape
    made = ff.shape[0] // samples
    return pl.pallas_call(
        top_kernel,
        grid=(samples,),
        in_specs=[
            by_sample(made, width),
            by_sample(1, made, width),
            const(1, width),
            by_sample(1, made, width),
        ],
        out_specs=[by_sample(1, made, width), by_sample(made, width), by_sample(made, width)],
        out_shape=[
            jax.ShapeDtypeStruct((samples, made, width), BF),
            jax.ShapeDtypeStruct(ff.shape, F32),
            jax.ShapeDtypeStruct(ff.shape, BF),
        ],
        compiler_params=params(),
        name="top",
    )(ff, embeds, gain, cot)


def fill(blocks, out):
    at = 0
    for block in blocks:
        out[at : at + block.shape[0]] = block[...]
        at += block.shape[0]


def weight_kernel(blocks, _, *refs):
    w_up, w_down, grad_down, grad_up, rows, grads = refs[2 * blocks :]

    @pl.when(pl.program_id(0) == 0)
    def _():
        fill(refs[:blocks], rows)
        fill(refs[blocks : 2 * blocks], grads)

    shares, units, width = grad_down.shape
    up = w_up[...].reshape(shares * units, width)
    down = w_down[...].reshape(shares * units, width)
    part = min(units * shares, PART)
    each = part // units
    for n in range(shares // each):
        at = slice(n * part, (n + 1) * part)
        hidden, slope = activate(nt(up[at], rows[...]))
        gate = (nt(down[at], grads[...]) * slope).astype(BF)
        for out, left, right in ((grad_down, hidden, grads), (grad_up, gate, rows)):
            grad = nn(left, right[...]).reshape(each, units, width)
            out[n * each : (n + 1) * each] = grad.astype(out.dtype)


def weight_grads(at, rows, grads, w_up, w_down, kind, deps, name):
    shares, _, units, width = w_up.shape
    blocks = len(rows)
    count = sum(block.shape[0] for block in rows)
    step = max(1, min(shares, 512 // units if count <= 1024 else 128 // units))
    shared = pl.BlockSpec((step, 1, units, width), lambda g, at: (g, at[0], 0, 0))
    given = pl.BlockSpec((step, units, width), lambda g, at: (g, 0, 0))
    return pl.pallas_call(
        ordered(functools.partial(weight_kernel, blocks), 1 + 2 * blocks + 2, deps),
        grid_spec=pltpu.PrefetchScalarGridSpec(
            num_scalar_prefetch=1,
            grid=(shares // step,),
            in_specs=[const(*block.shape) for block in (*rows, *grads)]
            + [shared, shared]
            + unread(deps),
            out_specs=[given, given],
            scratch_shapes=[pltpu.VMEM((count, width), BF)] * 2,
        ),
        out_shape=[jax.ShapeDtypeStruct((shares, units, width), kind)] * 2,
        compiler_params=params(),
        name=name,
    )(at, *rows, *grads, w_up, w_down, *deps)


def split_kernel(count, each, at, *refs):
    ins, outs = refs[: -count * len(each)], refs[-count * len(each) :]
    for k in reversed(range(count)):
        here = lax.rem(at[0] + k, count)
        first = 0
        for n, terms in enumerate(each):
            total = ins[first][:, here].astype(F32)
            for ref in ins[first + 1 : first + terms]:
                total = total + ref[:, here].astype(F32)
            out = outs[n * count + k]
            out[...] = total.astype(out.dtype)
            first += terms


def split_sum(at, count, sums, kind, deps, name):
    outs = []
    for arrays in sums:
        before, _, units, width = arrays[0].shape
        outs += [((before, units, width), kind if k == 0 else BF) for k in range(count)]
    each = [len(arrays) for arrays in sums]
    pieces = whole(
        ordered(functools.partial(split_kernel, count, each), 1 + sum(each), deps),
        outs,
        name,
        in_specs=[pl.BlockSpec(memory_space=pltpu.SMEM)]
        + [pl.BlockSpec(memory_space=pltpu.VMEM)] * sum(each)
        + unread(deps),
    )(at, *[array for arrays in sums for array in arrays], *deps)
    return [pieces[n * count : (n + 1) * count] for n in range(len(sums))]


def join_kernel(at, *refs):
    ins, out = refs[:-1], refs[-1]
    count = len(ins)
    for k, ref in enumerate(ins):
        out[:, lax.rem(at[0] + (count - k), count)] = ref[...].astype(out.dtype)


def join(at, arrays, kind, deps, name):
    before, units, width = arrays[0].shape
    (out,) = whole(
        ordered(join_kernel, 1 + len(arrays), deps),
        [((before, len(arrays), units, width), kind)],
        name,
        in_specs=[pl.BlockSpec(memory_space=pltpu.SMEM)]
        + [pl.BlockSpec(memory_space=pltpu.VMEM)] * len(arrays)
        + unread(deps),
    )(at, *arrays, *deps)
    return out


def join_last_kernel(_, piece, *refs):
    refs[-1][:, 0] = piece[...].astype(F32)


def join_last(at, piece, filled, name):
    before, units, width = piece.shape
    step = max(1, before // 4)
    return pl.pallas_call(
        join_last_kernel,
        grid_spec=pltpu.PrefetchScalarGridSpec(
            num_scalar_prefetch=1,
            grid=(before // step,),
            in_specs=[pl.BlockSpec((step, units, width), lambda g, at: (g, 0, 0))] + unread(filled),
            out_specs=pl.BlockSpec((step, 1, units, width), lambda g, at: (g, at[0], 0, 0)),
        ),
        out_shape=pltpu.HBM((before, 2, units, width), F32),
        input_output_aliases={2: 0} if filled else {},
        compiler_params=params(),
        name=name,
    )(at, piece, *filled)


def tail_kernel(
    upstream, inter, gain, crossed, mixing, grad_top, partial, proj_y, proj_p, slot_col, *refs
):
    out, place = refs[-2:]
    owners, _, slots, width = out.shape
    fields = owners * slots
    made = mixing.shape[1]

    @pl.when(pl.program_id(0) == 0)
    def _():
        field = lax.broadcasted_iota(jnp.int32, (fields, fields), 1)
        place[...] = jnp.where(field == slot_col[...], 1.0, 0.0).astype(BF)

    unit, scale = layer_norm(inter[...])
    grad_inter = norm_back(unit, scale, gain[...], upstream[...]).astype(BF)
    grad_mixing = nt(grad_inter, crossed[0]).astype(BF)
    grad_crossed = tn(mixing[0], grad_inter).astype(BF)
    grad = partial[0] + tn(proj_p[...], grad_mixing) + nt(proj_y[...], grad_crossed)
    head = (grad[:made] + grad_top[...]).astype(BF)
    grad = jnp.concatenate([head, grad[made:].astype(BF)], axis=0)
    out[:, 0] = nn(place[...], grad).astype(BF).reshape(owners, slots, width)


def tail(upstream, kept, gain, proj_y, proj_p, slot_field, owners, deps):
    inter, crossed, mixing, grad_top, partial = kept
    samples, fields, width = partial.shape
    rank = proj_y.shape[1]
    made = mixing.shape[1]
    slots = fields // owners
    return pl.pallas_call(
        ordered(tail_kernel, 10, deps),
        grid=(samples,),
        in_specs=[
            by_sample(made, rank),
            by_sample(made, rank),
            const(1, rank),
            by_sample(1, width, rank),
            by_sample(1, made, width),
            by_sample(made, width),
            by_sample(1, fields, width),
            const(fields, rank),
            const(made, fields),
            const(fields, 1),
        ]
        + unread(deps),
        out_specs=pl.BlockSpec((owners, 1, slots, width), lambda b: (0, b, 0, 0)),
        out_shape=jax.ShapeDtypeStruct((owners, samples, slots, width), BF),
        scratch_shapes=[pltpu.VMEM((fields, fields), BF)],
        compiler_params=params(),
        name="tail",
    )(
        upstream,
        inter,
        gain,
        crossed,
        mixing,
        grad_top,
        partial,
        proj_y,
        proj_p,
        slot_field[:, None],
        *deps,
    )


def whole(kernel, shapes, name, **options):
    return pl.pallas_call(
        kernel,
        out_shape=[jax.ShapeDtypeStruct(shape, kind) for shape, kind in shapes],
        compiler_params=params(),
        name=name,
        **options,
    )


def turn(value, axis, size, shift):
    return lax.ppermute(value, axis, [(i, (i + shift) % size) for i in range(size)])


def after(value, *others):
    return lax.optimization_barrier((value, *others))[0]


def body(
    sizes,
    tables,
    bag_ids,
    bag_lengths,
    slot_field,
    proj_y,
    proj_p,
    linear_w,
    fm_gain,
    w_up,
    w_down,
    out_gain,
    cotangent,
):
    wide = sizes["wide"]
    emb = tuple(axis for axis in sizes if axis != "wide")
    owners = 2 ** len(emb)
    width = tables.shape[2]
    made = proj_p.shape[0]
    cot = cotangent[0]
    samples = cot.shape[0]
    gain_fm, gain_out = fm_gain[None, :], out_gain[None, :]
    places = {axis: lax.axis_index(axis).astype(jnp.int32)[None] for axis in emb}

    *outer, mid, near = emb

    def spread(value):
        return [turn(value, "wide", wide, k) for k in range(1, wide)]

    def exchange(value):
        flat = value.reshape(owners * samples, *value.shape[2:])
        moved = lax.all_to_all(flat, emb, split_axis=0, concat_axis=0, tiled=True)
        return moved.reshape(value.shape)

    fetched = spread(lax.select(places[near][0] == 0, w_up, w_down))
    (pooled,) = pool_bags(tables, bag_ids[0], bag_lengths[0], owners, 1)
    received = exchange(pooled)
    embeds, crossed, mixing, inter, rows = front(
        received, slot_field, proj_y, proj_p, gain_fm, [], samples, 0, [], "front"
    )
    all_rows = [rows, *spread(rows)]
    ff = mlp(up_kernel, places[near], [rows], w_up, w_down, [], [], None, [], "up_own")
    fetched, _ = lax.optimization_barrier((fetched, rows))
    traded = [turn(weight, near, 2, 1) for weight in fetched]
    ff = mlp(up_kernel, places[near], [rows], w_up, w_down, fetched, traded, ff, [], "up_other", False)
    layer_out, grad_top, grads = top(ff, embeds, gain_out, cot)
    all_grads = [grads, *spread(grads)]
    layer_out, partial = linear(embeds, linear_w, gain_out, cot, layer_out, [grads])

    units = w_up.shape[0] // owners
    shared = (owners // 2, 2, units, width)
    shares = (w_up.reshape(shared), w_down.reshape(shared))
    away = weight_grads(1 - places[near], all_rows, all_grads, *shares, BF, [partial], "weights_1")
    arrived = [turn(part, near, 2, 1) for part in away]
    kept_parts = weight_grads(places[near], all_rows, all_grads, *shares, F32, [away[0]], "weights_0")
    last = [kept_parts[0]]
    sums = [list(terms) for terms in zip(kept_parts, arrived)]

    def cut(arrays, size):
        return [a.reshape(-1, size, units, width) for a in arrays]

    def halve(n, axis):
        nonlocal last
        name = f"{('down', 'up')[n]}_split_{axis}"
        ((keep, away),) = split_sum(places[axis], 2, [cut(sums[n], 2)], F32, last, name)
        last = [away]
        sums[n] = [keep, turn(away, axis, 2, 1)]

    halve(0, mid)
    halve(1, mid)
    upstream = mlp(back_kernel, places[near], [rows, grads], w_up, w_down, fetched, traded, None, last, "back")
    last = [upstream]
    halve(0, outer[-1])
    slot_grads = tail(
        upstream,
        (inter, crossed, mixing, grad_top, partial),
        gain_fm,
        proj_y,
        proj_p,
        slot_field,
        owners,
        last,
    )
    last = [slot_grads]
    halve(1, outer[-1])
    returned = exchange(slot_grads)
    for axis in reversed(outer[:-1]):
        halve(0, axis)
        halve(1, axis)
    weights, orders = [], []
    for n, name in enumerate(("down", "up")):
        ((share,),) = split_sum(places[near], 1, [cut(sums[n], 1)], BF, last, f"{name}_share")
        last = [share]
        weights.append(share.reshape(-1, width))
        orders.append((*outer, mid, near) if n == 0 else (*outer[:1], mid, *outer[1:], near))
    done = [[], []]
    for step in range(len(emb)):
        for n, name in enumerate(("down", "up")):
            axis = orders[n][step]
            at = emb.index(axis)
            before = 2 ** sum(emb.index(other) < at for other in done[n])
            value = weights[n].reshape(before, -1, width)
            other = turn(value, axis, 2, 1)
            if step == len(emb) - 1:
                joined = join_last(places[axis], value, [], f"{name}_keep_{axis}")
                joined = join_last(1 - places[axis], other, [joined], f"{name}_join_{axis}")
            else:
                joined = join(places[axis], [value, other], BF, last, f"{name}_join_{axis}")
                last = [joined]
            weights[n] = joined.reshape(-1, width)
            done[n].append(axis)
    down, up = [w.reshape(-1, width) for w in weights]
    return (layer_out[None], returned.reshape(1, owners * samples, -1, width), up, down)


def solution(mesh):
    emb, wide = mesh.shape["emb"], mesh.shape["wide"]
    names = tuple(f"emb_{k}" for k in range(emb.bit_length() - 1))
    split = Mesh(mesh.devices.reshape((2,) * len(names) + (wide,)), (*names, "wide"))
    return jax.shard_map(
        functools.partial(body, dict(split.shape)),
        mesh=split,
        in_specs=(
            P(names, None, None),
            P("wide", None, names, None),
            P("wide", None, names),
            P(),
            P(),
            P(),
            P(),
            P(),
            P("wide", None),
            P("wide", None),
            P(),
            P("wide", names, None, None),
        ),
        out_specs=(
            P("wide", names, None, None),
            P("wide", None, names, None),
            P("wide", None),
            P("wide", None),
        ),
        check_vma=False,
    )
```

time: 239 us -> 208 us (0.87)
  waiting for transfers between devices: 67.5 us -> 48.8 us
  starting transfers between devices: 48 us -> 29.9 us
  local copies, waits for them, and re-layouts: 33.1 us -> 15.6 us
  blocking collectives: 20.7 us -> 32.2 us
  Pallas kernels: 66.2 us -> 73.9 us
  other arithmetic: 1.05 us -> 3.49 us
    ppermute x28 -> x20, waiting for transfers between devices: 67.5 us -> 48.8 us  [turn(): lax.ppermute(value, axis, [(i, (i + shift) % size) for i in range(size)])]
    unnamed x122 -> x56, local copies, waits for them, and re-layouts: 33 us -> 15.4 us
    ppermute x28 -> x20, starting transfers between devices: 34.4 us -> 22.5 us  [turn(): lax.ppermute(value, axis, [(i, (i + shift) % size) for i in range(size)])]
    all_to_all x1, blocking collectives: 20.7 us -> 32.2 us  [exchange(): moved = lax.all_to_all(flat, emb, split_axis=0, concat_axis=0, tiled=True)]
    pallas_call x23 -> x27, Pallas kernels: 59.4 us -> 69.9 us  [the longest x3 22.7 us: mlp(): pl.pallas_call(ordered(functools.partial(kernel, steps, int(own), len(beg...]
    all_to_all x2 -> x1, starting transfers between devices: 13.6 us -> 7.34 us  [exchange(): moved = lax.all_to_all(flat, emb, split_axis=0, concat_axis=0, tiled=True)]
    select_n x0 -> x1, other arithmetic: none -> 3.15 us  [body(): fetched = spread(lax.select(places[near][0] == 0, w_up, w_down))]
    pallas_call x1, Pallas kernels: 6.84 us -> 3.94 us  [pool_bags(): pl.pallas_call(pool_kernel, grid=(slots // step,), in_specs=[pl.BlockSpec...]
  transfers between devices with their start and end apart: 30 -> 21, of which waited for: 13 -> 7; matrix products, arithmetic and copies ran while one was open for 0% -> 0% of each run, Pallas kernels for 16% -> 31%
where the time goes in v3:
time: 208 us; the launch traced here: 205 us
  Pallas kernels  73.9 us (36%)
  waiting for transfers between devices  48.8 us (23%)
  blocking collectives  32.2 us (15%)
  starting transfers between devices  29.9 us (14%)
  local copies, waits for them, and re-layouts  15.6 us (8%)
  other arithmetic  3.49 us (2%)
    ppermute x20, waiting for transfers between devices, turn(): lax.ppermute(value, axis, [(i, (i + shift) % size) for i in range(size)])  48.8 us
    all_to_all x1, blocking collectives, exchange(): moved = lax.all_to_all(flat, emb, split_axis=0, concat_axis=0, tiled=True)  32.2 us
    pallas_call x3, Pallas kernels, mlp(): pl.pallas_call(ordered(functools.partial(kernel, steps, int(own), len(beg...  22.7 us
    ppermute x20, starting transfers between devices, turn(): lax.ppermute(value, axis, [(i, (i + shift) % size) for i in range(size)])  22.5 us
    unnamed x56, local copies, waits for them, and re-layouts  15.4 us
    pallas_call x2, Pallas kernels, weight_grads(): pl.pallas_call(ordered(functools.partial(weight_kernel, blocks), 1 + 2 *...  14.9 us
    pallas_call x4, Pallas kernels, join_last(): pl.pallas_call(join_last_kernel, grid_spec=pltpu.PrefetchScalarGridSpec(n...  9.07 us
    all_to_all x1, starting transfers between devices, exchange(): moved = lax.all_to_all(flat, emb, split_axis=0, concat_axis=0, tiled=True)  7.34 us
  transfers between devices with their start and end apart: 21, of which 7 were waited for; matrix products, arithmetic and copies ran while one was open for 0% of the time, Pallas kernels for 31%

profile of v3, /device:TPU:9, one launch (start us, length us, event | category | flops | bytes accessed | tf_op | source)
XLA Modules:
  0.0 204.8 jit_solution(10910096083408730175)
XLA Ops:
  0.7 3.2 %broadcast_select_fusion = bf16[4096,256]{1,0:T(8,128)(2,1)} fusion(bf16[4096,256]{1,0:T(8,128)(2,1)} %refs_3_.5, bf16[4096,256]{1,0:T(8,128)(2,1)} %refs_4_.1, pred[]{:T(512)S(6)} %eq.3), kind=kLoop, calls=%fused_computation | loop fusion | flops 1048576 | bytes 6291457 | tf_op jit(solution)/shard_map/select_n | solution.py:570
  3.8 1.2 collective-permute-start
  5.8 3.4 %copy-done.4 = bf16[32,512,256]{2,1,0:T(8,128)(2,1)S(1)} copy-done((bf16[32,512,256]{2,1,0:T(8,128)(2,1)S(1)}, bf16[32,512,256]{2,1,0:T(8,128)(2,1)}, u32[]{:S(2)}) %copy-start.4) | copy-done | bytes 8388632
  9.2 3.9 %pool.1 = bf16[16,4,32,256]{3,2,1,0:T(8,128)(2,1)S(1)} custom-call(s32[32,64,4]{2,1,0:T(8,128)S(1)} %fusion.ids_ref, bf16[32,512,256]{2,1,0:T(8,128)(2,1)S(1)} %copy-done.4), custom_call_target="tpu_custom_call" | custom-call | tf_op jit(solution)/shard_map/pool/pallas_call | solution.py:88
  13.1 32.2 %all_to_all.10 = bf16[64,32,256]{2,1,0:T(8,128)(2,1)S(1)} all-to-all(bf16[64,32,256]{2,1,0:T(8,128)(2,1)S(1)} %bitcast.60), channel_id=1, replica_groups=mesh['emb_0'=2,'emb_1'=2,'emb_2'=2,'emb_3'=2,'wide'=2] {'emb_0','emb_1',..., dimensions={0} | all-to-all | bytes 2097152 | tf_op jit(solution)/shard_map/all_to_all | solution.py:567
  45.4 4.8 %front.1 = (bf16[4,512,256]{2,1,0:T(8,128)(2,1)S(1)}, bf16[4,256,256]{2,1,0:T(8,128)(2,1)}, bf16[4,128,256]{2,1,0:T(8,128)(2,1)}, f32[512,256]{1,0:T(8,128)}, bf16[512,256]{1,0:T(8,128)(2,1)S(1)}) custom-call(bf16[16,4,32,256]{3,2,1,0:T(8,128)(2,1)S(1)} %bitcast.61, s32[1,512]{1,0:T(1,128)S(1)} %bitcast.79, bf16[512,256]{1,0:T(8,128)(2,1)S(1)} %copy-done.14, ...), custom_call_target="tpu_custom_call" | custom-call | tf_op jit(solution)/shard_map/front/pallas_call | solution.py:141
  50.6 1.6 collective-permute-start.1
  52.2 1.2 collective-permute-start.2
  53.4 4.2 %up_own.1.refs_2_ = f32[512,256]{1,0:T(8,128)S(1)} custom-call(s32[1]{0:T(128)} %bitcast.9.refs_0_._, bf16[512,256]{1,0:T(8,128)(2,1)S(1)} %get-tuple-element.32.refs_1_, bf16[4096,256]{1,0:T(8,128)(2,1)S(1)} %copy-done, bf16[4096,256]{1,0:T(8,128)(2,1)S(1)} %copy-done.1), custom_call_target="tpu_custom_call" | custom-call | tf_op jit(solution)/shard_map/up_own/pallas_call | solution.py:277
  57.6 5.9 %up_other.1.ff = f32[512,256]{1,0:T(8,128)S(1)} custom-call(s32[1]{0:T(128)} %bitcast.9.refs_0_._, bf16[512,256]{1,0:T(8,128)(2,1)S(1)} %get-tuple-element.32.refs_1_, f32[512,256]{1,0:T(8,128)S(1)} %up_own.1.refs_2_, bf16[4096,256]{1,0:T(8,128)(2,1)} %collective-permute-done.refs_3_.refs_5_, bf16[4096,256]{1,0:T(8,128)(2,1)S(1)} %collective-permute-done.1.refs_4_.refs_6_), custom_call_target="tpu_custom_call" | custom-call | tf_op jit(solution)/shard_map/up_other/pallas_call | solution.py:277
  63.6 1.1 top.1
  64.8 0.8 copy-done.18
  65.8 4.7 %linear.1 = (bf16[4,512,256]{2,1,0:T(8,128)(2,1)}, f32[4,512,256]{2,1,0:T(8,128)}) custom-call(bf16[4,512,256]{2,1,0:T(8,128)(2,1)S(1)} %get-tuple-element.31.embeds.refs_0_, bf16[384,512]{1,0:T(8,128)(2,1)S(1)} %copy-done.20, f32[1,256]{1,0:T(1,128)S(1)} %bitcast.82, bf16[4,512,256]{2,1,0:T(8,128)(2,1)S(1)} %bitcast.59, ...), custom_call_target="tpu_custom_call" | custom-call | tf_op jit(solution)/shard_map/linear/pallas_call | solution.py:190
  70.5 2.7 %collective-permute-done.3.refs_4_ = bf16[512,256]{1,0:T(8,128)(2,1)S(1)} collective-permute-done((bf16[512,256]{1,0:T(8,128)(2,1)S(1)}, bf16[512,256]{1,0:T(8,128)(2,1)S(1)}, u32[]{:S(2)}, u32[]{:S(2)}) %collective-permute-start.3) | collective-permute-done | bytes 262176 | tf_op jit(solution)/shard_map/ppermute | solution.py:528
  73.2 1.6 copy-done.7
  74.8 7.9 %weights_1.1 = (bf16[8,256,256]{2,1,0:T(8,128)(2,1)}, bf16[8,256,256]{2,1,0:T(8,128)(2,1)}) custom-call(s32[1]{0:T(128)S(6)} %sub.2.refs_0_._, bf16[512,256]{1,0:T(8,128)(2,1)S(1)} %get-tuple-element.32.refs_1_, bf16[512,256]{1,0:T(8,128)(2,1)S(1)} %collective-permute-done.2.refs_2_, bf16[512,256]{1,0:T(8,128)(2,1)S(1)} %get-tuple-element.35.refs_5_.refs_3_.refs_2_, ...), custom_call_target="tpu_custom_call" | custom-call | tf_op jit(solution)/shard_map/weights_1/pallas_call | solution.py:362
  82.6 1.1 collective-permute-start.5
  83.8 1.6 copy-done.2
  85.4 7.1 %weights_0.1 = (f32[8,256,256]{2,1,0:T(8,128)S(1)}, f32[8,256,256]{2,1,0:T(8,128)S(1)}) custom-call(s32[1]{0:T(128)} %bitcast.9.refs_0_._, bf16[512,256]{1,0:T(8,128)(2,1)S(1)} %get-tuple-element.32.refs_1_, bf16[512,256]{1,0:T(8,128)(2,1)S(1)} %collective-permute-done.2.refs_2_, bf16[512,256]{1,0:T(8,128)(2,1)S(1)} %get-tuple-element.35.refs_5_.refs_3_.refs_2_, ...), custom_call_target="tpu_custom_call" | custom-call | tf_op jit(solution)/shard_map/weights_0/pallas_call | solution.py:362
  92.4 2.2 %down_split_emb_2.1 = (f32[4,256,256]{2,1,0:T(8,128)S(1)}, bf16[4,256,256]{2,1,0:T(8,128)(2,1)}) custom-call(s32[1]{0:T(128)} %bitcast.11.refs_0_, f32[4,2,256,256]{3,2,1,0:T(8,128)S(1)} %bitcast.53, bf16[4,2,256,256]{3,2,1,0:T(8,128)(2,1)} %bitcast.17.refs_2_, f32[8,256,256]{2,1,0:T(8,128)S(1)} %get-tuple-element.41.refs_3_), custom_call_target="tpu_custom_call" | custom-call | tf_op jit(solution)/shard_map/down_split_emb_2/pallas_call | solution.py:399
  94.6 1.0 copy-done.10
  95.6 1.2 collective-permute-start.6
  96.8 2.2 %up_split_emb_2.1 = (f32[4,256,256]{2,1,0:T(8,128)S(1)}, bf16[4,256,256]{2,1,0:T(8,128)(2,1)}) custom-call(s32[1]{0:T(128)} %bitcast.11.refs_0_, f32[4,2,256,256]{3,2,1,0:T(8,128)S(1)} %bitcast.68, bf16[4,2,256,256]{3,2,1,0:T(8,128)(2,1)} %bitcast.15.refs_2_, bf16[4,256,256]{2,1,0:T(8,128)(2,1)} %get-tuple-element.42.refs_3_), custom_call_target="tpu_custom_call" | custom-call | tf_op jit(solution)/shard_map/up_split_emb_2/pallas_call | solution.py:399
  99.1 1.0 copy-done.12
  100.5 1.6 copy-done.3
  102.0 1.6 copy-done.6
  103.7 12.6 %back.1.refs_3_.refs_0_ = f32[512,256]{1,0:T(8,128)S(1)} custom-call(s32[1]{0:T(128)} %bitcast.9.refs_0_._, bf16[512,256]{1,0:T(8,128)(2,1)S(1)} %get-tuple-element.32.refs_1_, bf16[512,256]{1,0:T(8,128)(2,1)S(1)} %get-tuple-element.35.refs_5_.refs_3_.refs_2_, bf16[4096,256]{1,0:T(8,128)(2,1)S(1)} %copy-done, bf16[4096,256]{1,0:T(8,128)(2,1)S(1)} %copy-done.3, ...), custom_call_target="tpu_custom_call" | custom-call | tf_op jit(solution)/shard_map/back/pallas_call | solution.py:277
  116.3 1.3 down_split_emb_1.1
  118.0 5.4 %tail.1.refs_3_ = bf16[16,4,32,256]{3,2,1,0:T(8,128)(2,1)} custom-call(f32[512,256]{1,0:T(8,128)S(1)} %back.1.refs_3_.refs_0_, f32[512,256]{1,0:T(8,128)S(1)} %copy-done.17, f32[1,256]{1,0:T(1,128)S(1)} %bitcast.84, bf16[4,256,256]{2,1,0:T(8,128)(2,1)S(1)} %copy-done.16, bf16[4,128,256]{2,1,0:T(8,128)(2,1)S(1)} %copy-done.21, f32[512,256]{1,0:T(8,128)S(1)} %copy-done.19, ...), custom_call_target="tpu_custom_call" | custom-call | tf_op jit(solution)/shard_map/tail/pallas_call | solution.py:481
  123.4 1.1 up_split_emb_1.1
  124.5 1.2 collective-permute-start.8
  125.8 2.4 %collective-permute-start.11 = (bf16[1,256,256]{2,1,0:T(8,128)(2,1)S(1)}, bf16[1,256,256]{2,1,0:T(8,128)(2,1)S(1)}, u32[]{:S(2)}, u32[]{:S(2)}) collective-permute-start(bf16[1,256,256]{2,1,0:T(8,128)(2,1)S(1)} %get-tuple-element.54.refs_3_), channel_id=1, source_target_pairs={{0,16},{16,0},{1,17},{17,1},{2,18},{18,2},{3,19},{19,3},{4,20},{20... | collective-permute-start | bytes 393224 | tf_op jit(solution)/shard_map/ppermute | solution.py:528
  128.2 5.0 %collective-permute-done.8 = bf16[2,256,256]{2,1,0:T(8,128)(2,1)S(1)} collective-permute-done((bf16[2,256,256]{2,1,0:T(8,128)(2,1)S(1)}, bf16[2,256,256]{2,1,0:T(8,128)(2,1)S(1)}, u32[]{:S(2)}, u32[]{:S(2)}) %collective-permute-start.8) | collective-permute-done | bytes 262176 | tf_op jit(solution)/shard_map/ppermute | solution.py:528
  133.3 2.7 %collective-permute-start.10 = (bf16[1,256,256]{2,1,0:T(8,128)(2,1)S(1)}, bf16[1,256,256]{2,1,0:T(8,128)(2,1)S(1)}, u32[]{:S(2)}, u32[]{:S(2)}) collective-permute-start(bf16[1,256,256]{2,1,0:T(8,128)(2,1)S(1)} %get-tuple-element.56.refs_3_), channel_id=1, source_target_pairs={{0,16},{16,0},{1,17},{17,1},{2,18},{18,2},{3,19},{19,3},{4,20},{20... | collective-permute-start | bytes 393224 | tf_op jit(solution)/shard_map/ppermute | solution.py:528
  136.1 6.7 %collective-permute-done.10 = bf16[1,256,256]{2,1,0:T(8,128)(2,1)S(1)} collective-permute-done((bf16[1,256,256]{2,1,0:T(8,128)(2,1)S(1)}, bf16[1,256,256]{2,1,0:T(8,128)(2,1)S(1)}, u32[]{:S(2)}, u32[]{:S(2)}) %collective-permute-start.10) | collective-permute-done | bytes 131104 | tf_op jit(solution)/shard_map/ppermute | solution.py:528
  142.8 3.4 %collective-permute-start.12 = (bf16[1,256,256]{2,1,0:T(8,128)(2,1)S(1)}, bf16[1,256,256]{2,1,0:T(8,128)(2,1)S(1)}, u32[]{:S(2)}, u32[]{:S(2)}) collective-permute-start(bf16[1,256,256]{2,1,0:T(8,128)(2,1)S(1)} %up_share.1.refs_3_.refs_1_), channel_id=1, source_target_pairs={{0,16},{16,0},{1,17},{17,1},{2,18},{18,2},{3,19},{19,3},{4,20},{20... | collective-permute-start | bytes 393224 | tf_op jit(solution)/shard_map/ppermute | solution.py:528
  146.2 7.3 %all-to-all-start.1 = ((bf16[64,32,256]{2,1,0:T(8,128)(2,1)}), bf16[64,32,256]{2,1,0:T(8,128)(2,1)}, u32[]{:S(2)}, u32[]{:S(2)}) async-start(bf16[64,32,256]{2,1,0:T(8,128)(2,1)} %bitcast.22), calls=%async_computation.1 | async-start | bytes 2097152 | tf_op jit(solution)/shard_map/all_to_all | solution.py:567
  153.7 1.5 collective-permute-start.14
  155.2 22.6 %collective-permute-done.15.refs_2_ = bf16[2,256,256]{2,1,0:T(8,128)(2,1)S(1)} collective-permute-done((bf16[2,256,256]{2,1,0:T(8,128)(2,1)S(1)}, bf16[2,256,256]{2,1,0:T(8,128)(2,1)S(1)}, u32[]{:S(2)}, u32[]{:S(2)}) %collective-permute-start.15) | collective-permute-done | bytes 262176 | tf_op jit(solution)/shard_map/ppermute | solution.py:528
  177.8 0.9 collective-permute-start.17
  178.8 1.1 collective-permute-start.16
  179.9 11.0 %collective-permute-done.17.refs_2_ = bf16[4,256,256]{2,1,0:T(8,128)(2,1)S(1)} collective-permute-done((bf16[4,256,256]{2,1,0:T(8,128)(2,1)S(1)}, bf16[4,256,256]{2,1,0:T(8,128)(2,1)S(1)}, u32[]{:S(2)}, u32[]{:S(2)}) %collective-permute-start.17) | collective-permute-done | bytes 524320 | tf_op jit(solution)/shard_map/ppermute | solution.py:528
  191.3 2.0 collective-permute-start.18
  193.4 1.8 up_keep_emb_3.1.refs_0_
  195.2 1.8 down_keep_emb_3.1.refs_0_
  197.1 3.6 %up_join_emb_3.1 = f32[8,2,256,256]{3,2,1,0:T(8,128)} custom-call(s32[1]{0:T(128)S(6)} %sub.2.refs_0_._, bf16[8,256,256]{2,1,0:T(8,128)(2,1)} %collective-permute-done.18.piece, f32[8,2,256,256]{3,2,1,0:T(8,128)} %up_keep_emb_3.1.refs_0_), custom_call_target="tpu_custom_call", output_to_operand_aliasing={{}: (2, {})} | custom-call | tf_op jit(solution)/shard_map/up_join_emb_3/pallas_call | solution.py:437
  200.7 1.8 down_join_emb_3.1
  202.5 2.3 %copy.24 = bf16[1,64,32,256]{3,2,1,0:T(8,128)(2,1)} copy(bf16[1,64,32,256]{3,2,1,0:T(8,128)(2,1)} %bitcast.23) | data formatting | bytes 2097152
  (82 shorter events, 3.3 us)
Async XLA Ops:
  0.6 4.4 %copy-start.25 = (s32[1,64,32,4]{1,3,2,0:T(4,128)S(1)}, s32[1,64,32,4]{1,3,2,0:T(4,128)}, u32[]{:S(2)}) copy-start(s32[1,64,32,4]{1,3,2,0:T(4,128)} %param.13) | copy-start | bytes 98308
  0.6 4.8 %copy-start.26 = (s32[1,64,32]{1,2,0:T(8,128)S(1)}, s32[1,64,32]{1,2,0:T(8,128)}, u32[]{:S(2)}) copy-start(s32[1,64,32]{1,2,0:T(8,128)} %param.14) | copy-start | bytes 24580
  3.8 46.8 %collective-permute-start = (bf16[4096,256]{1,0:T(8,128)(2,1)}, bf16[4096,256]{1,0:T(8,128)(2,1)}, u32[]{:S(2)}, u32[]{:S(2)}) collective-permute-start(bf16[4096,256]{1,0:T(8,128)(2,1)} %broadcast_select_fusion), channel_id=1, source_target_pairs={{0,1},{1,0},{2,3},{3,2},{4,5},{5,4},{6,7},{7,6},{8,9},{9,8},{10,11... | collective-permute-start | bytes 6291464 | tf_op jit(solution)/shard_map/ppermute | solution.py:528
  5.8 3.4 %copy-start.4 = (bf16[32,512,256]{2,1,0:T(8,128)(2,1)S(1)}, bf16[32,512,256]{2,1,0:T(8,128)(2,1)}, u32[]{:S(2)}) copy-start(bf16[32,512,256]{2,1,0:T(8,128)(2,1)} %tables_ref.1) | copy-start | bytes 25165828
  9.2 36.2 %copy-start.14 = (bf16[512,256]{1,0:T(8,128)(2,1)S(1)}, bf16[512,256]{1,0:T(8,128)(2,1)}, u32[]{:S(2)}) copy-start(bf16[512,256]{1,0:T(8,128)(2,1)} %refs_7_.1) | copy-start | bytes 786436
  9.2 36.2 %copy-start.15 = (bf16[128,512]{1,0:T(8,128)(2,1)S(1)}, bf16[128,512]{1,0:T(8,128)(2,1)}, u32[]{:S(2)}) copy-start(bf16[128,512]{1,0:T(8,128)(2,1)} %refs_8_.1) | copy-start | bytes 393220
  9.2 44.2 %copy-start.1 = (bf16[4096,256]{1,0:T(8,128)(2,1)S(1)}, bf16[4096,256]{1,0:T(8,128)(2,1)}, u32[]{:S(2)}) copy-start(bf16[4096,256]{1,0:T(8,128)(2,1)} %refs_4_.1) | copy-start | bytes 6291460
  13.1 32.3 %copy-start.22 = (s32[512]{0:T(512)S(1)}, s32[512]{0:T(512)}, u32[]{:S(2)}) copy-start(s32[512]{0:T(512)} %param.15) | copy-start | bytes 6148
  13.1 32.3 %copy-start.24 = (f32[256]{0:T(256)S(1)}, f32[256]{0:T(256)}, u32[]{:S(2)}) copy-start(f32[256]{0:T(256)} %param.19) | copy-start | bytes 3076
  13.1 40.3 %copy-start = (bf16[4096,256]{1,0:T(8,128)(2,1)S(1)}, bf16[4096,256]{1,0:T(8,128)(2,1)}, u32[]{:S(2)}) copy-start(bf16[4096,256]{1,0:T(8,128)(2,1)} %refs_3_.5) | copy-start | bytes 6291460
  50.6 7.0 %collective-permute-start.1 = (bf16[4096,256]{1,0:T(8,128)(2,1)}, bf16[4096,256]{1,0:T(8,128)(2,1)S(1)}, u32[]{:S(2)}, u32[]{:S(2)}) collective-permute-start(bf16[4096,256]{1,0:T(8,128)(2,1)} %collective-permute-done.refs_3_.refs_5_), channel_id=1, source_target_pairs={{0,2},{2,0},{1,3},{3,1},{4,6},{6,4},{5,7},{7,5},{8,10},{10,8},{9,1... | collective-permute-start | bytes 6291464 | tf_op jit(solution)/shard_map/ppermute | solution.py:528
  52.2 18.3 %collective-permute-start.2 = (bf16[512,256]{1,0:T(8,128)(2,1)S(1)}, bf16[512,256]{1,0:T(8,128)(2,1)S(1)}, u32[]{:S(2)}, u32[]{:S(2)}) collective-permute-start(bf16[512,256]{1,0:T(8,128)(2,1)S(1)} %get-tuple-element.32.refs_1_), channel_id=1, source_target_pairs={{0,1},{1,0},{2,3},{3,2},{4,5},{5,4},{6,7},{7,6},{8,9},{9,8},{10,11... | collective-permute-start | bytes 786440 | tf_op jit(solution)/shard_map/ppermute | solution.py:528
  57.6 6.0 %copy-start.9 = (bf16[1,4,512,256]{3,2,1,0:T(8,128)(2,1)S(1)}, bf16[1,4,512,256]{3,2,1,0:T(8,128)(2,1)}, u32[]{:S(2)}) copy-start(bf16[1,4,512,256]{3,2,1,0:T(8,128)(2,1)} %param.23) | copy-start | bytes 3145732
  57.6 6.0 %copy-start.23 = (f32[256]{0:T(256)S(1)}, f32[256]{0:T(256)}, u32[]{:S(2)}) copy-start(f32[256]{0:T(256)} %param.22) | copy-start | bytes 3076
  57.6 6.0 %copy-start.5 = (bf16[4096,256]{1,0:T(8,128)(2,1)}, bf16[4096,256]{1,0:T(8,128)(2,1)S(1)}, u32[]{:S(2)}) copy-start(bf16[4096,256]{1,0:T(8,128)(2,1)S(1)} %collective-permute-done.1.refs_4_.refs_6_) | copy-start | bytes 6291460
  63.6 2.2 %copy-start.20 = (bf16[384,512]{1,0:T(8,128)(2,1)S(1)}, bf16[384,512]{1,0:T(8,128)(2,1)}, u32[]{:S(2)}) copy-start(bf16[384,512]{1,0:T(8,128)(2,1)} %refs_1_.1) | copy-start | bytes 1179652
  64.8 0.8 copy-start.18
  65.6 7.6 %collective-permute-start.3 = (bf16[512,256]{1,0:T(8,128)(2,1)S(1)}, bf16[512,256]{1,0:T(8,128)(2,1)S(1)}, u32[]{:S(2)}, u32[]{:S(2)}) collective-permute-start(bf16[512,256]{1,0:T(8,128)(2,1)S(1)} %get-tuple-element.35.refs_5_.refs_3_.refs_2_), channel_id=1, source_target_pairs={{0,1},{1,0},{2,3},{3,2},{4,5},{5,4},{6,7},{7,6},{8,9},{9,8},{10,11... | collective-permute-start | bytes 786440 | tf_op jit(solution)/shard_map/ppermute | solution.py:528
  73.2 1.6 copy-start.7
  82.6 9.8 %collective-permute-start.5 = (bf16[8,256,256]{2,1,0:T(8,128)(2,1)}, bf16[8,256,256]{2,1,0:T(8,128)(2,1)}, u32[]{:S(2)}, u32[]{:S(2)}) collective-permute-start(bf16[8,256,256]{2,1,0:T(8,128)(2,1)} %get-tuple-element.38.refs_7_), channel_id=1, source_target_pairs={{0,2},{2,0},{1,3},{3,1},{4,6},{6,4},{5,7},{7,5},{8,10},{10,8},{9,1... | collective-permute-start | bytes 3145736 | tf_op jit(solution)/shard_map/ppermute | solution.py:528
  83.8 13.1 %collective-permute-start.4 = (bf16[8,256,256]{2,1,0:T(8,128)(2,1)}, bf16[8,256,256]{2,1,0:T(8,128)(2,1)}, u32[]{:S(2)}, u32[]{:S(2)}) collective-permute-start(bf16[8,256,256]{2,1,0:T(8,128)(2,1)} %get-tuple-element.40), channel_id=1, source_target_pairs={{0,2},{2,0},{1,3},{3,1},{4,6},{6,4},{5,7},{7,5},{8,10},{10,8},{9,1... | collective-permute-start | bytes 3145736 | tf_op jit(solution)/shard_map/ppermute | solution.py:528
  83.8 1.6 copy-start.2
  94.6 1.0 copy-start.10
  95.6 20.6 %collective-permute-start.6 = (bf16[4,256,256]{2,1,0:T(8,128)(2,1)}, bf16[4,256,256]{2,1,0:T(8,128)(2,1)}, u32[]{:S(2)}, u32[]{:S(2)}) collective-permute-start(bf16[4,256,256]{2,1,0:T(8,128)(2,1)} %get-tuple-element.42.refs_3_), channel_id=1, source_target_pairs={{0,4},{4,0},{1,5},{5,1},{2,6},{6,2},{3,7},{7,3},{8,12},{12,8},{9,1... | collective-permute-start | bytes 1572872 | tf_op jit(solution)/shard_map/ppermute | solution.py:528
  99.1 1.0 copy-start.12
  100.1 23.3 %collective-permute-start.7 = (bf16[4,256,256]{2,1,0:T(8,128)(2,1)}, bf16[4,256,256]{2,1,0:T(8,128)(2,1)}, u32[]{:S(2)}, u32[]{:S(2)}) collective-permute-start(bf16[4,256,256]{2,1,0:T(8,128)(2,1)} %get-tuple-element.43.refs_7_), channel_id=1, source_target_pairs={{0,4},{4,0},{1,5},{5,1},{2,6},{6,2},{3,7},{7,3},{8,12},{12,8},{9,1... | collective-permute-start | bytes 1572872 | tf_op jit(solution)/shard_map/ppermute | solution.py:528
  100.4 1.6 copy-start.3
  102.0 1.6 copy-start.6
  103.6 12.6 %copy-start.11 = (f32[4,256,256]{2,1,0:T(8,128)S(1)}, f32[4,256,256]{2,1,0:T(8,128)}, u32[]{:S(2)}) copy-start(f32[4,256,256]{2,1,0:T(8,128)} %copy-done.10) | copy-start | bytes 3145732
  103.6 14.2 %copy-start.16 = (bf16[4,256,256]{2,1,0:T(8,128)(2,1)S(1)}, bf16[4,256,256]{2,1,0:T(8,128)(2,1)}, u32[]{:S(2)}) copy-start(bf16[4,256,256]{2,1,0:T(8,128)(2,1)} %get-tuple-element.45.refs_3_) | copy-start | bytes 1572868
  103.6 14.2 %copy-start.17 = (f32[512,256]{1,0:T(8,128)S(1)}, f32[512,256]{1,0:T(8,128)}, u32[]{:S(2)}) copy-start(f32[512,256]{1,0:T(8,128)} %get-tuple-element.44.refs_1_) | copy-start | bytes 1572868
  103.6 14.2 %copy-start.19 = (f32[512,256]{1,0:T(8,128)S(1)}, f32[512,256]{1,0:T(8,128)}, u32[]{:S(2)}) copy-start(f32[512,256]{1,0:T(8,128)} %copy-done.18) | copy-start | bytes 1572868
  103.6 14.2 %copy-start.21 = (bf16[4,128,256]{2,1,0:T(8,128)(2,1)S(1)}, bf16[4,128,256]{2,1,0:T(8,128)(2,1)}, u32[]{:S(2)}) copy-start(bf16[4,128,256]{2,1,0:T(8,128)(2,1)} %get-tuple-element.46.refs_4_) | copy-start | bytes 786436
  116.2 1.8 copy-start.8
  117.6 8.2 %collective-permute-start.9 = (bf16[2,256,256]{2,1,0:T(8,128)(2,1)S(1)}, bf16[2,256,256]{2,1,0:T(8,128)(2,1)S(1)}, u32[]{:S(2)}, u32[]{:S(2)}) collective-permute-start(bf16[2,256,256]{2,1,0:T(8,128)(2,1)S(1)} %get-tuple-element.49.refs_10_), channel_id=1, source_target_pairs={{0,8},{8,0},{1,9},{9,1},{2,10},{10,2},{3,11},{11,3},{4,12},{12,4},... | collective-permute-start | bytes 786440 | tf_op jit(solution)/shard_map/ppermute | solution.py:528
  118.0 5.4 %copy-start.13 = (f32[4,256,256]{2,1,0:T(8,128)S(1)}, f32[4,256,256]{2,1,0:T(8,128)}, u32[]{:S(2)}) copy-start(f32[4,256,256]{2,1,0:T(8,128)} %copy-done.12) | copy-start | bytes 3145732
  124.5 8.7 %collective-permute-start.8 = (bf16[2,256,256]{2,1,0:T(8,128)(2,1)S(1)}, bf16[2,256,256]{2,1,0:T(8,128)(2,1)S(1)}, u32[]{:S(2)}, u32[]{:S(2)}) collective-permute-start(bf16[2,256,256]{2,1,0:T(8,128)(2,1)S(1)} %get-tuple-element.52.refs_3_), channel_id=1, source_target_pairs={{0,8},{8,0},{1,9},{9,1},{2,10},{10,2},{3,11},{11,3},{4,12},{12,4},... | collective-permute-start | bytes 786440 | tf_op jit(solution)/shard_map/ppermute | solution.py:528
  125.8 10.1 %collective-permute-start.11 = (bf16[1,256,256]{2,1,0:T(8,128)(2,1)S(1)}, bf16[1,256,256]{2,1,0:T(8,128)(2,1)S(1)}, u32[]{:S(2)}, u32[]{:S(2)}) collective-permute-start(bf16[1,256,256]{2,1,0:T(8,128)(2,1)S(1)} %get-tuple-element.54.refs_3_), channel_id=1, source_target_pairs={{0,16},{16,0},{1,17},{17,1},{2,18},{18,2},{3,19},{19,3},{4,20},{20... | collective-permute-start | bytes 393224 | tf_op jit(solution)/shard_map/ppermute | solution.py:528
  133.3 9.5 %collective-permute-start.10 = (bf16[1,256,256]{2,1,0:T(8,128)(2,1)S(1)}, bf16[1,256,256]{2,1,0:T(8,128)(2,1)S(1)}, u32[]{:S(2)}, u32[]{:S(2)}) collective-permute-start(bf16[1,256,256]{2,1,0:T(8,128)(2,1)S(1)} %get-tuple-element.56.refs_3_), channel_id=1, source_target_pairs={{0,16},{16,0},{1,17},{17,1},{2,18},{18,2},{3,19},{19,3},{4,20},{20... | collective-permute-start | bytes 393224 | tf_op jit(solution)/shard_map/ppermute | solution.py:528
  136.0 17.5 %collective-permute-start.13 = (bf16[1,256,256]{2,1,0:T(8,128)(2,1)S(1)}, bf16[1,256,256]{2,1,0:T(8,128)(2,1)S(1)}, u32[]{:S(2)}, u32[]{:S(2)}) collective-permute-start(bf16[1,256,256]{2,1,0:T(8,128)(2,1)S(1)} %down_share.1.refs_3_.refs_1_), channel_id=1, source_target_pairs={{0,16},{16,0},{1,17},{17,1},{2,18},{18,2},{3,19},{19,3},{4,20},{20... | collective-permute-start | bytes 393224 | tf_op jit(solution)/shard_map/ppermute | solution.py:528
  142.8 10.9 %collective-permute-start.12 = (bf16[1,256,256]{2,1,0:T(8,128)(2,1)S(1)}, bf16[1,256,256]{2,1,0:T(8,128)(2,1)S(1)}, u32[]{:S(2)}, u32[]{:S(2)}) collective-permute-start(bf16[1,256,256]{2,1,0:T(8,128)(2,1)S(1)} %up_share.1.refs_3_.refs_1_), channel_id=1, source_target_pairs={{0,16},{16,0},{1,17},{17,1},{2,18},{18,2},{3,19},{19,3},{4,20},{20... | collective-permute-start | bytes 393224 | tf_op jit(solution)/shard_map/ppermute | solution.py:528
  146.2 50.9 %all-to-all-start.1 = ((bf16[64,32,256]{2,1,0:T(8,128)(2,1)}), bf16[64,32,256]{2,1,0:T(8,128)(2,1)}, u32[]{:S(2)}, u32[]{:S(2)}) async-start(bf16[64,32,256]{2,1,0:T(8,128)(2,1)} %bitcast.22), calls=%async_computation.1 | async-start | bytes 2097152 | tf_op jit(solution)/shard_map/all_to_all | solution.py:567
  153.6 24.2 %collective-permute-start.15 = (bf16[2,256,256]{2,1,0:T(8,128)(2,1)S(1)}, bf16[2,256,256]{2,1,0:T(8,128)(2,1)S(1)}, u32[]{:S(2)}, u32[]{:S(2)}) collective-permute-start(bf16[2,256,256]{2,1,0:T(8,128)(2,1)S(1)} %bitcast.64), channel_id=1, source_target_pairs={{0,8},{8,0},{1,9},{9,1},{2,10},{10,2},{3,11},{11,3},{4,12},{12,4},... | collective-permute-start | bytes 786440 | tf_op jit(solution)/shard_map/ppermute | solution.py:528
  153.7 25.0 %collective-permute-start.14 = (bf16[2,256,256]{2,1,0:T(8,128)(2,1)S(1)}, bf16[2,256,256]{2,1,0:T(8,128)(2,1)S(1)}, u32[]{:S(2)}, u32[]{:S(2)}) collective-permute-start(bf16[2,256,256]{2,1,0:T(8,128)(2,1)S(1)} %bitcast.66), channel_id=1, source_target_pairs={{0,4},{4,0},{1,5},{5,1},{2,6},{6,2},{3,7},{7,3},{8,12},{12,8},{9,1... | collective-permute-start | bytes 786440 | tf_op jit(solution)/shard_map/ppermute | solution.py:528
  177.8 13.1 %collective-permute-start.17 = (bf16[4,256,256]{2,1,0:T(8,128)(2,1)S(1)}, bf16[4,256,256]{2,1,0:T(8,128)(2,1)S(1)}, u32[]{:S(2)}, u32[]{:S(2)}) collective-permute-start(bf16[4,256,256]{2,1,0:T(8,128)(2,1)S(1)} %bitcast.54), channel_id=1, source_target_pairs={{0,4},{4,0},{1,5},{5,1},{2,6},{6,2},{3,7},{7,3},{8,12},{12,8},{9,1... | collective-permute-start | bytes 1572872 | tf_op jit(solution)/shard_map/ppermute | solution.py:528
  178.8 12.4 %collective-permute-start.16 = (bf16[2,512,256]{2,1,0:T(8,128)(2,1)S(1)}, bf16[2,512,256]{2,1,0:T(8,128)(2,1)S(1)}, u32[]{:S(2)}, u32[]{:S(2)}) collective-permute-start(bf16[2,512,256]{2,1,0:T(8,128)(2,1)S(1)} %bitcast.56), channel_id=1, source_target_pairs={{0,8},{8,0},{1,9},{9,1},{2,10},{10,2},{3,11},{11,3},{4,12},{12,4},... | collective-permute-start | bytes 1572872 | tf_op jit(solution)/shard_map/ppermute | solution.py:528
  191.3 5.8 %collective-permute-start.18 = (bf16[8,256,256]{2,1,0:T(8,128)(2,1)S(1)}, bf16[8,256,256]{2,1,0:T(8,128)(2,1)}, u32[]{:S(2)}, u32[]{:S(2)}) collective-permute-start(bf16[8,256,256]{2,1,0:T(8,128)(2,1)S(1)} %bitcast.62), channel_id=1, source_target_pairs={{0,2},{2,0},{1,3},{3,1},{4,6},{6,4},{5,7},{7,5},{8,10},{10,8},{9,1... | collective-permute-start | bytes 3145736 | tf_op jit(solution)/shard_map/ppermute | solution.py:528
  193.3 7.3 %collective-permute-start.19 = (bf16[8,256,256]{2,1,0:T(8,128)(2,1)S(1)}, bf16[8,256,256]{2,1,0:T(8,128)(2,1)S(1)}, u32[]{:S(2)}, u32[]{:S(2)}) collective-permute-start(bf16[8,256,256]{2,1,0:T(8,128)(2,1)S(1)} %bitcast.51), channel_id=1, source_target_pairs={{0,2},{2,0},{1,3},{3,1},{4,6},{6,4},{5,7},{7,5},{8,10},{10,8},{9,1... | collective-permute-start | bytes 3145736 | tf_op jit(solution)/shard_map/ppermute | solution.py:528

commit v4 on v3

--- a/solution.py
+++ b/solution.py
@@ -12,12 +12,13 @@
 VMEM_BYTES = 24 * 1024 * 1024
 BF = jnp.bfloat16
 F32 = jnp.float32
+WIDE_BYTES = 56 * 1024 * 1024
 LANES = 128
 PART = 256
 
 
-def params():
-    return pltpu.CompilerParams(vmem_limit_bytes=VMEM_BYTES)
+def params(limit=VMEM_BYTES):
+    return pltpu.CompilerParams(vmem_limit_bytes=limit)
 
 
 def ordered(kernel, ins, deps):
@@ -171,13 +172,13 @@
     )(received, slot_field[None, :], proj_y, proj_p, gain, *filled, *deps)
 
 
-def linear_kernel(embeds, linear_w, gain, cot, before, layer_out, partial):
+def linear_kernel(embeds, linear_w, gain, cot, layer_out, partial):
     made = linear_w.shape[0]
     first = embeds.shape[1] - made
     x = embeds[0]
     summed = nn(linear_w[...], x) + x[first:].astype(F32)
     unit, scale = layer_norm(summed)
-    layer_out[0, :first] = before[0]
+    layer_out[0, :first] = jnp.zeros_like(layer_out[0, :first])
     layer_out[0, first:] = (unit * gain[...]).astype(BF)
     grad = norm_back(unit, scale, gain[...], cot[0, first:].astype(F32))
     back = tn(linear_w[...], grad.astype(BF))
@@ -185,24 +186,23 @@
     partial[0, first:] = back[first:] + grad
 
 
-def linear(embeds, linear_w, gain, cot, top_out, deps):
+def linear(embeds, linear_w, gain, cot, deps):
     samples, fields, width = embeds.shape
     return pl.pallas_call(
-        ordered(linear_kernel, 5, deps),
+        ordered(linear_kernel, 4, deps),
         grid=(samples,),
         in_specs=[
             by_sample(1, fields, width),
             const(*linear_w.shape),
             const(1, width),
             by_sample(1, fields, width),
-            by_sample(1, top_out.shape[1], width),
         ]
         + unread(deps),
         out_specs=[by_sample(1, fields, width)] * 2,
         out_shape=[pltpu.HBM(cot.shape, BF), pltpu.HBM(cot.shape, F32)],
         compiler_params=params(),
         name="linear",
-    )(embeds, linear_w, gain, cot, top_out, *deps)
+    )(embeds, linear_w, gain, cot, *deps)
 
 
 def activate(gate):
@@ -224,18 +224,27 @@
     return steps, specs
 
 
-def tiles_at(steps, own, near, refs):
+def at_tiles(steps, own, near, refs, work):
     step = pl.program_id(0)
     count = len(refs) // 2 - own
-    up, down = (refs[0][...], refs[1][...]) if own else (None, None)
+
+    if own:
+
+        @pl.when(step < steps)
+        def _():
+            work(refs[0], refs[1])
+
     for n in range(count):
-        fetched, traded = refs[2 * own + n][...], refs[2 * own + count + n][...]
-        far_up = jnp.where(near[0] == 0, fetched, traded)
-        far_down = jnp.where(near[0] == 0, traded, fetched)
-        here = step < (n + own) * steps
-        up = far_up if up is None else jnp.where(here, up, far_up)
-        down = far_down if down is None else jnp.where(here, down, far_down)
-    return (up, down)
+        fetched, traded = refs[2 * own + n], refs[2 * own + count + n]
+        here = jnp.logical_and(step >= (n + own) * steps, step < (n + own + 1) * steps)
+
+        @pl.when(jnp.logical_and(here, near[0] == 0))
+        def _(up=fetched, down=traded):
+            work(up, down)
+
+        @pl.when(jnp.logical_and(here, near[0] != 0))
+        def _(up=traded, down=fetched):
+            work(up, down)
 
 
 def accumulate(out, begun, term):
@@ -249,27 +258,31 @@
 
 
 def up_kernel(steps, own, begun, near, rows, *refs):
-    up, down = tiles_at(steps, own, near, refs[begun:-1])
-    term = None
-    for at in range(0, up.shape[0], PART):
-        hidden, _ = activate(nt(rows[...], up[at : at + PART]))
-        more = nn(hidden, down[at : at + PART])
-        term = more if term is None else term + more
-    accumulate(refs[-1], refs[0] if begun else None, term)
+    def work(up, down):
+        hidden, _ = activate(nt(rows[...], up[...]))
+        accumulate(refs[-1], refs[0] if begun else None, nn(hidden, down[...]))
+
+    at_tiles(steps, own, near, refs[begun:-1], work)
 
 
 def back_kernel(steps, own, begun, near, rows, grads, *refs):
-    up, down = tiles_at(steps, own, near, refs[begun:-1])
-    term = None
-    for at in range(0, up.shape[0], PART):
-        part = up[at : at + PART]
-        _, slope = activate(nt(rows[...], part))
-        more = nn((nt(grads[...], down[at : at + PART]) * slope).astype(BF), part)
-        term = more if term is None else term + more
-    accumulate(refs[-1], refs[0] if begun else None, term)
-
-
-def mlp(kernel, near, blocks, w_up, w_down, fetched, traded, begun, deps, name, own=True):
+    def work(up, down):
+        term = None
+        gate, grad = nt(rows[...], up[:PART, :]), nt(grads[...], down[:PART, :])
+        for at in range(0, up.shape[0], PART):
+            now, grad_now, after = gate, grad, at + PART
+            if after < up.shape[0]:
+                gate = nt(rows[...], up[after : after + PART, :])
+                grad = nt(grads[...], down[after : after + PART, :])
+            _, slope = activate(now)
+            more = nn((grad_now * slope).astype(BF), up[at:after, :])
+            term = more if term is None else term + more
+        accumulate(refs[-1], refs[0] if begun else None, term)
+
+    at_tiles(steps, own, near, refs[begun:-1], work)
+
+
+def mlp(kernel, near, blocks, w_up, w_down, fetched, traded, begun, deps, name, own=True, limit=VMEM_BYTES):
     steps, specs = tiles_of(w_up, fetched, own, 1024)
     begun = [] if begun is None else [begun]
     weights = [w_up, w_down] if own else []
@@ -286,12 +299,12 @@
             out_specs=const(*blocks[0].shape),
         ),
         out_shape=jax.ShapeDtypeStruct(blocks[0].shape, F32),
-        compiler_params=params(),
+        compiler_params=params(limit),
         name=name,
     )(near, *blocks, *begun, *weights, *fetched, *traded, *deps)
 
 
-def top_kernel(ff, embeds, gain, cot, layer_out, grad, grad_ff):
+def top_kernel(ff, embeds, gain, cot, _, layer_out, grad, grad_ff):
     summed = ff[...] + embeds[0].astype(F32)
     unit, scale = layer_norm(summed)
     layer_out[0] = (unit * gain[...]).astype(BF)
@@ -300,7 +313,7 @@
     grad_ff[...] = g.astype(BF)
 
 
-def top(ff, embeds, gain, cot):
+def top(ff, embeds, gain, cot, layer_out):
     samples, _, width = embeds.shape
     made = ff.shape[0] // samples
     return pl.pallas_call(
@@ -311,16 +324,18 @@
             by_sample(1, made, width),
             const(1, width),
             by_sample(1, made, width),
-        ],
+        ]
+        + unread([layer_out]),
         out_specs=[by_sample(1, made, width), by_sample(made, width), by_sample(made, width)],
         out_shape=[
-            jax.ShapeDtypeStruct((samples, made, width), BF),
+            pltpu.HBM(cot.shape, BF),
             jax.ShapeDtypeStruct(ff.shape, F32),
             jax.ShapeDtypeStruct(ff.shape, BF),
         ],
+        input_output_aliases={4: 0},
         compiler_params=params(),
         name="top",
-    )(ff, embeds, gain, cot)
+    )(ff, embeds, gain, cot, layer_out)
 
 
 def fill(blocks, out):
@@ -341,22 +356,17 @@
     shares, units, width = grad_down.shape
     up = w_up[...].reshape(shares * units, width)
     down = w_down[...].reshape(shares * units, width)
-    part = min(units * shares, PART)
-    each = part // units
-    for n in range(shares // each):
-        at = slice(n * part, (n + 1) * part)
-        hidden, slope = activate(nt(up[at], rows[...]))
-        gate = (nt(down[at], grads[...]) * slope).astype(BF)
-        for out, left, right in ((grad_down, hidden, grads), (grad_up, gate, rows)):
-            grad = nn(left, right[...]).reshape(each, units, width)
-            out[n * each : (n + 1) * each] = grad.astype(out.dtype)
+    hidden, slope = activate(nt(up, rows[...]))
+    gated = (nt(down, grads[...]) * slope).astype(BF)
+    for out, left, right in ((grad_down, hidden, grads), (grad_up, gated, rows)):
+        out[...] = nn(left, right[...]).reshape(shares, units, width).astype(out.dtype)
 
 
 def weight_grads(at, rows, grads, w_up, w_down, kind, deps, name):
     shares, _, units, width = w_up.shape
     blocks = len(rows)
     count = sum(block.shape[0] for block in rows)
-    step = max(1, min(shares, 512 // units if count <= 1024 else 128 // units))
+    step = max(1, min(shares, 1024 // units if count <= 1024 else 128 // units))
     shared = pl.BlockSpec((step, 1, units, width), lambda g, at: (g, at[0], 0, 0))
     given = pl.BlockSpec((step, units, width), lambda g, at: (g, 0, 0))
     return pl.pallas_call(
@@ -371,7 +381,7 @@
             scratch_shapes=[pltpu.VMEM((count, width), BF)] * 2,
         ),
         out_shape=[jax.ShapeDtypeStruct((shares, units, width), kind)] * 2,
-        compiler_params=params(),
+        compiler_params=params(WIDE_BYTES),
         name=name,
     )(at, *rows, *grads, w_up, w_down, *deps)
 
@@ -427,26 +437,29 @@
     return out
 
 
-def join_last_kernel(_, piece, *refs):
-    refs[-1][:, 0] = piece[...].astype(F32)
-
-
-def join_last(at, piece, filled, name):
-    before, units, width = piece.shape
+def join_last_kernel(count, _, *refs):
+    for piece, out in zip(refs[:count], refs[-count:]):
+        out[:, 0] = piece[...].astype(F32)
+
+
+def join_last(at, pieces, filled, name):
+    before, units, width = pieces[0].shape
+    count = len(pieces)
     step = max(1, before // 4)
     return pl.pallas_call(
-        join_last_kernel,
+        functools.partial(join_last_kernel, count),
         grid_spec=pltpu.PrefetchScalarGridSpec(
             num_scalar_prefetch=1,
             grid=(before // step,),
-            in_specs=[pl.BlockSpec((step, units, width), lambda g, at: (g, 0, 0))] + unread(filled),
-            out_specs=pl.BlockSpec((step, 1, units, width), lambda g, at: (g, at[0], 0, 0)),
+            in_specs=[pl.BlockSpec((step, units, width), lambda g, at: (g, 0, 0))] * count
+            + unread(filled),
+            out_specs=[pl.BlockSpec((step, 1, units, width), lambda g, at: (g, at[0], 0, 0))] * count,
         ),
-        out_shape=pltpu.HBM((before, 2, units, width), F32),
-        input_output_aliases={2: 0} if filled else {},
+        out_shape=[pltpu.HBM((before, 2, units, width), F32)] * count,
+        input_output_aliases={1 + count + n: n for n in range(len(filled))},
         compiler_params=params(),
         name=name,
-    )(at, piece, *filled)
+    )(at, *pieces, *filled)
 
 
 def tail_kernel(
@@ -574,38 +587,30 @@
         received, slot_field, proj_y, proj_p, gain_fm, [], samples, 0, [], "front"
     )
     all_rows = [rows, *spread(rows)]
-    ff = mlp(up_kernel, places[near], [rows], w_up, w_down, [], [], None, [], "up_own")
     fetched, _ = lax.optimization_barrier((fetched, rows))
     traded = [turn(weight, near, 2, 1) for weight in fetched]
+    layer_out, partial = linear(embeds, linear_w, gain_out, cot, [rows])
+    ff = mlp(up_kernel, places[near], [rows], w_up, w_down, [], [], None, [partial], "up_own")
     ff = mlp(up_kernel, places[near], [rows], w_up, w_down, fetched, traded, ff, [], "up_other", False)
-    layer_out, grad_top, grads = top(ff, embeds, gain_out, cot)
+    layer_out, grad_top, grads = top(ff, embeds, gain_out, cot, layer_out)
     all_grads = [grads, *spread(grads)]
-    layer_out, partial = linear(embeds, linear_w, gain_out, cot, layer_out, [grads])
 
     units = w_up.shape[0] // owners
     shared = (owners // 2, 2, units, width)
     shares = (w_up.reshape(shared), w_down.reshape(shared))
-    away = weight_grads(1 - places[near], all_rows, all_grads, *shares, BF, [partial], "weights_1")
-    arrived = [turn(part, near, 2, 1) for part in away]
-    kept_parts = weight_grads(places[near], all_rows, all_grads, *shares, F32, [away[0]], "weights_0")
-    last = [kept_parts[0]]
-    sums = [list(terms) for terms in zip(kept_parts, arrived)]
-
-    def cut(arrays, size):
-        return [a.reshape(-1, size, units, width) for a in arrays]
-
-    def halve(n, axis):
-        nonlocal last
-        name = f"{('down', 'up')[n]}_split_{axis}"
-        ((keep, away),) = split_sum(places[axis], 2, [cut(sums[n], 2)], F32, last, name)
-        last = [away]
-        sums[n] = [keep, turn(away, axis, 2, 1)]
-
-    halve(0, mid)
-    halve(1, mid)
-    upstream = mlp(back_kernel, places[near], [rows, grads], w_up, w_down, fetched, traded, None, last, "back")
-    last = [upstream]
-    halve(0, outer[-1])
+    upstream = mlp(
+        back_kernel,
+        places[near],
+        [rows, grads],
+        w_up,
+        w_down,
+        fetched,
+        traded,
+        None,
+        [],
+        "back",
+        limit=WIDE_BYTES,
+    )
     slot_grads = tail(
         upstream,
         (inter, crossed, mixing, grad_top, partial),
@@ -614,37 +619,57 @@
         proj_p,
         slot_field,
         owners,
-        last,
+        [*all_rows[1:], *all_grads[1:]],
     )
-    last = [slot_grads]
-    halve(1, outer[-1])
     returned = exchange(slot_grads)
-    for axis in reversed(outer[:-1]):
-        halve(0, axis)
-        halve(1, axis)
-    weights, orders = [], []
+    away = weight_grads(1 - places[near], all_rows, all_grads, *shares, BF, [slot_grads], "weights_1")
+    arrived = [turn(part, near, 2, 1) for part in away]
+    kept_parts = weight_grads(places[near], all_rows, all_grads, *shares, BF, [away[0]], "weights_0")
+    last = [kept_parts[0]]
+    sums = [list(terms) for terms in zip(kept_parts, arrived)]
+
+    orders = [(*outer, mid, near), (*outer[:1], mid, *outer[1:], near)]
+    left = [list(emb[:-1]), list(emb[:-1])]
+
+    def halve(n, step):
+        nonlocal last
+        axis = orders[n][step]
+        before = 2 ** left[n].index(axis)
+        left[n].remove(axis)
+        terms = [term.reshape(before, 2, -1, width) for term in sums[n]]
+        name = f"{('down', 'up')[n]}_split_{axis}"
+        ((keep, away),) = split_sum(places[axis], 2, [terms], F32, last, name)
+        last = [away]
+        sums[n] = [keep, turn(away, axis, 2, 1)]
+
+    for step in range(len(emb) - 2, -1, -1):
+        halve(0, step)
+        halve(1, step)
+        if step == len(emb) - 2:
+            last = [*last, returned]
+    weights = []
     for n, name in enumerate(("down", "up")):
-        ((share,),) = split_sum(places[near], 1, [cut(sums[n], 1)], BF, last, f"{name}_share")
+        terms = [term.reshape(1, 1, units, width) for term in sums[n]]
+        ((share,),) = split_sum(places[near], 1, [terms], BF, last, f"{name}_share")
         last = [share]
         weights.append(share.reshape(-1, width))
-        orders.append((*outer, mid, near) if n == 0 else (*outer[:1], mid, *outer[1:], near))
     done = [[], []]
-    for step in range(len(emb)):
+    for step in range(len(emb) - 1):
         for n, name in enumerate(("down", "up")):
             axis = orders[n][step]
             at = emb.index(axis)
             before = 2 ** sum(emb.index(other) < at for other in done[n])
             value = weights[n].reshape(before, -1, width)
             other = turn(value, axis, 2, 1)
-            if step == len(emb) - 1:
-                joined = join_last(places[axis], value, [], f"{name}_keep_{axis}")
-                joined = join_last(1 - places[axis], other, [joined], f"{name}_join_{axis}")
-            else:
-                joined = join(places[axis], [value, other], BF, last, f"{name}_join_{axis}")
-                last = [joined]
+            joined = join(places[axis], [value, other], BF, last, f"{name}_join_{axis}")
+            last = [joined]
             weights[n] = joined.reshape(-1, width)
             done[n].append(axis)
-    down, up = [w.reshape(-1, width) for w in weights]
+    mine = [value.reshape(owners // 2, units, width) for value in weights]
+    others = [turn(value, near, 2, 1) for value in mine]
+    joined = join_last(places[near], mine, [], "weights_mine")
+    joined = join_last(1 - places[near], others, joined, "weights_others")
+    down, up = [value.reshape(-1, width) for value in joined]
     return (layer_out[None], returned.reshape(1, owners * samples, -1, width), up, down)
 
 

time: 208 us -> 199 us (0.957)
  waiting for transfers between devices: 48.8 us -> 35.6 us
  starting transfers between devices: 29.9 us -> 39.8 us
  Pallas kernels: 73.9 us -> 70.1 us
    ppermute x20, waiting for transfers between devices: 48.8 us -> 35.6 us  [turn(): lax.ppermute(value, axis, [(i, (i + shift) % size) for i in range(size)])]
    ppermute x20, starting transfers between devices: 22.5 us -> 33.5 us  [turn(): lax.ppermute(value, axis, [(i, (i + shift) % size) for i in range(size)])]
    pallas_call x5 -> x3, Pallas kernels: 13.7 us -> 9.55 us  [the longest x2 4.86 us: join_last(): pl.pallas_call(functools.partial(join_last_kernel, count), grid_spec=pltp...]
    unnamed x56 -> x64, local copies, waits for them, and re-layouts: 15.4 us -> 14.3 us
  transfers between devices with their start and end apart: 21 -> 21, of which waited for: 7 -> 10; matrix products, arithmetic and copies ran while one was open for 0% -> 0% of each run, Pallas kernels for 31% -> 32%
where the time goes in v4:
time: 199 us; the launch traced here: 197 us
  Pallas kernels  70.1 us (35%)
  starting transfers between devices  39.8 us (20%)
  waiting for transfers between devices  35.6 us (18%)
  blocking collectives  32.2 us (16%)
  local copies, waits for them, and re-layouts  14.4 us (7%)
  other arithmetic  3.49 us (2%)
    ppermute x20, waiting for transfers between devices, turn(): lax.ppermute(value, axis, [(i, (i + shift) % size) for i in range(size)])  35.6 us
    ppermute x20, starting transfers between devices, turn(): lax.ppermute(value, axis, [(i, (i + shift) % size) for i in range(size)])  33.5 us
    all_to_all x1, blocking collectives, exchange(): moved = lax.all_to_all(flat, emb, split_axis=0, concat_axis=0, tiled=True)  32.2 us
    pallas_call x3, Pallas kernels, mlp(): pl.pallas_call(ordered(functools.partial(kernel, steps, int(own), len(beg...  22.2 us
    pallas_call x2, Pallas kernels, weight_grads(): pl.pallas_call(ordered(functools.partial(weight_kernel, blocks), 1 + 2 *...  16.4 us
    unnamed x64, local copies, waits for them, and re-layouts  14.3 us
    all_to_all x1, starting transfers between devices, exchange(): moved = lax.all_to_all(flat, emb, split_axis=0, concat_axis=0, tiled=True)  6.23 us
    pallas_call x8, Pallas kernels, split_sum(): whole(ordered(functools.partial(split_kernel, count, each), 1 + sum(each)...  5.69 us
  transfers between devices with their start and end apart: 21, of which 10 were waited for; matrix products, arithmetic and copies ran while one was open for 0% of the time, Pallas kernels for 32%

profile of v4, /device:TPU:9, one launch (start us, length us, event | category | flops | bytes accessed | tf_op | source)
XLA Modules:
  0.0 196.7 jit_solution(8480578911520805598)
XLA Ops:
  0.7 3.2 %broadcast_select_fusion = bf16[4096,256]{1,0:T(8,128)(2,1)} fusion(bf16[4096,256]{1,0:T(8,128)(2,1)} %refs_3_.5, bf16[4096,256]{1,0:T(8,128)(2,1)} %refs_4_.1, pred[]{:T(512)S(6)} %eq.3), kind=kLoop, calls=%fused_computation | loop fusion | flops 1048576 | bytes 6291457 | tf_op jit(solution)/shard_map/select_n | solution.py:583
  3.8 1.2 collective-permute-start
  5.8 3.4 %copy-done.3 = bf16[32,512,256]{2,1,0:T(8,128)(2,1)S(1)} copy-done((bf16[32,512,256]{2,1,0:T(8,128)(2,1)S(1)}, bf16[32,512,256]{2,1,0:T(8,128)(2,1)}, u32[]{:S(2)}) %copy-start.3) | copy-done | bytes 8388632
  9.2 3.9 %pool.1 = bf16[16,4,32,256]{3,2,1,0:T(8,128)(2,1)S(1)} custom-call(s32[32,64,4]{2,1,0:T(8,128)S(1)} %fusion.ids_ref, bf16[32,512,256]{2,1,0:T(8,128)(2,1)S(1)} %copy-done.3), custom_call_target="tpu_custom_call" | custom-call | tf_op jit(solution)/shard_map/pool/pallas_call | solution.py:89
  13.2 32.2 %all_to_all.10 = bf16[64,32,256]{2,1,0:T(8,128)(2,1)S(1)} all-to-all(bf16[64,32,256]{2,1,0:T(8,128)(2,1)S(1)} %bitcast.60), channel_id=1, replica_groups=mesh['emb_0'=2,'emb_1'=2,'emb_2'=2,'emb_3'=2,'wide'=2] {'emb_0','emb_1',..., dimensions={0} | all-to-all | bytes 2097152 | tf_op jit(solution)/shard_map/all_to_all | solution.py:580
  45.5 4.8 %front.1 = (bf16[4,512,256]{2,1,0:T(8,128)(2,1)S(1)}, bf16[4,256,256]{2,1,0:T(8,128)(2,1)}, bf16[4,128,256]{2,1,0:T(8,128)(2,1)}, f32[512,256]{1,0:T(8,128)}, bf16[512,256]{1,0:T(8,128)(2,1)S(1)}) custom-call(bf16[16,4,32,256]{3,2,1,0:T(8,128)(2,1)S(1)} %bitcast.66, s32[1,512]{1,0:T(1,128)S(1)} %bitcast.84, bf16[512,256]{1,0:T(8,128)(2,1)S(1)} %copy-done.13, ...), custom_call_target="tpu_custom_call" | custom-call | tf_op jit(solution)/shard_map/front/pallas_call | solution.py:142
  50.6 1.6 collective-permute-start.1
  52.2 1.2 collective-permute-start.2
  53.4 4.7 %linear.1 = (bf16[4,512,256]{2,1,0:T(8,128)(2,1)}, f32[4,512,256]{2,1,0:T(8,128)}) custom-call(bf16[4,512,256]{2,1,0:T(8,128)(2,1)S(1)} %get-tuple-element.36.refs_0_.embeds, bf16[384,512]{1,0:T(8,128)(2,1)S(1)} %copy-done.24, f32[1,256]{1,0:T(1,128)S(1)} %bitcast.86, bf16[4,512,256]{2,1,0:T(8,128)(2,1)S(1)} %bitcast.63, ...), custom_call_target="tpu_custom_call" | custom-call | tf_op jit(solution)/shard_map/linear/pallas_call | solution.py:191
  58.1 1.6 copy-done.4
  59.7 3.6 %up_own.1.refs_2_ = f32[512,256]{1,0:T(8,128)S(1)} custom-call(s32[1]{0:T(128)} %bitcast.refs_0_._, bf16[512,256]{1,0:T(8,128)(2,1)S(1)} %get-tuple-element.35.refs_4_.refs_1_, bf16[4096,256]{1,0:T(8,128)(2,1)S(1)} %copy-done, bf16[4096,256]{1,0:T(8,128)(2,1)S(1)} %copy-done.1, f32[4,512,256]{2,1,0:T(8,128)S(1)} %copy-done.4), custom_call_target="tpu_custom_call" | custom-call | tf_op jit(solution)/shard_map/up_own/pallas_call | solution.py:290
  63.4 5.3 %up_other.1.ff = f32[512,256]{1,0:T(8,128)S(1)} custom-call(s32[1]{0:T(128)} %bitcast.refs_0_._, bf16[512,256]{1,0:T(8,128)(2,1)S(1)} %get-tuple-element.35.refs_4_.refs_1_, f32[512,256]{1,0:T(8,128)S(1)} %up_own.1.refs_2_, bf16[4096,256]{1,0:T(8,128)(2,1)} %collective-permute-done.refs_3_.refs_5_, bf16[4096,256]{1,0:T(8,128)(2,1)S(1)} %collective-permute-done.1.refs_4_.refs_6_), custom_call_target="tpu_custom_call" | custom-call | tf_op jit(solution)/shard_map/up_other/pallas_call | solution.py:290
  68.7 2.0 top.1
  71.4 13.3 %back.1.refs_0_ = f32[512,256]{1,0:T(8,128)} custom-call(s32[1]{0:T(128)} %bitcast.refs_0_._, bf16[512,256]{1,0:T(8,128)(2,1)} %copy-done.2, bf16[512,256]{1,0:T(8,128)(2,1)} %copy-done.10, bf16[4096,256]{1,0:T(8,128)(2,1)} %refs_3_.5, bf16[4096,256]{1,0:T(8,128)(2,1)} %refs_4_.1, bf16[4096,256]{1,0:T(8,128)(2,1)} %collective-permute-done.refs_3_.refs_5_, ...), custom_call_target="tpu_custom_call" | custom-call | tf_op jit(solution)/shard_map/back/pallas_call | solution.py:290
  84.7 1.2 copy-done.12
  85.9 5.3 %tail.1.refs_7_ = bf16[16,4,32,256]{3,2,1,0:T(8,128)(2,1)} custom-call(f32[512,256]{1,0:T(8,128)S(1)} %copy-done.12, f32[512,256]{1,0:T(8,128)S(1)} %copy-done.23, f32[1,256]{1,0:T(1,128)S(1)} %bitcast.89, bf16[4,256,256]{2,1,0:T(8,128)(2,1)S(1)} %copy-done.22, bf16[4,128,256]{2,1,0:T(8,128)(2,1)S(1)} %copy-done.25, ...), custom_call_target="tpu_custom_call" | custom-call | tf_op jit(solution)/shard_map/tail/pallas_call | solution.py:494
  91.3 6.2 %all-to-all-start.1 = ((bf16[64,32,256]{2,1,0:T(8,128)(2,1)}), bf16[64,32,256]{2,1,0:T(8,128)(2,1)S(1)}, u32[]{:S(2)}, u32[]{:S(2)}) async-start(bf16[64,32,256]{2,1,0:T(8,128)(2,1)} %bitcast.12), calls=%async_computation.1 | async-start | bytes 2097152 | tf_op jit(solution)/shard_map/all_to_all | solution.py:580
  97.5 8.2 %weights_1.1 = (bf16[8,256,256]{2,1,0:T(8,128)(2,1)}, bf16[8,256,256]{2,1,0:T(8,128)(2,1)}) custom-call(s32[1]{0:T(128)S(6)} %sub.4.refs_0_._, bf16[512,256]{1,0:T(8,128)(2,1)} %copy-done.2, bf16[512,256]{1,0:T(8,128)(2,1)} %copy-done.9, bf16[512,256]{1,0:T(8,128)(2,1)} %copy-done.10, bf16[512,256]{1,0:T(8,128)(2,1)} %copy-done.11, ...), custom_call_target="tpu_custom_call" | custom-call | tf_op jit(solution)/shard_map/weights_1/pallas_call | solution.py:372
  106.2 8.2 %weights_0.1 = (bf16[8,256,256]{2,1,0:T(8,128)(2,1)}, bf16[8,256,256]{2,1,0:T(8,128)(2,1)}) custom-call(s32[1]{0:T(128)} %bitcast.refs_0_._, bf16[512,256]{1,0:T(8,128)(2,1)} %copy-done.2, bf16[512,256]{1,0:T(8,128)(2,1)} %copy-done.9, bf16[512,256]{1,0:T(8,128)(2,1)} %copy-done.10, bf16[512,256]{1,0:T(8,128)(2,1)} %copy-done.11, ...), custom_call_target="tpu_custom_call" | custom-call | tf_op jit(solution)/shard_map/weights_0/pallas_call | solution.py:372
  114.4 1.0 copy-done.17
  115.3 1.2 copy-done.8
  116.6 1.2 copy-done.18
  117.8 1.0 down_split_emb_2.1
  118.8 1.2 collective-permute-start.5
  120.0 1.2 copy-done.16
  121.2 0.9 up_split_emb_1.1
  122.1 1.0 copy-done.14
  123.4 9.7 %collective-permute-done.5 = bf16[4,256,256]{2,1,0:T(8,128)(2,1)} collective-permute-done((bf16[4,256,256]{2,1,0:T(8,128)(2,1)}, bf16[4,256,256]{2,1,0:T(8,128)(2,1)}, u32[]{:S(2)}, u32[]{:S(2)}) %collective-permute-start.5) | collective-permute-done | bytes 524320 | tf_op jit(solution)/shard_map/ppermute | solution.py:541
  133.1 1.8 down_split_emb_1.1
  136.3 1.8 up_split_emb_2.1
  138.1 1.5 collective-permute-start.10
  139.6 3.4 %collective-permute-done.7 = bf16[2,256,256]{2,1,0:T(8,128)(2,1)S(1)} collective-permute-done((bf16[2,256,256]{2,1,0:T(8,128)(2,1)}, bf16[2,256,256]{2,1,0:T(8,128)(2,1)S(1)}, u32[]{:S(2)}, u32[]{:S(2)}) %collective-permute-start.7) | collective-permute-done | bytes 262176 | tf_op jit(solution)/shard_map/ppermute | solution.py:541
  143.0 1.7 collective-permute-start.9
  145.1 2.7 %collective-permute-start.12 = (bf16[1,256,256]{2,1,0:T(8,128)(2,1)S(1)}, bf16[1,256,256]{2,1,0:T(8,128)(2,1)S(1)}, u32[]{:S(2)}, u32[]{:S(2)}) collective-permute-start(bf16[1,256,256]{2,1,0:T(8,128)(2,1)S(1)} %get-tuple-element.60.refs_3_), channel_id=1, source_target_pairs={{0,16},{16,0},{1,17},{17,1},{2,18},{18,2},{3,19},{19,3},{4,20},{20... | collective-permute-start | bytes 393224 | tf_op jit(solution)/shard_map/ppermute | solution.py:541
  148.0 1.7 collective-permute-start.11
  149.6 5.6 %collective-permute-done.12 = bf16[1,256,256]{2,1,0:T(8,128)(2,1)S(1)} collective-permute-done((bf16[1,256,256]{2,1,0:T(8,128)(2,1)S(1)}, bf16[1,256,256]{2,1,0:T(8,128)(2,1)S(1)}, u32[]{:S(2)}, u32[]{:S(2)}) %collective-permute-start.12) | collective-permute-done | bytes 131104 | tf_op jit(solution)/shard_map/ppermute | solution.py:541
  155.3 3.2 %collective-permute-start.14 = (bf16[1,256,256]{2,1,0:T(8,128)(2,1)S(1)}, bf16[1,256,256]{2,1,0:T(8,128)(2,1)S(1)}, u32[]{:S(2)}, u32[]{:S(2)}) collective-permute-start(bf16[1,256,256]{2,1,0:T(8,128)(2,1)S(1)} %up_share.1.refs_3_.refs_1_), channel_id=1, source_target_pairs={{0,16},{16,0},{1,17},{17,1},{2,18},{18,2},{3,19},{19,3},{4,20},{20... | collective-permute-start | bytes 393224 | tf_op jit(solution)/shard_map/ppermute | solution.py:541
  158.5 8.0 %collective-permute-start.13 = (bf16[2,256,256]{2,1,0:T(8,128)(2,1)S(1)}, bf16[2,256,256]{2,1,0:T(8,128)(2,1)S(1)}, u32[]{:S(2)}, u32[]{:S(2)}) collective-permute-start(bf16[2,256,256]{2,1,0:T(8,128)(2,1)S(1)} %bitcast.67), channel_id=1, source_target_pairs={{0,8},{8,0},{1,9},{9,1},{2,10},{10,2},{3,11},{11,3},{4,12},{12,4},... | collective-permute-start | bytes 786440 | tf_op jit(solution)/shard_map/ppermute | solution.py:541
  166.5 1.6 collective-permute-start.16
  168.1 3.5 %collective-permute-done.13.refs_2_ = bf16[2,256,256]{2,1,0:T(8,128)(2,1)S(1)} collective-permute-done((bf16[2,256,256]{2,1,0:T(8,128)(2,1)S(1)}, bf16[2,256,256]{2,1,0:T(8,128)(2,1)S(1)}, u32[]{:S(2)}, u32[]{:S(2)}) %collective-permute-start.13) | collective-permute-done | bytes 262176 | tf_op jit(solution)/shard_map/ppermute | solution.py:541
  171.7 3.0 %collective-permute-start.15 = (bf16[4,256,256]{2,1,0:T(8,128)(2,1)S(1)}, bf16[4,256,256]{2,1,0:T(8,128)(2,1)S(1)}, u32[]{:S(2)}, u32[]{:S(2)}) collective-permute-start(bf16[4,256,256]{2,1,0:T(8,128)(2,1)S(1)} %bitcast.56), channel_id=1, source_target_pairs={{0,4},{4,0},{1,5},{5,1},{2,6},{6,2},{3,7},{7,3},{8,12},{12,8},{9,1... | collective-permute-start | bytes 1572872 | tf_op jit(solution)/shard_map/ppermute | solution.py:541
  174.8 1.6 collective-permute-start.18
  176.4 10.8 %collective-permute-done.15.refs_2_ = bf16[4,256,256]{2,1,0:T(8,128)(2,1)S(1)} collective-permute-done((bf16[4,256,256]{2,1,0:T(8,128)(2,1)S(1)}, bf16[4,256,256]{2,1,0:T(8,128)(2,1)S(1)}, u32[]{:S(2)}, u32[]{:S(2)}) %collective-permute-start.15) | collective-permute-done | bytes 524320 | tf_op jit(solution)/shard_map/ppermute | solution.py:541
  187.3 2.2 %collective-permute-start.17 = (bf16[8,256,256]{2,1,0:T(8,128)(2,1)S(1)}, bf16[8,256,256]{2,1,0:T(8,128)(2,1)S(1)}, u32[]{:S(2)}, u32[]{:S(2)}) collective-permute-start(bf16[8,256,256]{2,1,0:T(8,128)(2,1)S(1)} %bitcast.52), channel_id=1, source_target_pairs={{0,2},{2,0},{1,3},{3,1},{4,6},{6,4},{5,7},{7,5},{8,10},{10,8},{9,1... | collective-permute-start | bytes 3145736 | tf_op jit(solution)/shard_map/ppermute | solution.py:541
  189.7 2.4 %weights_mine.1 = (f32[8,2,256,256]{3,2,1,0:T(8,128)}, f32[8,2,256,256]{3,2,1,0:T(8,128)}) custom-call(s32[1]{0:T(128)} %bitcast.refs_0_._, bf16[8,256,256]{2,1,0:T(8,128)(2,1)S(1)} %bitcast.53, bf16[8,256,256]{2,1,0:T(8,128)(2,1)S(1)} %bitcast.62), custom_call_target="tpu_custom_call" | custom-call | tf_op jit(solution)/shard_map/weights_mine/pallas_call | solution.py:449
  192.1 1.2 collective-permute-done.19.refs_1_
  193.3 2.4 %weights_others.1 = (f32[8,2,256,256]{3,2,1,0:T(8,128)}, f32[8,2,256,256]{3,2,1,0:T(8,128)}) custom-call(s32[1]{0:T(128)S(6)} %sub.4.refs_0_._, bf16[8,256,256]{2,1,0:T(8,128)(2,1)S(1)} %collective-permute-done.17.refs_0_, bf16[8,256,256]{2,1,0:T(8,128)(2,1)S(1)} %collective-permute-done.19.refs_1_, ...), custom_call_target="tpu_custom_call", output_to_operand_aliasing={{0}: (3, {}), {1}: (4, {})} | custom-call | tf_op jit(solution)/shard_map/weights_others/pallas_call | solution.py:449
  195.7 1.0 copy.26
  (88 shorter events, 5.0 us)
Async XLA Ops:
  0.6 4.4 %copy-start.29 = (s32[1,64,32,4]{1,3,2,0:T(4,128)S(1)}, s32[1,64,32,4]{1,3,2,0:T(4,128)}, u32[]{:S(2)}) copy-start(s32[1,64,32,4]{1,3,2,0:T(4,128)} %param.13) | copy-start | bytes 98308
  0.6 4.8 %copy-start.30 = (s32[1,64,32]{1,2,0:T(8,128)S(1)}, s32[1,64,32]{1,2,0:T(8,128)}, u32[]{:S(2)}) copy-start(s32[1,64,32]{1,2,0:T(8,128)} %param.14) | copy-start | bytes 24580
  3.8 46.8 %collective-permute-start = (bf16[4096,256]{1,0:T(8,128)(2,1)}, bf16[4096,256]{1,0:T(8,128)(2,1)}, u32[]{:S(2)}, u32[]{:S(2)}) collective-permute-start(bf16[4096,256]{1,0:T(8,128)(2,1)} %broadcast_select_fusion), channel_id=1, source_target_pairs={{0,1},{1,0},{2,3},{3,2},{4,5},{5,4},{6,7},{7,6},{8,9},{9,8},{10,11... | collective-permute-start | bytes 6291464 | tf_op jit(solution)/shard_map/ppermute | solution.py:541
  5.8 3.4 %copy-start.3 = (bf16[32,512,256]{2,1,0:T(8,128)(2,1)S(1)}, bf16[32,512,256]{2,1,0:T(8,128)(2,1)}, u32[]{:S(2)}) copy-start(bf16[32,512,256]{2,1,0:T(8,128)(2,1)} %tables_ref.1) | copy-start | bytes 25165828
  13.1 32.3 %copy-start.13 = (bf16[512,256]{1,0:T(8,128)(2,1)S(1)}, bf16[512,256]{1,0:T(8,128)(2,1)}, u32[]{:S(2)}) copy-start(bf16[512,256]{1,0:T(8,128)(2,1)} %refs_7_.1) | copy-start | bytes 786436
  13.1 32.3 %copy-start.19 = (bf16[128,512]{1,0:T(8,128)(2,1)S(1)}, bf16[128,512]{1,0:T(8,128)(2,1)}, u32[]{:S(2)}) copy-start(bf16[128,512]{1,0:T(8,128)(2,1)} %refs_8_.1) | copy-start | bytes 393220
  13.1 32.3 %copy-start.26 = (s32[512]{0:T(512)S(1)}, s32[512]{0:T(512)}, u32[]{:S(2)}) copy-start(s32[512]{0:T(512)} %param.15) | copy-start | bytes 6148
  13.1 32.3 %copy-start.28 = (f32[256]{0:T(256)S(1)}, f32[256]{0:T(256)}, u32[]{:S(2)}) copy-start(f32[256]{0:T(256)} %param.19) | copy-start | bytes 3076
  13.2 40.2 %copy-start.7 = (bf16[1,4,512,256]{3,2,1,0:T(8,128)(2,1)S(1)}, bf16[1,4,512,256]{3,2,1,0:T(8,128)(2,1)}, u32[]{:S(2)}) copy-start(bf16[1,4,512,256]{3,2,1,0:T(8,128)(2,1)} %param.23) | copy-start | bytes 3145732
  13.2 40.2 %copy-start.24 = (bf16[384,512]{1,0:T(8,128)(2,1)S(1)}, bf16[384,512]{1,0:T(8,128)(2,1)}, u32[]{:S(2)}) copy-start(bf16[384,512]{1,0:T(8,128)(2,1)} %refs_1_.1) | copy-start | bytes 1179652
  13.2 40.2 %copy-start.27 = (f32[256]{0:T(256)S(1)}, f32[256]{0:T(256)}, u32[]{:S(2)}) copy-start(f32[256]{0:T(256)} %param.22) | copy-start | bytes 3076
  45.4 12.7 %copy-start = (bf16[4096,256]{1,0:T(8,128)(2,1)S(1)}, bf16[4096,256]{1,0:T(8,128)(2,1)}, u32[]{:S(2)}) copy-start(bf16[4096,256]{1,0:T(8,128)(2,1)} %refs_3_.5) | copy-start | bytes 6291460
  45.4 12.6 %copy-start.1 = (bf16[4096,256]{1,0:T(8,128)(2,1)S(1)}, bf16[4096,256]{1,0:T(8,128)(2,1)}, u32[]{:S(2)}) copy-start(bf16[4096,256]{1,0:T(8,128)(2,1)} %refs_4_.1) | copy-start | bytes 6291460
  50.2 13.1 %copy-start.2 = (bf16[512,256]{1,0:T(8,128)(2,1)}, bf16[512,256]{1,0:T(8,128)(2,1)S(1)}, u32[]{:S(2)}) copy-start(bf16[512,256]{1,0:T(8,128)(2,1)S(1)} %get-tuple-element.35.refs_4_.refs_1_) | copy-start | bytes 786436
  50.6 12.7 %collective-permute-start.1 = (bf16[4096,256]{1,0:T(8,128)(2,1)}, bf16[4096,256]{1,0:T(8,128)(2,1)S(1)}, u32[]{:S(2)}, u32[]{:S(2)}) collective-permute-start(bf16[4096,256]{1,0:T(8,128)(2,1)} %collective-permute-done.refs_3_.refs_5_), channel_id=1, source_target_pairs={{0,2},{2,0},{1,3},{3,1},{4,6},{6,4},{5,7},{7,5},{8,10},{10,8},{9,1... | collective-permute-start | bytes 6291464 | tf_op jit(solution)/shard_map/ppermute | solution.py:541
  52.2 32.5 %collective-permute-start.2 = (bf16[512,256]{1,0:T(8,128)(2,1)S(1)}, bf16[512,256]{1,0:T(8,128)(2,1)S(1)}, u32[]{:S(2)}, u32[]{:S(2)}) collective-permute-start(bf16[512,256]{1,0:T(8,128)(2,1)S(1)} %get-tuple-element.35.refs_4_.refs_1_), channel_id=1, source_target_pairs={{0,1},{1,0},{2,3},{3,2},{4,5},{5,4},{6,7},{7,6},{8,9},{9,8},{10,11... | collective-permute-start | bytes 786440 | tf_op jit(solution)/shard_map/ppermute | solution.py:541
  58.1 1.6 copy-start.4
  63.3 5.3 %copy-start.6 = (bf16[4096,256]{1,0:T(8,128)(2,1)}, bf16[4096,256]{1,0:T(8,128)(2,1)S(1)}, u32[]{:S(2)}) copy-start(bf16[4096,256]{1,0:T(8,128)(2,1)S(1)} %collective-permute-done.1.refs_4_.refs_6_) | copy-start | bytes 6291460
  70.6 14.0 %collective-permute-start.3 = (bf16[512,256]{1,0:T(8,128)(2,1)S(1)}, bf16[512,256]{1,0:T(8,128)(2,1)S(1)}, u32[]{:S(2)}, u32[]{:S(2)}) collective-permute-start(bf16[512,256]{1,0:T(8,128)(2,1)S(1)} %get-tuple-element.41.refs_2_.refs_3_), channel_id=1, source_target_pairs={{0,1},{1,0},{2,3},{3,2},{4,5},{5,4},{6,7},{7,6},{8,9},{9,8},{10,11... | collective-permute-start | bytes 786440 | tf_op jit(solution)/shard_map/ppermute | solution.py:541
  71.3 13.3 %copy-start.5 = (f32[4,512,256]{2,1,0:T(8,128)S(1)}, f32[4,512,256]{2,1,0:T(8,128)}, u32[]{:S(2)}) copy-start(f32[4,512,256]{2,1,0:T(8,128)} %get-tuple-element.37.refs_4_.refs_6_) | copy-start | bytes 6291460
  71.3 13.3 %copy-start.22 = (bf16[4,256,256]{2,1,0:T(8,128)(2,1)S(1)}, bf16[4,256,256]{2,1,0:T(8,128)(2,1)}, u32[]{:S(2)}) copy-start(bf16[4,256,256]{2,1,0:T(8,128)(2,1)} %get-tuple-element.43.refs_3_) | copy-start | bytes 1572868
  71.3 13.4 %copy-start.23 = (f32[512,256]{1,0:T(8,128)S(1)}, f32[512,256]{1,0:T(8,128)}, u32[]{:S(2)}) copy-start(f32[512,256]{1,0:T(8,128)} %get-tuple-element.42.refs_1_) | copy-start | bytes 1572868
  71.4 13.4 %copy-start.25 = (bf16[4,128,256]{2,1,0:T(8,128)(2,1)S(1)}, bf16[4,128,256]{2,1,0:T(8,128)(2,1)}, u32[]{:S(2)}) copy-start(bf16[4,128,256]{2,1,0:T(8,128)(2,1)} %get-tuple-element.44.refs_4_) | copy-start | bytes 786436
  84.7 6.6 %copy-start.9 = (bf16[512,256]{1,0:T(8,128)(2,1)}, bf16[512,256]{1,0:T(8,128)(2,1)S(1)}, u32[]{:S(2)}) copy-start(bf16[512,256]{1,0:T(8,128)(2,1)S(1)} %collective-permute-done.2.refs_10_.refs_2_) | copy-start | bytes 786436
  84.7 6.6 %copy-start.11 = (bf16[512,256]{1,0:T(8,128)(2,1)}, bf16[512,256]{1,0:T(8,128)(2,1)S(1)}, u32[]{:S(2)}) copy-start(bf16[512,256]{1,0:T(8,128)(2,1)S(1)} %collective-permute-done.3.refs_11_.refs_4_) | copy-start | bytes 786436
  84.7 1.2 copy-start.12
  91.3 41.9 %all-to-all-start.1 = ((bf16[64,32,256]{2,1,0:T(8,128)(2,1)}), bf16[64,32,256]{2,1,0:T(8,128)(2,1)S(1)}, u32[]{:S(2)}, u32[]{:S(2)}) async-start(bf16[64,32,256]{2,1,0:T(8,128)(2,1)} %bitcast.12), calls=%async_computation.1 | async-start | bytes 2097152 | tf_op jit(solution)/shard_map/all_to_all | solution.py:580
  105.7 8.7 %collective-permute-start.4 = (bf16[8,256,256]{2,1,0:T(8,128)(2,1)}, bf16[8,256,256]{2,1,0:T(8,128)(2,1)S(1)}, u32[]{:S(2)}, u32[]{:S(2)}) collective-permute-start(bf16[8,256,256]{2,1,0:T(8,128)(2,1)} %get-tuple-element.46.refs_7_), channel_id=1, source_target_pairs={{0,2},{2,0},{1,3},{3,1},{4,6},{6,4},{5,7},{7,5},{8,10},{10,8},{9,1... | collective-permute-start | bytes 3145736 | tf_op jit(solution)/shard_map/ppermute | solution.py:541
  106.0 13.9 %collective-permute-start.6 = (bf16[8,256,256]{2,1,0:T(8,128)(2,1)}, bf16[8,256,256]{2,1,0:T(8,128)(2,1)S(1)}, u32[]{:S(2)}, u32[]{:S(2)}) collective-permute-start(bf16[8,256,256]{2,1,0:T(8,128)(2,1)} %get-tuple-element.51), channel_id=1, source_target_pairs={{0,2},{2,0},{1,3},{3,1},{4,6},{6,4},{5,7},{7,5},{8,10},{10,8},{9,1... | collective-permute-start | bytes 3145736 | tf_op jit(solution)/shard_map/ppermute | solution.py:541
  115.3 1.2 copy-start.8
  116.6 1.2 copy-start.18
  118.8 14.3 %collective-permute-start.5 = (bf16[4,256,256]{2,1,0:T(8,128)(2,1)}, bf16[4,256,256]{2,1,0:T(8,128)(2,1)}, u32[]{:S(2)}, u32[]{:S(2)}) collective-permute-start(bf16[4,256,256]{2,1,0:T(8,128)(2,1)} %get-tuple-element.49.refs_3_), channel_id=1, source_target_pairs={{0,4},{4,0},{1,5},{5,1},{2,6},{6,2},{3,7},{7,3},{8,12},{12,8},{9,1... | collective-permute-start | bytes 1572872 | tf_op jit(solution)/shard_map/ppermute | solution.py:541
  120.0 1.2 copy-start.16
  123.1 13.2 %copy-start.15 = (f32[2,512,256]{2,1,0:T(8,128)S(1)}, f32[2,512,256]{2,1,0:T(8,128)}, u32[]{:S(2)}) copy-start(f32[2,512,256]{2,1,0:T(8,128)} %copy-done.14) | copy-start | bytes 3145732
  123.1 13.1 %collective-permute-start.8 = (bf16[2,512,256]{2,1,0:T(8,128)(2,1)}, bf16[2,512,256]{2,1,0:T(8,128)(2,1)}, u32[]{:S(2)}, u32[]{:S(2)}) collective-permute-start(bf16[2,512,256]{2,1,0:T(8,128)(2,1)} %get-tuple-element.52.refs_3_), channel_id=1, source_target_pairs={{0,8},{8,0},{1,9},{9,1},{2,10},{10,2},{3,11},{11,3},{4,12},{12,4},... | collective-permute-start | bytes 1572872 | tf_op jit(solution)/shard_map/ppermute | solution.py:541
  135.7 7.3 %copy-start.21 = (f32[2,256,256]{2,1,0:T(8,128)S(1)}, f32[2,256,256]{2,1,0:T(8,128)}, u32[]{:S(2)}) copy-start(f32[2,256,256]{2,1,0:T(8,128)} %copy-done.20) | copy-start | bytes 1572868
  135.7 7.3 %collective-permute-start.7 = (bf16[2,256,256]{2,1,0:T(8,128)(2,1)}, bf16[2,256,256]{2,1,0:T(8,128)(2,1)S(1)}, u32[]{:S(2)}, u32[]{:S(2)}) collective-permute-start(bf16[2,256,256]{2,1,0:T(8,128)(2,1)} %get-tuple-element.54.refs_3_), channel_id=1, source_target_pairs={{0,8},{8,0},{1,9},{9,1},{2,10},{10,2},{3,11},{11,3},{4,12},{12,4},... | collective-permute-start | bytes 786440 | tf_op jit(solution)/shard_map/ppermute | solution.py:541
  138.1 7.0 %collective-permute-start.10 = (bf16[2,256,256]{2,1,0:T(8,128)(2,1)}, bf16[2,256,256]{2,1,0:T(8,128)(2,1)S(1)}, u32[]{:S(2)}, u32[]{:S(2)}) collective-permute-start(bf16[2,256,256]{2,1,0:T(8,128)(2,1)} %get-tuple-element.56.refs_3_), channel_id=1, source_target_pairs={{0,4},{4,0},{1,5},{5,1},{2,6},{6,2},{3,7},{7,3},{8,12},{12,8},{9,1... | collective-permute-start | bytes 786440 | tf_op jit(solution)/shard_map/ppermute | solution.py:541
  143.0 4.9 %collective-permute-start.9 = (bf16[1,256,256]{2,1,0:T(8,128)(2,1)S(1)}, bf16[1,256,256]{2,1,0:T(8,128)(2,1)S(1)}, u32[]{:S(2)}, u32[]{:S(2)}) collective-permute-start(bf16[1,256,256]{2,1,0:T(8,128)(2,1)S(1)} %get-tuple-element.58.refs_3_), channel_id=1, source_target_pairs={{0,16},{16,0},{1,17},{17,1},{2,18},{18,2},{3,19},{19,3},{4,20},{20... | collective-permute-start | bytes 393224 | tf_op jit(solution)/shard_map/ppermute | solution.py:541
  145.1 10.2 %collective-permute-start.12 = (bf16[1,256,256]{2,1,0:T(8,128)(2,1)S(1)}, bf16[1,256,256]{2,1,0:T(8,128)(2,1)S(1)}, u32[]{:S(2)}, u32[]{:S(2)}) collective-permute-start(bf16[1,256,256]{2,1,0:T(8,128)(2,1)S(1)} %get-tuple-element.60.refs_3_), channel_id=1, source_target_pairs={{0,16},{16,0},{1,17},{17,1},{2,18},{18,2},{3,19},{19,3},{4,20},{20... | collective-permute-start | bytes 393224 | tf_op jit(solution)/shard_map/ppermute | solution.py:541
  148.0 10.5 %collective-permute-start.11 = (bf16[1,256,256]{2,1,0:T(8,128)(2,1)S(1)}, bf16[1,256,256]{2,1,0:T(8,128)(2,1)S(1)}, u32[]{:S(2)}, u32[]{:S(2)}) collective-permute-start(bf16[1,256,256]{2,1,0:T(8,128)(2,1)S(1)} %down_share.1.refs_3_.refs_1_), channel_id=1, source_target_pairs={{0,16},{16,0},{1,17},{17,1},{2,18},{18,2},{3,19},{19,3},{4,20},{20... | collective-permute-start | bytes 393224 | tf_op jit(solution)/shard_map/ppermute | solution.py:541
  155.3 11.2 %collective-permute-start.14 = (bf16[1,256,256]{2,1,0:T(8,128)(2,1)S(1)}, bf16[1,256,256]{2,1,0:T(8,128)(2,1)S(1)}, u32[]{:S(2)}, u32[]{:S(2)}) collective-permute-start(bf16[1,256,256]{2,1,0:T(8,128)(2,1)S(1)} %up_share.1.refs_3_.refs_1_), channel_id=1, source_target_pairs={{0,16},{16,0},{1,17},{17,1},{2,18},{18,2},{3,19},{19,3},{4,20},{20... | collective-permute-start | bytes 393224 | tf_op jit(solution)/shard_map/ppermute | solution.py:541
  158.5 13.2 %collective-permute-start.13 = (bf16[2,256,256]{2,1,0:T(8,128)(2,1)S(1)}, bf16[2,256,256]{2,1,0:T(8,128)(2,1)S(1)}, u32[]{:S(2)}, u32[]{:S(2)}) collective-permute-start(bf16[2,256,256]{2,1,0:T(8,128)(2,1)S(1)} %bitcast.67), channel_id=1, source_target_pairs={{0,8},{8,0},{1,9},{9,1},{2,10},{10,2},{3,11},{11,3},{4,12},{12,4},... | collective-permute-start | bytes 786440 | tf_op jit(solution)/shard_map/ppermute | solution.py:541
  166.5 8.2 %collective-permute-start.16 = (bf16[2,256,256]{2,1,0:T(8,128)(2,1)S(1)}, bf16[2,256,256]{2,1,0:T(8,128)(2,1)S(1)}, u32[]{:S(2)}, u32[]{:S(2)}) collective-permute-start(bf16[2,256,256]{2,1,0:T(8,128)(2,1)S(1)} %bitcast.69), channel_id=1, source_target_pairs={{0,4},{4,0},{1,5},{5,1},{2,6},{6,2},{3,7},{7,3},{8,12},{12,8},{9,1... | collective-permute-start | bytes 786440 | tf_op jit(solution)/shard_map/ppermute | solution.py:541
  171.7 15.5 %collective-permute-start.15 = (bf16[4,256,256]{2,1,0:T(8,128)(2,1)S(1)}, bf16[4,256,256]{2,1,0:T(8,128)(2,1)S(1)}, u32[]{:S(2)}, u32[]{:S(2)}) collective-permute-start(bf16[4,256,256]{2,1,0:T(8,128)(2,1)S(1)} %bitcast.56), channel_id=1, source_target_pairs={{0,4},{4,0},{1,5},{5,1},{2,6},{6,2},{3,7},{7,3},{8,12},{12,8},{9,1... | collective-permute-start | bytes 1572872 | tf_op jit(solution)/shard_map/ppermute | solution.py:541
  174.8 14.7 %collective-permute-start.18 = (bf16[2,512,256]{2,1,0:T(8,128)(2,1)S(1)}, bf16[2,512,256]{2,1,0:T(8,128)(2,1)S(1)}, u32[]{:S(2)}, u32[]{:S(2)}) collective-permute-start(bf16[2,512,256]{2,1,0:T(8,128)(2,1)S(1)} %bitcast.58), channel_id=1, source_target_pairs={{0,8},{8,0},{1,9},{9,1},{2,10},{10,2},{3,11},{11,3},{4,12},{12,4},... | collective-permute-start | bytes 1572872 | tf_op jit(solution)/shard_map/ppermute | solution.py:541
  187.3 4.8 %collective-permute-start.17 = (bf16[8,256,256]{2,1,0:T(8,128)(2,1)S(1)}, bf16[8,256,256]{2,1,0:T(8,128)(2,1)S(1)}, u32[]{:S(2)}, u32[]{:S(2)}) collective-permute-start(bf16[8,256,256]{2,1,0:T(8,128)(2,1)S(1)} %bitcast.52), channel_id=1, source_target_pairs={{0,2},{2,0},{1,3},{3,1},{4,6},{6,4},{5,7},{7,5},{8,10},{10,8},{9,1... | collective-permute-start | bytes 3145736 | tf_op jit(solution)/shard_map/ppermute | solution.py:541
  189.6 3.7 %collective-permute-start.19 = (bf16[8,256,256]{2,1,0:T(8,128)(2,1)S(1)}, bf16[8,256,256]{2,1,0:T(8,128)(2,1)S(1)}, u32[]{:S(2)}, u32[]{:S(2)}) collective-permute-start(bf16[8,256,256]{2,1,0:T(8,128)(2,1)S(1)} %bitcast.61), channel_id=1, source_target_pairs={{0,2},{2,0},{1,3},{3,1},{4,6},{6,4},{5,7},{7,5},{8,10},{10,8},{9,1... | collective-permute-start | bytes 3145736 | tf_op jit(solution)/shard_map/ppermute | solution.py:541
  (4 other events, 3.4 us)

commit v5 on v4

--- a/solution.py
+++ b/solution.py
@@ -445,7 +445,7 @@
 def join_last(at, pieces, filled, name):
     before, units, width = pieces[0].shape
     count = len(pieces)
-    step = max(1, before // 4)
+    step = max(1, before // 2)
     return pl.pallas_call(
         functools.partial(join_last_kernel, count),
         grid_spec=pltpu.PrefetchScalarGridSpec(

time: 199 us -> 198 us (level)
  no operation moved by 1% of the time
where the time goes in v5:
time: 198 us; the launch traced here: 196 us
  Pallas kernels  69.6 us (35%)
  starting transfers between devices  39.8 us (20%)
  waiting for transfers between devices  35.9 us (18%)
  blocking collectives  32.2 us (16%)
  local copies, waits for them, and re-layouts  14.4 us (7%)
  other arithmetic  3.49 us (2%)
    ppermute x20, waiting for transfers between devices, turn(): lax.ppermute(value, axis, [(i, (i + shift) % size) for i in range(size)])  35.9 us
    ppermute x20, starting transfers between devices, turn(): lax.ppermute(value, axis, [(i, (i + shift) % size) for i in range(size)])  33.5 us
    all_to_all x1, blocking collectives, exchange(): moved = lax.all_to_all(flat, emb, split_axis=0, concat_axis=0, tiled=True)  32.2 us
    pallas_call x3, Pallas kernels, mlp(): pl.pallas_call(ordered(functools.partial(kernel, steps, int(own), len(beg...  22.2 us
    pallas_call x2, Pallas kernels, weight_grads(): pl.pallas_call(ordered(functools.partial(weight_kernel, blocks), 1 + 2 *...  16.4 us
    unnamed x64, local copies, waits for them, and re-layouts  14.3 us
    all_to_all x1, starting transfers between devices, exchange(): moved = lax.all_to_all(flat, emb, split_axis=0, concat_axis=0, tiled=True)  6.23 us
    pallas_call x8, Pallas kernels, split_sum(): whole(ordered(functools.partial(split_kernel, count, each), 1 + sum(each)...  5.69 us
  transfers between devices with their start and end apart: 21, of which 10 were waited for; matrix products, arithmetic and copies ran while one was open for 0% of the time, Pallas kernels for 32%

profile of v5, /device:TPU:9, one launch (start us, length us, event | category | flops | bytes accessed | tf_op | source)
XLA Modules:
  0.0 196.4 jit_solution(233563525447716070)
XLA Ops:
  0.7 3.2 %broadcast_select_fusion = bf16[4096,256]{1,0:T(8,128)(2,1)} fusion(bf16[4096,256]{1,0:T(8,128)(2,1)} %refs_3_.5, bf16[4096,256]{1,0:T(8,128)(2,1)} %refs_4_.1, pred[]{:T(512)S(6)} %eq.3), kind=kLoop, calls=%fused_computation | loop fusion | flops 1048576 | bytes 6291457 | tf_op jit(solution)/shard_map/select_n | solution.py:583
  3.8 1.2 collective-permute-start
  5.8 3.4 %copy-done.3 = bf16[32,512,256]{2,1,0:T(8,128)(2,1)S(1)} copy-done((bf16[32,512,256]{2,1,0:T(8,128)(2,1)S(1)}, bf16[32,512,256]{2,1,0:T(8,128)(2,1)}, u32[]{:S(2)}) %copy-start.3) | copy-done | bytes 8388632
  9.2 3.9 %pool.1 = bf16[16,4,32,256]{3,2,1,0:T(8,128)(2,1)S(1)} custom-call(s32[32,64,4]{2,1,0:T(8,128)S(1)} %fusion.ids_ref, bf16[32,512,256]{2,1,0:T(8,128)(2,1)S(1)} %copy-done.3), custom_call_target="tpu_custom_call" | custom-call | tf_op jit(solution)/shard_map/pool/pallas_call | solution.py:89
  13.2 32.2 %all_to_all.10 = bf16[64,32,256]{2,1,0:T(8,128)(2,1)S(1)} all-to-all(bf16[64,32,256]{2,1,0:T(8,128)(2,1)S(1)} %bitcast.60), channel_id=1, replica_groups=mesh['emb_0'=2,'emb_1'=2,'emb_2'=2,'emb_3'=2,'wide'=2] {'emb_0','emb_1',..., dimensions={0} | all-to-all | bytes 2097152 | tf_op jit(solution)/shard_map/all_to_all | solution.py:580
  45.5 4.8 %front.1 = (bf16[4,512,256]{2,1,0:T(8,128)(2,1)S(1)}, bf16[4,256,256]{2,1,0:T(8,128)(2,1)}, bf16[4,128,256]{2,1,0:T(8,128)(2,1)}, f32[512,256]{1,0:T(8,128)}, bf16[512,256]{1,0:T(8,128)(2,1)S(1)}) custom-call(bf16[16,4,32,256]{3,2,1,0:T(8,128)(2,1)S(1)} %bitcast.66, s32[1,512]{1,0:T(1,128)S(1)} %bitcast.84, bf16[512,256]{1,0:T(8,128)(2,1)S(1)} %copy-done.13, ...), custom_call_target="tpu_custom_call" | custom-call | tf_op jit(solution)/shard_map/front/pallas_call | solution.py:142
  50.6 1.6 collective-permute-start.1
  52.2 1.2 collective-permute-start.2
  53.4 4.7 %linear.1 = (bf16[4,512,256]{2,1,0:T(8,128)(2,1)}, f32[4,512,256]{2,1,0:T(8,128)}) custom-call(bf16[4,512,256]{2,1,0:T(8,128)(2,1)S(1)} %get-tuple-element.36.refs_0_.embeds, bf16[384,512]{1,0:T(8,128)(2,1)S(1)} %copy-done.24, f32[1,256]{1,0:T(1,128)S(1)} %bitcast.86, bf16[4,512,256]{2,1,0:T(8,128)(2,1)S(1)} %bitcast.63, ...), custom_call_target="tpu_custom_call" | custom-call | tf_op jit(solution)/shard_map/linear/pallas_call | solution.py:191
  58.1 1.6 copy-done.4
  59.7 3.6 %up_own.1.refs_2_ = f32[512,256]{1,0:T(8,128)S(1)} custom-call(s32[1]{0:T(128)} %bitcast.refs_0_._, bf16[512,256]{1,0:T(8,128)(2,1)S(1)} %get-tuple-element.35.refs_4_.refs_1_, bf16[4096,256]{1,0:T(8,128)(2,1)S(1)} %copy-done, bf16[4096,256]{1,0:T(8,128)(2,1)S(1)} %copy-done.1, f32[4,512,256]{2,1,0:T(8,128)S(1)} %copy-done.4), custom_call_target="tpu_custom_call" | custom-call | tf_op jit(solution)/shard_map/up_own/pallas_call | solution.py:290
  63.4 5.3 %up_other.1.ff = f32[512,256]{1,0:T(8,128)S(1)} custom-call(s32[1]{0:T(128)} %bitcast.refs_0_._, bf16[512,256]{1,0:T(8,128)(2,1)S(1)} %get-tuple-element.35.refs_4_.refs_1_, f32[512,256]{1,0:T(8,128)S(1)} %up_own.1.refs_2_, bf16[4096,256]{1,0:T(8,128)(2,1)} %collective-permute-done.refs_3_.refs_5_, bf16[4096,256]{1,0:T(8,128)(2,1)S(1)} %collective-permute-done.1.refs_4_.refs_6_), custom_call_target="tpu_custom_call" | custom-call | tf_op jit(solution)/shard_map/up_other/pallas_call | solution.py:290
  68.7 2.0 top.1
  71.4 13.3 %back.1.refs_0_ = f32[512,256]{1,0:T(8,128)} custom-call(s32[1]{0:T(128)} %bitcast.refs_0_._, bf16[512,256]{1,0:T(8,128)(2,1)} %copy-done.2, bf16[512,256]{1,0:T(8,128)(2,1)} %copy-done.10, bf16[4096,256]{1,0:T(8,128)(2,1)} %refs_3_.5, bf16[4096,256]{1,0:T(8,128)(2,1)} %refs_4_.1, bf16[4096,256]{1,0:T(8,128)(2,1)} %collective-permute-done.refs_3_.refs_5_, ...), custom_call_target="tpu_custom_call" | custom-call | tf_op jit(solution)/shard_map/back/pallas_call | solution.py:290
  84.7 1.2 copy-done.12
  85.9 5.3 %tail.1.refs_7_ = bf16[16,4,32,256]{3,2,1,0:T(8,128)(2,1)} custom-call(f32[512,256]{1,0:T(8,128)S(1)} %copy-done.12, f32[512,256]{1,0:T(8,128)S(1)} %copy-done.23, f32[1,256]{1,0:T(1,128)S(1)} %bitcast.89, bf16[4,256,256]{2,1,0:T(8,128)(2,1)S(1)} %copy-done.22, bf16[4,128,256]{2,1,0:T(8,128)(2,1)S(1)} %copy-done.25, ...), custom_call_target="tpu_custom_call" | custom-call | tf_op jit(solution)/shard_map/tail/pallas_call | solution.py:494
  91.3 6.2 %all-to-all-start.1 = ((bf16[64,32,256]{2,1,0:T(8,128)(2,1)}), bf16[64,32,256]{2,1,0:T(8,128)(2,1)S(1)}, u32[]{:S(2)}, u32[]{:S(2)}) async-start(bf16[64,32,256]{2,1,0:T(8,128)(2,1)} %bitcast.12), calls=%async_computation.1 | async-start | bytes 2097152 | tf_op jit(solution)/shard_map/all_to_all | solution.py:580
  97.5 8.2 %weights_1.1 = (bf16[8,256,256]{2,1,0:T(8,128)(2,1)}, bf16[8,256,256]{2,1,0:T(8,128)(2,1)}) custom-call(s32[1]{0:T(128)S(6)} %sub.4.refs_0_._, bf16[512,256]{1,0:T(8,128)(2,1)} %copy-done.2, bf16[512,256]{1,0:T(8,128)(2,1)} %copy-done.9, bf16[512,256]{1,0:T(8,128)(2,1)} %copy-done.10, bf16[512,256]{1,0:T(8,128)(2,1)} %copy-done.11, ...), custom_call_target="tpu_custom_call" | custom-call | tf_op jit(solution)/shard_map/weights_1/pallas_call | solution.py:372
  106.2 8.2 %weights_0.1 = (bf16[8,256,256]{2,1,0:T(8,128)(2,1)}, bf16[8,256,256]{2,1,0:T(8,128)(2,1)}) custom-call(s32[1]{0:T(128)} %bitcast.refs_0_._, bf16[512,256]{1,0:T(8,128)(2,1)} %copy-done.2, bf16[512,256]{1,0:T(8,128)(2,1)} %copy-done.9, bf16[512,256]{1,0:T(8,128)(2,1)} %copy-done.10, bf16[512,256]{1,0:T(8,128)(2,1)} %copy-done.11, ...), custom_call_target="tpu_custom_call" | custom-call | tf_op jit(solution)/shard_map/weights_0/pallas_call | solution.py:372
  114.4 1.0 copy-done.17
  115.3 1.2 copy-done.8
  116.6 1.2 copy-done.18
  117.8 1.0 down_split_emb_2.1
  118.8 1.2 collective-permute-start.5
  120.0 1.2 copy-done.16
  121.2 0.9 up_split_emb_1.1
  122.1 1.0 copy-done.14
  123.4 9.7 %collective-permute-done.5 = bf16[4,256,256]{2,1,0:T(8,128)(2,1)} collective-permute-done((bf16[4,256,256]{2,1,0:T(8,128)(2,1)}, bf16[4,256,256]{2,1,0:T(8,128)(2,1)}, u32[]{:S(2)}, u32[]{:S(2)}) %collective-permute-start.5) | collective-permute-done | bytes 524320 | tf_op jit(solution)/shard_map/ppermute | solution.py:541
  133.1 1.8 down_split_emb_1.1
  136.3 1.8 up_split_emb_2.1
  138.1 1.5 collective-permute-start.10
  139.6 3.4 %collective-permute-done.7 = bf16[2,256,256]{2,1,0:T(8,128)(2,1)S(1)} collective-permute-done((bf16[2,256,256]{2,1,0:T(8,128)(2,1)}, bf16[2,256,256]{2,1,0:T(8,128)(2,1)S(1)}, u32[]{:S(2)}, u32[]{:S(2)}) %collective-permute-start.7) | collective-permute-done | bytes 262176 | tf_op jit(solution)/shard_map/ppermute | solution.py:541
  143.0 1.7 collective-permute-start.9
  145.1 2.7 %collective-permute-start.12 = (bf16[1,256,256]{2,1,0:T(8,128)(2,1)S(1)}, bf16[1,256,256]{2,1,0:T(8,128)(2,1)S(1)}, u32[]{:S(2)}, u32[]{:S(2)}) collective-permute-start(bf16[1,256,256]{2,1,0:T(8,128)(2,1)S(1)} %get-tuple-element.60.refs_3_), channel_id=1, source_target_pairs={{0,16},{16,0},{1,17},{17,1},{2,18},{18,2},{3,19},{19,3},{4,20},{20... | collective-permute-start | bytes 393224 | tf_op jit(solution)/shard_map/ppermute | solution.py:541
  148.0 1.7 collective-permute-start.11
  149.6 5.6 %collective-permute-done.12 = bf16[1,256,256]{2,1,0:T(8,128)(2,1)S(1)} collective-permute-done((bf16[1,256,256]{2,1,0:T(8,128)(2,1)S(1)}, bf16[1,256,256]{2,1,0:T(8,128)(2,1)S(1)}, u32[]{:S(2)}, u32[]{:S(2)}) %collective-permute-start.12) | collective-permute-done | bytes 131104 | tf_op jit(solution)/shard_map/ppermute | solution.py:541
  155.3 3.2 %collective-permute-start.14 = (bf16[1,256,256]{2,1,0:T(8,128)(2,1)S(1)}, bf16[1,256,256]{2,1,0:T(8,128)(2,1)S(1)}, u32[]{:S(2)}, u32[]{:S(2)}) collective-permute-start(bf16[1,256,256]{2,1,0:T(8,128)(2,1)S(1)} %up_share.1.refs_3_.refs_1_), channel_id=1, source_target_pairs={{0,16},{16,0},{1,17},{17,1},{2,18},{18,2},{3,19},{19,3},{4,20},{20... | collective-permute-start | bytes 393224 | tf_op jit(solution)/shard_map/ppermute | solution.py:541
  158.5 8.0 %collective-permute-start.13 = (bf16[2,256,256]{2,1,0:T(8,128)(2,1)S(1)}, bf16[2,256,256]{2,1,0:T(8,128)(2,1)S(1)}, u32[]{:S(2)}, u32[]{:S(2)}) collective-permute-start(bf16[2,256,256]{2,1,0:T(8,128)(2,1)S(1)} %bitcast.67), channel_id=1, source_target_pairs={{0,8},{8,0},{1,9},{9,1},{2,10},{10,2},{3,11},{11,3},{4,12},{12,4},... | collective-permute-start | bytes 786440 | tf_op jit(solution)/shard_map/ppermute | solution.py:541
  166.5 1.6 collective-permute-start.16
  168.1 3.5 %collective-permute-done.13.refs_2_ = bf16[2,256,256]{2,1,0:T(8,128)(2,1)S(1)} collective-permute-done((bf16[2,256,256]{2,1,0:T(8,128)(2,1)S(1)}, bf16[2,256,256]{2,1,0:T(8,128)(2,1)S(1)}, u32[]{:S(2)}, u32[]{:S(2)}) %collective-permute-start.13) | collective-permute-done | bytes 262176 | tf_op jit(solution)/shard_map/ppermute | solution.py:541
  171.7 3.0 %collective-permute-start.15 = (bf16[4,256,256]{2,1,0:T(8,128)(2,1)S(1)}, bf16[4,256,256]{2,1,0:T(8,128)(2,1)S(1)}, u32[]{:S(2)}, u32[]{:S(2)}) collective-permute-start(bf16[4,256,256]{2,1,0:T(8,128)(2,1)S(1)} %bitcast.56), channel_id=1, source_target_pairs={{0,4},{4,0},{1,5},{5,1},{2,6},{6,2},{3,7},{7,3},{8,12},{12,8},{9,1... | collective-permute-start | bytes 1572872 | tf_op jit(solution)/shard_map/ppermute | solution.py:541
  174.8 1.6 collective-permute-start.18
  176.4 10.8 %collective-permute-done.15.refs_2_ = bf16[4,256,256]{2,1,0:T(8,128)(2,1)S(1)} collective-permute-done((bf16[4,256,256]{2,1,0:T(8,128)(2,1)S(1)}, bf16[4,256,256]{2,1,0:T(8,128)(2,1)S(1)}, u32[]{:S(2)}, u32[]{:S(2)}) %collective-permute-start.15) | collective-permute-done | bytes 524320 | tf_op jit(solution)/shard_map/ppermute | solution.py:541
  187.3 2.2 %collective-permute-start.17 = (bf16[8,256,256]{2,1,0:T(8,128)(2,1)S(1)}, bf16[8,256,256]{2,1,0:T(8,128)(2,1)S(1)}, u32[]{:S(2)}, u32[]{:S(2)}) collective-permute-start(bf16[8,256,256]{2,1,0:T(8,128)(2,1)S(1)} %bitcast.52), channel_id=1, source_target_pairs={{0,2},{2,0},{1,3},{3,1},{4,6},{6,4},{5,7},{7,5},{8,10},{10,8},{9,1... | collective-permute-start | bytes 3145736 | tf_op jit(solution)/shard_map/ppermute | solution.py:541
  189.7 2.2 %weights_mine.1 = (f32[8,2,256,256]{3,2,1,0:T(8,128)}, f32[8,2,256,256]{3,2,1,0:T(8,128)}) custom-call(s32[1]{0:T(128)} %bitcast.refs_0_._, bf16[8,256,256]{2,1,0:T(8,128)(2,1)S(1)} %bitcast.53, bf16[8,256,256]{2,1,0:T(8,128)(2,1)S(1)} %bitcast.62), custom_call_target="tpu_custom_call" | custom-call | tf_op jit(solution)/shard_map/weights_mine/pallas_call | solution.py:449
  191.9 1.4 collective-permute-done.19.refs_1_
  193.3 2.1 %weights_others.1 = (f32[8,2,256,256]{3,2,1,0:T(8,128)}, f32[8,2,256,256]{3,2,1,0:T(8,128)}) custom-call(s32[1]{0:T(128)S(6)} %sub.4.refs_0_._, bf16[8,256,256]{2,1,0:T(8,128)(2,1)S(1)} %collective-permute-done.17.refs_0_, bf16[8,256,256]{2,1,0:T(8,128)(2,1)S(1)} %collective-permute-done.19.refs_1_, ...), custom_call_target="tpu_custom_call", output_to_operand_aliasing={{0}: (3, {}), {1}: (4, {})} | custom-call | tf_op jit(solution)/shard_map/weights_others/pallas_call | solution.py:449
  195.4 1.0 copy.26
  (88 shorter events, 5.0 us)
Async XLA Ops:
  0.6 4.4 %copy-start.29 = (s32[1,64,32,4]{1,3,2,0:T(4,128)S(1)}, s32[1,64,32,4]{1,3,2,0:T(4,128)}, u32[]{:S(2)}) copy-start(s32[1,64,32,4]{1,3,2,0:T(4,128)} %param.13) | copy-start | bytes 98308
  0.6 4.8 %copy-start.30 = (s32[1,64,32]{1,2,0:T(8,128)S(1)}, s32[1,64,32]{1,2,0:T(8,128)}, u32[]{:S(2)}) copy-start(s32[1,64,32]{1,2,0:T(8,128)} %param.14) | copy-start | bytes 24580
  3.8 46.8 %collective-permute-start = (bf16[4096,256]{1,0:T(8,128)(2,1)}, bf16[4096,256]{1,0:T(8,128)(2,1)}, u32[]{:S(2)}, u32[]{:S(2)}) collective-permute-start(bf16[4096,256]{1,0:T(8,128)(2,1)} %broadcast_select_fusion), channel_id=1, source_target_pairs={{0,1},{1,0},{2,3},{3,2},{4,5},{5,4},{6,7},{7,6},{8,9},{9,8},{10,11... | collective-permute-start | bytes 6291464 | tf_op jit(solution)/shard_map/ppermute | solution.py:541
  5.8 3.4 %copy-start.3 = (bf16[32,512,256]{2,1,0:T(8,128)(2,1)S(1)}, bf16[32,512,256]{2,1,0:T(8,128)(2,1)}, u32[]{:S(2)}) copy-start(bf16[32,512,256]{2,1,0:T(8,128)(2,1)} %tables_ref.1) | copy-start | bytes 25165828
  13.1 32.3 %copy-start.13 = (bf16[512,256]{1,0:T(8,128)(2,1)S(1)}, bf16[512,256]{1,0:T(8,128)(2,1)}, u32[]{:S(2)}) copy-start(bf16[512,256]{1,0:T(8,128)(2,1)} %refs_7_.1) | copy-start | bytes 786436
  13.1 32.3 %copy-start.19 = (bf16[128,512]{1,0:T(8,128)(2,1)S(1)}, bf16[128,512]{1,0:T(8,128)(2,1)}, u32[]{:S(2)}) copy-start(bf16[128,512]{1,0:T(8,128)(2,1)} %refs_8_.1) | copy-start | bytes 393220
  13.1 32.3 %copy-start.26 = (s32[512]{0:T(512)S(1)}, s32[512]{0:T(512)}, u32[]{:S(2)}) copy-start(s32[512]{0:T(512)} %param.15) | copy-start | bytes 6148
  13.1 32.3 %copy-start.28 = (f32[256]{0:T(256)S(1)}, f32[256]{0:T(256)}, u32[]{:S(2)}) copy-start(f32[256]{0:T(256)} %param.19) | copy-start | bytes 3076
  13.2 40.2 %copy-start.7 = (bf16[1,4,512,256]{3,2,1,0:T(8,128)(2,1)S(1)}, bf16[1,4,512,256]{3,2,1,0:T(8,128)(2,1)}, u32[]{:S(2)}) copy-start(bf16[1,4,512,256]{3,2,1,0:T(8,128)(2,1)} %param.23) | copy-start | bytes 3145732
  13.2 40.2 %copy-start.24 = (bf16[384,512]{1,0:T(8,128)(2,1)S(1)}, bf16[384,512]{1,0:T(8,128)(2,1)}, u32[]{:S(2)}) copy-start(bf16[384,512]{1,0:T(8,128)(2,1)} %refs_1_.1) | copy-start | bytes 1179652
  13.2 40.2 %copy-start.27 = (f32[256]{0:T(256)S(1)}, f32[256]{0:T(256)}, u32[]{:S(2)}) copy-start(f32[256]{0:T(256)} %param.22) | copy-start | bytes 3076
  45.4 12.7 %copy-start = (bf16[4096,256]{1,0:T(8,128)(2,1)S(1)}, bf16[4096,256]{1,0:T(8,128)(2,1)}, u32[]{:S(2)}) copy-start(bf16[4096,256]{1,0:T(8,128)(2,1)} %refs_3_.5) | copy-start | bytes 6291460
  45.4 12.6 %copy-start.1 = (bf16[4096,256]{1,0:T(8,128)(2,1)S(1)}, bf16[4096,256]{1,0:T(8,128)(2,1)}, u32[]{:S(2)}) copy-start(bf16[4096,256]{1,0:T(8,128)(2,1)} %refs_4_.1) | copy-start | bytes 6291460
  50.2 13.1 %copy-start.2 = (bf16[512,256]{1,0:T(8,128)(2,1)}, bf16[512,256]{1,0:T(8,128)(2,1)S(1)}, u32[]{:S(2)}) copy-start(bf16[512,256]{1,0:T(8,128)(2,1)S(1)} %get-tuple-element.35.refs_4_.refs_1_) | copy-start | bytes 786436
  50.6 12.7 %collective-permute-start.1 = (bf16[4096,256]{1,0:T(8,128)(2,1)}, bf16[4096,256]{1,0:T(8,128)(2,1)S(1)}, u32[]{:S(2)}, u32[]{:S(2)}) collective-permute-start(bf16[4096,256]{1,0:T(8,128)(2,1)} %collective-permute-done.refs_3_.refs_5_), channel_id=1, source_target_pairs={{0,2},{2,0},{1,3},{3,1},{4,6},{6,4},{5,7},{7,5},{8,10},{10,8},{9,1... | collective-permute-start | bytes 6291464 | tf_op jit(solution)/shard_map/ppermute | solution.py:541
  52.2 32.5 %collective-permute-start.2 = (bf16[512,256]{1,0:T(8,128)(2,1)S(1)}, bf16[512,256]{1,0:T(8,128)(2,1)S(1)}, u32[]{:S(2)}, u32[]{:S(2)}) collective-permute-start(bf16[512,256]{1,0:T(8,128)(2,1)S(1)} %get-tuple-element.35.refs_4_.refs_1_), channel_id=1, source_target_pairs={{0,1},{1,0},{2,3},{3,2},{4,5},{5,4},{6,7},{7,6},{8,9},{9,8},{10,11... | collective-permute-start | bytes 786440 | tf_op jit(solution)/shard_map/ppermute | solution.py:541
  58.1 1.6 copy-start.4
  63.3 5.3 %copy-start.6 = (bf16[4096,256]{1,0:T(8,128)(2,1)}, bf16[4096,256]{1,0:T(8,128)(2,1)S(1)}, u32[]{:S(2)}) copy-start(bf16[4096,256]{1,0:T(8,128)(2,1)S(1)} %collective-permute-done.1.refs_4_.refs_6_) | copy-start | bytes 6291460
  70.6 14.0 %collective-permute-start.3 = (bf16[512,256]{1,0:T(8,128)(2,1)S(1)}, bf16[512,256]{1,0:T(8,128)(2,1)S(1)}, u32[]{:S(2)}, u32[]{:S(2)}) collective-permute-start(bf16[512,256]{1,0:T(8,128)(2,1)S(1)} %get-tuple-element.41.refs_2_.refs_3_), channel_id=1, source_target_pairs={{0,1},{1,0},{2,3},{3,2},{4,5},{5,4},{6,7},{7,6},{8,9},{9,8},{10,11... | collective-permute-start | bytes 786440 | tf_op jit(solution)/shard_map/ppermute | solution.py:541
  71.3 13.3 %copy-start.5 = (f32[4,512,256]{2,1,0:T(8,128)S(1)}, f32[4,512,256]{2,1,0:T(8,128)}, u32[]{:S(2)}) copy-start(f32[4,512,256]{2,1,0:T(8,128)} %get-tuple-element.37.refs_4_.refs_6_) | copy-start | bytes 6291460
  71.3 13.3 %copy-start.22 = (bf16[4,256,256]{2,1,0:T(8,128)(2,1)S(1)}, bf16[4,256,256]{2,1,0:T(8,128)(2,1)}, u32[]{:S(2)}) copy-start(bf16[4,256,256]{2,1,0:T(8,128)(2,1)} %get-tuple-element.43.refs_3_) | copy-start | bytes 1572868
  71.3 13.4 %copy-start.23 = (f32[512,256]{1,0:T(8,128)S(1)}, f32[512,256]{1,0:T(8,128)}, u32[]{:S(2)}) copy-start(f32[512,256]{1,0:T(8,128)} %get-tuple-element.42.refs_1_) | copy-start | bytes 1572868
  71.4 13.4 %copy-start.25 = (bf16[4,128,256]{2,1,0:T(8,128)(2,1)S(1)}, bf16[4,128,256]{2,1,0:T(8,128)(2,1)}, u32[]{:S(2)}) copy-start(bf16[4,128,256]{2,1,0:T(8,128)(2,1)} %get-tuple-element.44.refs_4_) | copy-start | bytes 786436
  84.7 6.6 %copy-start.9 = (bf16[512,256]{1,0:T(8,128)(2,1)}, bf16[512,256]{1,0:T(8,128)(2,1)S(1)}, u32[]{:S(2)}) copy-start(bf16[512,256]{1,0:T(8,128)(2,1)S(1)} %collective-permute-done.2.refs_10_.refs_2_) | copy-start | bytes 786436
  84.7 6.6 %copy-start.11 = (bf16[512,256]{1,0:T(8,128)(2,1)}, bf16[512,256]{1,0:T(8,128)(2,1)S(1)}, u32[]{:S(2)}) copy-start(bf16[512,256]{1,0:T(8,128)(2,1)S(1)} %collective-permute-done.3.refs_11_.refs_4_) | copy-start | bytes 786436
  84.7 1.2 copy-start.12
  91.3 41.9 %all-to-all-start.1 = ((bf16[64,32,256]{2,1,0:T(8,128)(2,1)}), bf16[64,32,256]{2,1,0:T(8,128)(2,1)S(1)}, u32[]{:S(2)}, u32[]{:S(2)}) async-start(bf16[64,32,256]{2,1,0:T(8,128)(2,1)} %bitcast.12), calls=%async_computation.1 | async-start | bytes 2097152 | tf_op jit(solution)/shard_map/all_to_all | solution.py:580
  105.7 8.7 %collective-permute-start.4 = (bf16[8,256,256]{2,1,0:T(8,128)(2,1)}, bf16[8,256,256]{2,1,0:T(8,128)(2,1)S(1)}, u32[]{:S(2)}, u32[]{:S(2)}) collective-permute-start(bf16[8,256,256]{2,1,0:T(8,128)(2,1)} %get-tuple-element.46.refs_7_), channel_id=1, source_target_pairs={{0,2},{2,0},{1,3},{3,1},{4,6},{6,4},{5,7},{7,5},{8,10},{10,8},{9,1... | collective-permute-start | bytes 3145736 | tf_op jit(solution)/shard_map/ppermute | solution.py:541
  106.0 13.9 %collective-permute-start.6 = (bf16[8,256,256]{2,1,0:T(8,128)(2,1)}, bf16[8,256,256]{2,1,0:T(8,128)(2,1)S(1)}, u32[]{:S(2)}, u32[]{:S(2)}) collective-permute-start(bf16[8,256,256]{2,1,0:T(8,128)(2,1)} %get-tuple-element.51), channel_id=1, source_target_pairs={{0,2},{2,0},{1,3},{3,1},{4,6},{6,4},{5,7},{7,5},{8,10},{10,8},{9,1... | collective-permute-start | bytes 3145736 | tf_op jit(solution)/shard_map/ppermute | solution.py:541
  115.3 1.2 copy-start.8
  116.6 1.2 copy-start.18
  118.8 14.3 %collective-permute-start.5 = (bf16[4,256,256]{2,1,0:T(8,128)(2,1)}, bf16[4,256,256]{2,1,0:T(8,128)(2,1)}, u32[]{:S(2)}, u32[]{:S(2)}) collective-permute-start(bf16[4,256,256]{2,1,0:T(8,128)(2,1)} %get-tuple-element.49.refs_3_), channel_id=1, source_target_pairs={{0,4},{4,0},{1,5},{5,1},{2,6},{6,2},{3,7},{7,3},{8,12},{12,8},{9,1... | collective-permute-start | bytes 1572872 | tf_op jit(solution)/shard_map/ppermute | solution.py:541
  120.0 1.2 copy-start.16
  123.1 13.2 %copy-start.15 = (f32[2,512,256]{2,1,0:T(8,128)S(1)}, f32[2,512,256]{2,1,0:T(8,128)}, u32[]{:S(2)}) copy-start(f32[2,512,256]{2,1,0:T(8,128)} %copy-done.14) | copy-start | bytes 3145732
  123.1 13.1 %collective-permute-start.8 = (bf16[2,512,256]{2,1,0:T(8,128)(2,1)}, bf16[2,512,256]{2,1,0:T(8,128)(2,1)}, u32[]{:S(2)}, u32[]{:S(2)}) collective-permute-start(bf16[2,512,256]{2,1,0:T(8,128)(2,1)} %get-tuple-element.52.refs_3_), channel_id=1, source_target_pairs={{0,8},{8,0},{1,9},{9,1},{2,10},{10,2},{3,11},{11,3},{4,12},{12,4},... | collective-permute-start | bytes 1572872 | tf_op jit(solution)/shard_map/ppermute | solution.py:541
  135.7 7.3 %copy-start.21 = (f32[2,256,256]{2,1,0:T(8,128)S(1)}, f32[2,256,256]{2,1,0:T(8,128)}, u32[]{:S(2)}) copy-start(f32[2,256,256]{2,1,0:T(8,128)} %copy-done.20) | copy-start | bytes 1572868
  135.7 7.3 %collective-permute-start.7 = (bf16[2,256,256]{2,1,0:T(8,128)(2,1)}, bf16[2,256,256]{2,1,0:T(8,128)(2,1)S(1)}, u32[]{:S(2)}, u32[]{:S(2)}) collective-permute-start(bf16[2,256,256]{2,1,0:T(8,128)(2,1)} %get-tuple-element.54.refs_3_), channel_id=1, source_target_pairs={{0,8},{8,0},{1,9},{9,1},{2,10},{10,2},{3,11},{11,3},{4,12},{12,4},... | collective-permute-start | bytes 786440 | tf_op jit(solution)/shard_map/ppermute | solution.py:541
  138.1 7.0 %collective-permute-start.10 = (bf16[2,256,256]{2,1,0:T(8,128)(2,1)}, bf16[2,256,256]{2,1,0:T(8,128)(2,1)S(1)}, u32[]{:S(2)}, u32[]{:S(2)}) collective-permute-start(bf16[2,256,256]{2,1,0:T(8,128)(2,1)} %get-tuple-element.56.refs_3_), channel_id=1, source_target_pairs={{0,4},{4,0},{1,5},{5,1},{2,6},{6,2},{3,7},{7,3},{8,12},{12,8},{9,1... | collective-permute-start | bytes 786440 | tf_op jit(solution)/shard_map/ppermute | solution.py:541
  143.0 4.9 %collective-permute-start.9 = (bf16[1,256,256]{2,1,0:T(8,128)(2,1)S(1)}, bf16[1,256,256]{2,1,0:T(8,128)(2,1)S(1)}, u32[]{:S(2)}, u32[]{:S(2)}) collective-permute-start(bf16[1,256,256]{2,1,0:T(8,128)(2,1)S(1)} %get-tuple-element.58.refs_3_), channel_id=1, source_target_pairs={{0,16},{16,0},{1,17},{17,1},{2,18},{18,2},{3,19},{19,3},{4,20},{20... | collective-permute-start | bytes 393224 | tf_op jit(solution)/shard_map/ppermute | solution.py:541
  145.1 10.2 %collective-permute-start.12 = (bf16[1,256,256]{2,1,0:T(8,128)(2,1)S(1)}, bf16[1,256,256]{2,1,0:T(8,128)(2,1)S(1)}, u32[]{:S(2)}, u32[]{:S(2)}) collective-permute-start(bf16[1,256,256]{2,1,0:T(8,128)(2,1)S(1)} %get-tuple-element.60.refs_3_), channel_id=1, source_target_pairs={{0,16},{16,0},{1,17},{17,1},{2,18},{18,2},{3,19},{19,3},{4,20},{20... | collective-permute-start | bytes 393224 | tf_op jit(solution)/shard_map/ppermute | solution.py:541
  148.0 10.5 %collective-permute-start.11 = (bf16[1,256,256]{2,1,0:T(8,128)(2,1)S(1)}, bf16[1,256,256]{2,1,0:T(8,128)(2,1)S(1)}, u32[]{:S(2)}, u32[]{:S(2)}) collective-permute-start(bf16[1,256,256]{2,1,0:T(8,128)(2,1)S(1)} %down_share.1.refs_3_.refs_1_), channel_id=1, source_target_pairs={{0,16},{16,0},{1,17},{17,1},{2,18},{18,2},{3,19},{19,3},{4,20},{20... | collective-permute-start | bytes 393224 | tf_op jit(solution)/shard_map/ppermute | solution.py:541
  155.3 11.2 %collective-permute-start.14 = (bf16[1,256,256]{2,1,0:T(8,128)(2,1)S(1)}, bf16[1,256,256]{2,1,0:T(8,128)(2,1)S(1)}, u32[]{:S(2)}, u32[]{:S(2)}) collective-permute-start(bf16[1,256,256]{2,1,0:T(8,128)(2,1)S(1)} %up_share.1.refs_3_.refs_1_), channel_id=1, source_target_pairs={{0,16},{16,0},{1,17},{17,1},{2,18},{18,2},{3,19},{19,3},{4,20},{20... | collective-permute-start | bytes 393224 | tf_op jit(solution)/shard_map/ppermute | solution.py:541
  158.5 13.2 %collective-permute-start.13 = (bf16[2,256,256]{2,1,0:T(8,128)(2,1)S(1)}, bf16[2,256,256]{2,1,0:T(8,128)(2,1)S(1)}, u32[]{:S(2)}, u32[]{:S(2)}) collective-permute-start(bf16[2,256,256]{2,1,0:T(8,128)(2,1)S(1)} %bitcast.67), channel_id=1, source_target_pairs={{0,8},{8,0},{1,9},{9,1},{2,10},{10,2},{3,11},{11,3},{4,12},{12,4},... | collective-permute-start | bytes 786440 | tf_op jit(solution)/shard_map/ppermute | solution.py:541
  166.5 8.2 %collective-permute-start.16 = (bf16[2,256,256]{2,1,0:T(8,128)(2,1)S(1)}, bf16[2,256,256]{2,1,0:T(8,128)(2,1)S(1)}, u32[]{:S(2)}, u32[]{:S(2)}) collective-permute-start(bf16[2,256,256]{2,1,0:T(8,128)(2,1)S(1)} %bitcast.69), channel_id=1, source_target_pairs={{0,4},{4,0},{1,5},{5,1},{2,6},{6,2},{3,7},{7,3},{8,12},{12,8},{9,1... | collective-permute-start | bytes 786440 | tf_op jit(solution)/shard_map/ppermute | solution.py:541
  171.7 15.5 %collective-permute-start.15 = (bf16[4,256,256]{2,1,0:T(8,128)(2,1)S(1)}, bf16[4,256,256]{2,1,0:T(8,128)(2,1)S(1)}, u32[]{:S(2)}, u32[]{:S(2)}) collective-permute-start(bf16[4,256,256]{2,1,0:T(8,128)(2,1)S(1)} %bitcast.56), channel_id=1, source_target_pairs={{0,4},{4,0},{1,5},{5,1},{2,6},{6,2},{3,7},{7,3},{8,12},{12,8},{9,1... | collective-permute-start | bytes 1572872 | tf_op jit(solution)/shard_map/ppermute | solution.py:541
  174.8 14.7 %collective-permute-start.18 = (bf16[2,512,256]{2,1,0:T(8,128)(2,1)S(1)}, bf16[2,512,256]{2,1,0:T(8,128)(2,1)S(1)}, u32[]{:S(2)}, u32[]{:S(2)}) collective-permute-start(bf16[2,512,256]{2,1,0:T(8,128)(2,1)S(1)} %bitcast.58), channel_id=1, source_target_pairs={{0,8},{8,0},{1,9},{9,1},{2,10},{10,2},{3,11},{11,3},{4,12},{12,4},... | collective-permute-start | bytes 1572872 | tf_op jit(solution)/shard_map/ppermute | solution.py:541
  187.3 4.6 %collective-permute-start.17 = (bf16[8,256,256]{2,1,0:T(8,128)(2,1)S(1)}, bf16[8,256,256]{2,1,0:T(8,128)(2,1)S(1)}, u32[]{:S(2)}, u32[]{:S(2)}) collective-permute-start(bf16[8,256,256]{2,1,0:T(8,128)(2,1)S(1)} %bitcast.52), channel_id=1, source_target_pairs={{0,2},{2,0},{1,3},{3,1},{4,6},{6,4},{5,7},{7,5},{8,10},{10,8},{9,1... | collective-permute-start | bytes 3145736 | tf_op jit(solution)/shard_map/ppermute | solution.py:541
  189.6 3.7 %collective-permute-start.19 = (bf16[8,256,256]{2,1,0:T(8,128)(2,1)S(1)}, bf16[8,256,256]{2,1,0:T(8,128)(2,1)S(1)}, u32[]{:S(2)}, u32[]{:S(2)}) collective-permute-start(bf16[8,256,256]{2,1,0:T(8,128)(2,1)S(1)} %bitcast.61), channel_id=1, source_target_pairs={{0,2},{2,0},{1,3},{3,1},{4,6},{6,4},{5,7},{7,5},{8,10},{10,8},{9,1... | collective-permute-start | bytes 3145736 | tf_op jit(solution)/shard_map/ppermute | solution.py:541
  (4 other events, 3.4 us)
